TPU v7x, 128 devices: a whole 4x4x4 slice. The times are simulated.
128 devices in a mesh: dp: 16 (over y, z), ep: 8 (over x, core).
Axes of the slice: x: 4, y: 4, z: 4, core: 2. Of those that a mesh axis runs over, the one named last changes fastest.
Arguments:
- hidden: bfloat16 [2, 1024, 7168], P(None, ('dp', 'ep')), may hold values from -6 to 6
- expert_ids: int32 [2, 1024, 8], P(None, ('dp', 'ep')), may hold values from 0 to 31, all different within a row; in each aligned block of 8 rows (0 to 7, 8 to 15, ..., all dimensions but the last counted through in order) at most 3 rows name the same one
- expert_gates: float32 [2, 1024, 8], P(None, ('dp', 'ep')), may hold values from 0.1 to 0.6
- w_gate: bfloat16 [32, 7168, 1024], P('dp', 'ep'), may hold values from -0.0625 to 0.0625
- w_up: bfloat16 [32, 7168, 1024], P('dp', 'ep'), may hold values from -0.0625 to 0.0625
- w_down: bfloat16 [32, 1024, 7168], P('dp', None, 'ep'), may hold values from -0.1875 to 0.1875
- w_latent: bfloat16 [7168, 576], P('ep'), may hold values from -0.0625 to 0.0625
- queries: bfloat16 [2, 1024, 128, 576], P(None, ('dp', 'ep')), may hold values from -16 to 16
- cache: bfloat16 [1024, 512, 576], P(('dp', 'ep')), may hold values from -8 to 8
- lengths: int32 [1024], replicated, may hold values from 2 to 510
- came_from: int32 [1024], replicated, may hold values from 0 to 1023, as said below
Outputs:
- expert_out: bfloat16 [2, 1024, 7168], P(None, ('dp', 'ep'))
- attended: bfloat16 [2, 1024, 128, 512], P(None, ('dp', 'ep'))
Inputs may be any that keep to these rules, and one draw needn't show every extreme that they name: `expert_ids`: in each step, no expert is picked by more than 3 of the 8 rows of one device, and the rows of one device pick distinct experts each. `came_from`: A permutation of the slots; a slot takes a row from a device with the same ep index; on every device exactly 2 rows leave and exactly 2 slots take a row from another device, never two from the same device.
All inputs are finite; a program needn't handle non-finite values.
Results may differ from a plain program's by a relative error of at most 0.0085.
Values may be sent and summed in bfloat16 or wider, within the bound.
No kernel may reach another device: no remote copies, remote signals or barrier semaphores. Data moves between devices by JAX's collectives and lax.ppermute only.
A program may use at most 128 MiB of HBM per device.

v0:
```python
import jax
import jax.numpy as jnp
from jax import lax
from jax.sharding import PartitionSpec as P

LAT = 512


SCORE_SCALE = 192.0 ** (-0.5)
EPSILON = 1e-06


def row_norm(values):
    return values * lax.rsqrt(jnp.mean(values * values, axis=-1, keepdims=True) + EPSILON)


def rotate_half(part, position):
    half = part.shape[-1] // 2
    freq = 10000.0 ** (-2.0 * jnp.arange(half, dtype=jnp.float32) / part.shape[-1])
    angle = position.astype(jnp.float32)[:, None] * freq[None, :]
    cosine = jnp.cos(angle)
    sine = jnp.sin(angle)
    first = part[:, :half]
    second = part[:, half:]
    return jnp.concatenate([first * cosine - second * sine, second * cosine + first * sine], axis=1)


def make_key(kv_raw, position):
    latent = row_norm(kv_raw[:, :LAT])
    return jnp.concatenate([latent, rotate_half(kv_raw[:, LAT:], position)], axis=1).astype(
        jnp.bfloat16
    )


def place_key(keys, new_key, position):
    spot = lax.broadcasted_iota(jnp.int32, keys.shape[:2], 1) == position[:, None]
    return jnp.where(spot[:, :, None], new_key[:, None, :], keys)


def attend(queries, keys, count):
    scores = (
        jnp.einsum("rhk,rck->rhc", queries, keys, preferred_element_type=jnp.float32) * SCORE_SCALE
    )
    valid = lax.broadcasted_iota(jnp.int32, keys.shape[:2], 1) < count[:, None]
    scores = jnp.where(valid[:, None, :], scores, -jnp.inf)
    top = jnp.max(scores, axis=2, keepdims=True)
    weights = jnp.exp(scores - top)
    probs = (weights / jnp.sum(weights, axis=2, keepdims=True)).astype(jnp.bfloat16)
    return jnp.einsum(
        "rhc,rcl->rhl", probs, keys[:, :, :LAT], preferred_element_type=jnp.float32
    ).astype(jnp.bfloat16)


def mixture(normed, ids, gates, w_gate, w_up, w_down, capacity):
    rows, topk = ids.shape
    n_dp = lax.axis_size("dp")
    n_ep = lax.axis_size("ep")
    local_exp = w_gate.shape[0]
    experts = local_exp * n_dp
    slices = w_gate.shape[1]
    flat = ids.reshape(rows * topk)
    onehot = (flat[:, None] == lax.broadcasted_iota(jnp.int32, (rows * topk, experts), 1)).astype(
        jnp.int32
    )
    before = jnp.cumsum(onehot, axis=0) - onehot
    rank = jnp.sum(before * onehot, axis=1)
    slot = (flat * capacity + rank).reshape(rows, topk)
    hits = slot[:, :, None] == lax.broadcasted_iota(jnp.int32, (rows, topk, experts * capacity), 2)
    placing = jnp.any(hits, axis=1).astype(jnp.bfloat16)
    outgoing = lax.dot_general(
        placing, normed, (((0,), (0,)), ((), ())), preferred_element_type=jnp.float32
    ).astype(jnp.bfloat16)
    outgoing = outgoing.reshape(n_dp, local_exp * capacity, n_ep, slices)
    arrived = lax.all_to_all(
        lax.all_to_all(outgoing, "dp", split_axis=0, concat_axis=0, tiled=True),
        "ep",
        split_axis=2,
        concat_axis=2,
        tiled=True,
    )
    arrived = arrived.reshape(n_dp, local_exp, capacity, n_ep, slices)
    gate_part = jnp.einsum("aecbd,edf->eacbf", arrived, w_gate, preferred_element_type=jnp.float32)
    up_part = jnp.einsum("aecbd,edf->eacbf", arrived, w_up, preferred_element_type=jnp.float32)
    gate_sum, up_sum = lax.psum((gate_part, up_part), "ep")
    act = (jax.nn.silu(gate_sum) * up_sum).astype(jnp.bfloat16)
    result = jnp.einsum("eacbf,efd->aecbd", act, w_down, preferred_element_type=jnp.float32).astype(
        jnp.bfloat16
    )
    result = result.reshape(n_dp, local_exp * capacity, n_ep, slices)
    returned = lax.all_to_all(
        lax.all_to_all(result, "dp", split_axis=0, concat_axis=0, tiled=True),
        "ep",
        split_axis=2,
        concat_axis=2,
        tiled=True,
    )
    returned = returned.reshape(experts * capacity, n_ep * slices)
    picked = jnp.take(returned, slot.reshape(rows * topk), axis=0).reshape(
        rows, topk, n_ep * slices
    )
    return jnp.sum(gates[:, :, None] * picked.astype(jnp.float32), axis=1)


def local(
    hidden,
    expert_ids,
    expert_gates,
    w_gate,
    w_up,
    w_down,
    w_latent,
    queries,
    cache,
    lengths,
    came_from,
):
    rows = hidden.shape[1]
    topk = expert_ids.shape[2]
    n_dp = lax.axis_size("dp")
    n_ep = lax.axis_size("ep")
    experts = w_gate.shape[0] * n_dp
    capacity = max(2, rows * topk * 3 // (2 * experts))
    my_dp = lax.axis_index("dp")
    my_ep = lax.axis_index("ep")
    my_dev = my_dp * n_ep + my_ep
    mine = my_dev * rows + lax.iota(jnp.int32, rows)
    own_len = jnp.take(lengths, mine)
    whole_latent = lax.all_gather(w_latent, "ep", axis=0, tiled=True)
    mixed_steps = []
    raw_steps = []
    for step in range(hidden.shape[0]):
        start = hidden[step].astype(jnp.float32)
        normed = row_norm(start).astype(jnp.bfloat16)
        mixed = mixture(
            normed, expert_ids[step], expert_gates[step], w_gate, w_up, w_down, capacity
        )
        lat_in = row_norm(start + mixed).astype(jnp.bfloat16)
        kv_raw = jnp.dot(lat_in, whole_latent, preferred_element_type=jnp.float32)
        mixed_steps.append(mixed)
        raw_steps.append(kv_raw)
    first_key = make_key(raw_steps[0], own_len)
    cache_one = place_key(cache, first_key, own_len)
    attended_one = attend(queries[0], cache_one, own_len + 1)
    column = lax.dynamic_index_in_dim(came_from.reshape(n_dp, n_ep, rows), my_ep, 1, keepdims=False)
    dp_ids = lax.iota(jnp.int32, n_dp)
    matches = column[:, :, None] == mine[None, None, :]
    leaving = jnp.any(matches, axis=1) & (dp_ids != my_dp)[:, None]
    own_src = jnp.take(came_from, mine)
    own_src_dev = own_src // rows
    staying = own_src[:, None] == mine[None, :]
    arriving = (own_src_dev != my_dev)[:, None] & (
        (own_src_dev // n_ep)[:, None] == dp_ids[None, :]
    )
    second_len = jnp.take(lengths, own_src)
    second_key = make_key(raw_steps[1], second_len + 1)
    outgoing = jnp.einsum(
        "pr,rcd->pcd", leaving.astype(jnp.bfloat16), cache_one, preferred_element_type=jnp.float32
    ).astype(jnp.bfloat16)
    incoming = lax.all_to_all(outgoing, "dp", split_axis=0, concat_axis=0, tiled=True)
    kept = jnp.einsum(
        "kr,rcd->kcd", staying.astype(jnp.bfloat16), cache_one, preferred_element_type=jnp.float32
    )
    brought = jnp.einsum(
        "kq,qcd->kcd", arriving.astype(jnp.bfloat16), incoming, preferred_element_type=jnp.float32
    )
    cache_two = (kept + brought).astype(jnp.bfloat16)
    cache_two = place_key(cache_two, second_key, second_len + 1)
    attended_two = attend(queries[1], cache_two, second_len + 2)
    expert_out = jnp.stack(mixed_steps).astype(jnp.bfloat16)
    attended = jnp.stack([attended_one, attended_two])
    return (expert_out, attended)


def solution(mesh):
    in_specs = (
        P(None, ("dp", "ep"), None),
        P(None, ("dp", "ep"), None),
        P(None, ("dp", "ep"), None),
        P("dp", "ep", None),
        P("dp", "ep", None),
        P("dp", None, "ep"),
        P("ep", None),
        P(None, ("dp", "ep"), None, None),
        P(("dp", "ep"), None, None),
        P(),
        P(),
    )
    out_specs = (P(None, ("dp", "ep"), None), P(None, ("dp", "ep"), None, None))
    return jax.shard_map(local, mesh=mesh, in_specs=in_specs, out_specs=out_specs, check_vma=False)
```

profile of v0, /device:TPU:80, one launch (start us, length us, event | category | flops | bytes accessed | tf_op | source)
XLA Modules:
  0.0 633.3 jit_solution(8097923857979581782)
XLA Ops:
  13.8 7.4 %all-to-all-start = ((bf16[16,6,8,896]{3,2,1,0:T(8,128)(2,1)}), bf16[16,6,8,896]{3,2,1,0:T(8,128)(2,1)S(1)}, u32[]{:S(2)}, u32[]{:S(2)}) async-start(bf16[16,6,8,896]{3,2,1,0:T(8,128)(2,1)} %bitcast.45), calls=%async_computation | async-start | bytes 2752512 | tf_op jit(solution)/shard_map/all_to_all | solution.py:75
  23.1 15.9 %all-to-all-done = bf16[16,6,8,896]{3,2,1,0:T(8,128)(2,1)S(1)} async-done(((bf16[16,6,8,896]{3,2,1,0:T(8,128)(2,1)}), bf16[16,6,8,896]{3,2,1,0:T(8,128)(2,1)S(1)}, u32[]{:S(2)}, u32[]{:S(2)}) %all-to-all-start) | async-done | bytes 1376288 | tf_op jit(solution)/shard_map/all_to_all | solution.py:75
  39.1 7.3 %all-to-all-start.4 = ((bf16[16,6,8,896]{3,2,1,0:T(8,128)(2,1)}), bf16[16,6,8,896]{3,2,1,0:T(8,128)(2,1)S(1)}, u32[]{:S(2)}, u32[]{:S(2)}) async-start(bf16[16,6,8,896]{3,2,1,0:T(8,128)(2,1)} %bitcast.151), calls=%async_computation.4 | async-start | bytes 2752512 | tf_op jit(solution)/shard_map/all_to_all | solution.py:75
  47.7 14.2 %all-to-all-done.4 = bf16[16,6,8,896]{3,2,1,0:T(8,128)(2,1)S(1)} async-done(((bf16[16,6,8,896]{3,2,1,0:T(8,128)(2,1)}), bf16[16,6,8,896]{3,2,1,0:T(8,128)(2,1)S(1)}, u32[]{:S(2)}, u32[]{:S(2)}) %all-to-all-start.4) | async-done | bytes 1376288 | tf_op jit(solution)/shard_map/all_to_all | solution.py:75
  61.9 4.3 all-to-all-start.1
  67.6 18.1 %all-to-all-done.1 = bf16[16,6,8,896]{3,0,1,2:T(8,128)(2,1)S(1)} async-done(((bf16[16,6,8,896]{3,0,1,2:T(8,128)(2,1)}), bf16[16,6,8,896]{3,0,1,2:T(8,128)(2,1)S(1)}, u32[]{:S(2)}, u32[]{:S(2)}) %all-to-all-start.1) | async-done | bytes 1376288 | tf_op jit(solution)/shard_map/all_to_all | solution.py:74
  89.4 5.8 fusion.17
  98.7 10.0 %all-to-all-done.5 = bf16[16,6,8,896]{3,0,1,2:T(8,128)(2,1)S(1)} async-done(((bf16[16,6,8,896]{3,0,1,2:T(8,128)(2,1)}), bf16[16,6,8,896]{3,0,1,2:T(8,128)(2,1)S(1)}, u32[]{:S(2)}, u32[]{:S(2)}) %all-to-all-start.5) | async-done | bytes 1376288 | tf_op jit(solution)/shard_map/all_to_all | solution.py:74
  108.7 5.7 fusion.15
  114.4 3.6 fusion.19
  118.8 143.0 %all-reduce.3.cloned.1.call-done = (f32[2,16,3,8,1024]{4,3,2,1,0:T(8,128)}, f32[2,16,3,8,1024]{4,3,2,1,0:T(8,128)}, f32[2,16,3,8,1024]{4,3,2,1,0:T(8,128)}, f32[2,16,3,8,1024]{4,3,2,1,0:T(8,128)}) async-done(((f32[2,16,3,8,1024]{4,3,2,1,0:T(8,128)}, f32[2,16,3,8,1024]{4,3,2,1,0:T(8,128)}, f32[2,16,3,8,1024]{4,3,2,1,0:T(8,128)}, f32[2,16,3,8,1024]{4,3,2,1,0:T(8,128)}), (f32[2,16,3,8,1024]{4,3,2,1,0:T(8,128)}, ...) | async-done | bytes 12582928 | tf_op jit(solution)/shard_map/psum | solution.py:84
  261.8 5.7 fusion.52
  268.7 7.2 %all-to-all-start.2 = ((bf16[16,6,8,896]{3,2,1,0:T(8,128)(2,1)}), bf16[16,6,8,896]{3,2,1,0:T(8,128)(2,1)S(1)}, u32[]{:S(2)}, u32[]{:S(2)}) async-start(bf16[16,6,8,896]{3,2,1,0:T(8,128)(2,1)} %bitcast.14), calls=%async_computation.2 | async-start | bytes 2752512 | tf_op jit(solution)/shard_map/all_to_all | solution.py:91
  275.9 5.7 fusion.49
  282.8 10.4 %all-to-all-done.2 = bf16[16,6,8,896]{3,2,1,0:T(8,128)(2,1)S(1)} async-done(((bf16[16,6,8,896]{3,2,1,0:T(8,128)(2,1)}), bf16[16,6,8,896]{3,2,1,0:T(8,128)(2,1)S(1)}, u32[]{:S(2)}, u32[]{:S(2)}) %all-to-all-start.2) | async-done | bytes 1376288 | tf_op jit(solution)/shard_map/all_to_all | solution.py:91
  293.2 7.6 %all-to-all-start.6 = ((bf16[16,6,8,896]{3,2,1,0:T(8,128)(2,1)}), bf16[16,6,8,896]{3,2,1,0:T(8,128)(2,1)S(1)}, u32[]{:S(2)}, u32[]{:S(2)}) async-start(bf16[16,6,8,896]{3,2,1,0:T(8,128)(2,1)} %bitcast.150), calls=%async_computation.6 | async-start | bytes 2752512 | tf_op jit(solution)/shard_map/all_to_all | solution.py:91
  302.9 12.7 %all-to-all-done.6 = bf16[16,6,8,896]{3,2,1,0:T(8,128)(2,1)S(1)} async-done(((bf16[16,6,8,896]{3,2,1,0:T(8,128)(2,1)}), bf16[16,6,8,896]{3,2,1,0:T(8,128)(2,1)S(1)}, u32[]{:S(2)}, u32[]{:S(2)}) %all-to-all-start.6) | async-done | bytes 1376288 | tf_op jit(solution)/shard_map/all_to_all | solution.py:91
  315.6 7.7 %all-to-all-start.3 = ((bf16[16,6,8,896]{3,0,1,2:T(8,128)(2,1)}), bf16[16,6,8,896]{3,0,1,2:T(8,128)(2,1)S(1)}, u32[]{:S(2)}, u32[]{:S(2)}) async-start(bf16[16,6,8,896]{3,0,1,2:T(8,128)(2,1)} %copy.95), calls=%async_computation.3 | async-start | bytes 2752512 | tf_op jit(solution)/shard_map/all_to_all | solution.py:90
  324.7 7.7 %copy.104 = bf16[8,512,576]{2,1,0:T(8,128)(2,1)} copy(bf16[8,512,576]{1,2,0:T(8,128)(2,1)} %param.23) | data formatting | bytes 9437184 | tf_op args[8]
  334.0 8.9 %all-to-all-done.3 = bf16[16,6,8,896]{3,0,1,2:T(8,128)(2,1)S(1)} async-done(((bf16[16,6,8,896]{3,0,1,2:T(8,128)(2,1)}), bf16[16,6,8,896]{3,0,1,2:T(8,128)(2,1)S(1)}, u32[]{:S(2)}, u32[]{:S(2)}) %all-to-all-start.3) | async-done | bytes 1376288 | tf_op jit(solution)/shard_map/all_to_all | solution.py:90
  342.8 4.3 all-to-all-start.7
  348.0 18.6 %all-to-all-done.7 = bf16[16,6,8,896]{3,0,1,2:T(8,128)(2,1)} async-done(((bf16[16,6,8,896]{3,0,1,2:T(8,128)(2,1)}), bf16[16,6,8,896]{3,0,1,2:T(8,128)(2,1)}, u32[]{:S(2)}, u32[]{:S(2)}) %all-to-all-start.7) | async-done | bytes 1376288 | tf_op jit(solution)/shard_map/all_to_all | solution.py:90
  374.6 5.7 fusion.82
  383.0 6.1 broadcast_select_fusion
  389.2 8.6 %copy.108 = bf16[8,512,576]{1,0,2:T(8,128)(2,1)} copy(bf16[8,512,576]{2,1,0:T(8,128)(2,1)} %broadcast_select_fusion) | data formatting | bytes 9437184 | tf_op jit(solution)/shard_map/jit(_where)/select_n | solution.py:37
  397.8 7.1 %convolution_convert_fusion.2 = bf16[16,512,576]{1,0,2:T(8,128)(2,1)} fusion(bf16[8,512,576]{1,0,2:T(8,128)(2,1)} %copy.108, pred[16,8]{0,1:T(8,128)(4,1)S(1)} %compare_reduce_fusion, pred[16]{0:T(512)(128)(4,1)S(1)} %iota_compare_fusion.9), kind=kOutput, calls=%fused_computation.12 | convolution fusion | flops 80216192 | bytes 14155920 | tf_op jit(solution)/shard_map/pr,rcd->pcd/dot_general | solution.py:156
  405.0 12.6 %copy.111 = bf16[16,512,576]{1,2,0:T(8,128)(2,1)} copy(bf16[16,512,576]{1,0,2:T(8,128)(2,1)} %convolution_convert_fusion.2) | data formatting | bytes 18874368 | tf_op jit(solution)/shard_map/convert_element_type | solution.py:158
  417.6 8.4 %all-to-all-start.8 = ((bf16[16,512,576]{1,2,0:T(8,128)(2,1)}), bf16[16,512,576]{1,2,0:T(8,128)(2,1)}, u32[]{:S(2)}, u32[]{:S(2)}) async-start(bf16[16,512,576]{1,2,0:T(8,128)(2,1)} %copy.111), calls=%async_computation.8 | async-start | bytes 18874368 | tf_op jit(solution)/shard_map/all_to_all | solution.py:159
  427.4 4.5 fusion.66
  433.8 5.2 fusion.122
  439.8 156.3 %all-to-all-done.8 = bf16[16,512,576]{1,2,0:T(8,128)(2,1)} async-done(((bf16[16,512,576]{1,2,0:T(8,128)(2,1)}), bf16[16,512,576]{1,2,0:T(8,128)(2,1)}, u32[]{:S(2)}, u32[]{:S(2)}) %all-to-all-start.8) | async-done | bytes 9437216 | tf_op jit(solution)/shard_map/all_to_all | solution.py:159
  596.1 20.5 %fusion.4 = bf16[8,512,576]{1,0,2:T(8,128)(2,1)S(1)} fusion(f32[8,512,576]{1,0,2:T(8,128)} %fusion.122, pred[8,512]{1,0:T(8,128)(4,1)S(1)} %iota_compare_fusion.4, bf16[16,512,576]{1,2,0:T(8,128)(2,1)} %all-to-all-done.8, bf16[8,576]{0,1:T(8,128)(2,1)S(1)} %copy.107, s32[8]{0:T(128)S(1)} %and_select_fusion.1, pred[8]{0:T(512)(128)(4,1)S(1)} %get-tuple-element.16), kind=kOutput, calls=%fused_computation.14 | convolution fusion | flops 82575616 | bytes 23606312 | tf_op jit(solution)/shard_map/kq,qcd->kcd/dot_general | solution.py:163
  (121 shorter events, 51.5 us)
Async XLA Ops:
  7.2 316.3 %copy-start = (s32[1024]{0:T(1024)S(1)}, s32[1024]{0:T(1024)}, u32[]{:S(2)}) copy-start(s32[1024]{0:T(1024)} %param.24) | copy-start | bytes 12292
  12.4 8.7 %copy-start.5 = (bf16[2,8,7168]{2,1,0:T(8,128)(2,1)S(1)}, bf16[2,8,7168]{2,1,0:T(8,128)(2,1)}, u32[]{:S(2)}) copy-start(bf16[2,8,7168]{2,1,0:T(8,128)(2,1)} %param.15) | copy-start | bytes 688132
  13.8 25.3 %all-to-all-start = ((bf16[16,6,8,896]{3,2,1,0:T(8,128)(2,1)}), bf16[16,6,8,896]{3,2,1,0:T(8,128)(2,1)S(1)}, u32[]{:S(2)}, u32[]{:S(2)}) async-start(bf16[16,6,8,896]{3,2,1,0:T(8,128)(2,1)} %bitcast.45), calls=%async_computation | async-start | bytes 2752512 | tf_op jit(solution)/shard_map/all_to_all | solution.py:75
  39.1 22.9 %all-to-all-start.4 = ((bf16[16,6,8,896]{3,2,1,0:T(8,128)(2,1)}), bf16[16,6,8,896]{3,2,1,0:T(8,128)(2,1)S(1)}, u32[]{:S(2)}, u32[]{:S(2)}) async-start(bf16[16,6,8,896]{3,2,1,0:T(8,128)(2,1)} %bitcast.151), calls=%async_computation.4 | async-start | bytes 2752512 | tf_op jit(solution)/shard_map/all_to_all | solution.py:75
  61.9 23.8 %all-to-all-start.1 = ((bf16[16,6,8,896]{3,0,1,2:T(8,128)(2,1)}), bf16[16,6,8,896]{3,0,1,2:T(8,128)(2,1)S(1)}, u32[]{:S(2)}, u32[]{:S(2)}) async-start(bf16[16,6,8,896]{3,0,1,2:T(8,128)(2,1)} %copy.90), calls=%async_computation.1 | async-start | bytes 2752512 | tf_op jit(solution)/shard_map/all_to_all | solution.py:74
  85.7 23.0 %all-to-all-start.5 = ((bf16[16,6,8,896]{3,0,1,2:T(8,128)(2,1)}), bf16[16,6,8,896]{3,0,1,2:T(8,128)(2,1)S(1)}, u32[]{:S(2)}, u32[]{:S(2)}) async-start(bf16[16,6,8,896]{3,0,1,2:T(8,128)(2,1)} %copy.97), calls=%async_computation.5 | async-start | bytes 2752512 | tf_op jit(solution)/shard_map/all_to_all | solution.py:74
  89.3 172.5 %all-reduce.3.cloned.1.call-start = ((), (), s32[]{:S(2)}) async-start(), calls=%async_computation.10 | async-start | bytes 25165824 | tf_op jit(solution)/shard_map/psum | solution.py:84
  89.3 5.8 copy-start.7
  108.7 5.7 copy-start.8
  118.0 256.6 %all-gather.2.cloned.1.call-start = ((), (), s32[]{:S(2)}) async-start(), calls=%async_computation.9 | async-start | bytes 9289728 | tf_op jit(solution)/shard_map/all_gather | solution.py:128
  268.7 24.5 %all-to-all-start.2 = ((bf16[16,6,8,896]{3,2,1,0:T(8,128)(2,1)}), bf16[16,6,8,896]{3,2,1,0:T(8,128)(2,1)S(1)}, u32[]{:S(2)}, u32[]{:S(2)}) async-start(bf16[16,6,8,896]{3,2,1,0:T(8,128)(2,1)} %bitcast.14), calls=%async_computation.2 | async-start | bytes 2752512 | tf_op jit(solution)/shard_map/all_to_all | solution.py:91
  281.6 19.2 %copy-start.2 = (s32[1024]{0:T(1024)S(1)}, s32[1024]{0:T(1024)}, u32[]{:S(2)}) copy-start(s32[1024]{0:T(1024)} %param.25) | copy-start | bytes 12292
  293.2 22.4 %all-to-all-start.6 = ((bf16[16,6,8,896]{3,2,1,0:T(8,128)(2,1)}), bf16[16,6,8,896]{3,2,1,0:T(8,128)(2,1)S(1)}, u32[]{:S(2)}, u32[]{:S(2)}) async-start(bf16[16,6,8,896]{3,2,1,0:T(8,128)(2,1)} %bitcast.150), calls=%async_computation.6 | async-start | bytes 2752512 | tf_op jit(solution)/shard_map/all_to_all | solution.py:91
  315.6 27.2 %all-to-all-start.3 = ((bf16[16,6,8,896]{3,0,1,2:T(8,128)(2,1)}), bf16[16,6,8,896]{3,0,1,2:T(8,128)(2,1)S(1)}, u32[]{:S(2)}, u32[]{:S(2)}) async-start(bf16[16,6,8,896]{3,0,1,2:T(8,128)(2,1)} %copy.95), calls=%async_computation.3 | async-start | bytes 2752512 | tf_op jit(solution)/shard_map/all_to_all | solution.py:90
  332.6 14.7 %copy-start.6 = (f32[2,8,8]{2,1,0:T(8,128)S(1)}, f32[2,8,8]{2,1,0:T(8,128)}, u32[]{:S(2)}) copy-start(f32[2,8,8]{2,1,0:T(8,128)} %param.17) | copy-start | bytes 1540
  342.8 23.8 %all-to-all-start.7 = ((bf16[16,6,8,896]{3,0,1,2:T(8,128)(2,1)}), bf16[16,6,8,896]{3,0,1,2:T(8,128)(2,1)}, u32[]{:S(2)}, u32[]{:S(2)}) async-start(bf16[16,6,8,896]{3,0,1,2:T(8,128)(2,1)} %copy.102), calls=%async_computation.7 | async-start | bytes 2752512 | tf_op jit(solution)/shard_map/all_to_all | solution.py:90
  374.6 5.9 copy-start.3
  417.6 178.5 %all-to-all-start.8 = ((bf16[16,512,576]{1,2,0:T(8,128)(2,1)}), bf16[16,512,576]{1,2,0:T(8,128)(2,1)}, u32[]{:S(2)}, u32[]{:S(2)}) async-start(bf16[16,512,576]{1,2,0:T(8,128)(2,1)} %copy.111), calls=%async_computation.8 | async-start | bytes 18874368 | tf_op jit(solution)/shard_map/all_to_all | solution.py:159
  426.2 7.6 %slice-start = ((s8[4718592]{0:T(1024)(128)(4,1)}), s8[524288]{0:T(1024)(128)(4,1)S(1)}, s32[]{:S(2)}) async-start(s8[4718592]{0:T(1024)(128)(4,1)} %bitcast.146), calls=%async_computation.11 | async-start | bytes 1048576
  427.4 6.4 %slice-start.1 = ((s8[4718592]{0:T(1024)(128)(4,1)}), s8[4194304]{0:T(1024)(128)(4,1)S(1)}, s32[]{:S(2)}) async-start(s8[4718592]{0:T(1024)(128)(4,1)} %bitcast.146), calls=%async_computation.12 | async-start | bytes 8388608
  431.9 7.1 %slice-start.2 = ((s8[5242880]{0:T(1024)(128)(4,1)}), s8[4194304]{0:T(1024)(128)(4,1)S(1)}, s32[]{:S(2)}) async-start(s8[5242880]{0:T(1024)(128)(4,1)} %bitcast.148), calls=%async_computation.13 | async-start | bytes 8388608
  433.8 5.2 slice-start.3
  596.1 20.5 %copy-start.9 = (bf16[2,8,128,576]{2,3,1,0:T(8,128)(2,1)S(1)}, bf16[2,8,128,576]{2,3,1,0:T(8,128)(2,1)}, u32[]{:S(2)}) copy-start(bf16[2,8,128,576]{2,3,1,0:T(8,128)(2,1)} %param.22) | copy-start | bytes 7077892
  616.6 3.3 copy-start.4
  619.9 2.2 slice-start.4
  622.1 4.1 copy-start.1
Sparse Core Ops, SparseCore 0:
  118.1 143.5 all-reduce.2
  263.5 48.9 all-gather.1
where the time goes:
time: 642 us; the launch traced here: 633 us
  waiting for transfers between devices  409 us (64%)
  matrix products  84 us (13%)
  starting transfers between devices  58.1 us (9%)
  local copies, waits for them, and re-layouts  48.7 us (8%)
  other arithmetic  19 us (3%)
  between operations  14.7 us (2%)
    all_to_all x1, waiting for transfers between devices, local(): lax.all_to_all(outgoing, 'dp', split_axis=0, concat_axis=0, tiled=True)  156 us
    psum x1, waiting for transfers between devices, mixture(): gate_sum, up_sum = lax.psum((gate_part, up_part), 'ep')  143 us
    all_to_all x2, waiting for transfers between devices, mixture(): lax.all_to_all(outgoing, 'dp', split_axis=0, concat_axis=0, tiled=True)  30.1 us
    all_to_all x2, waiting for transfers between devices, mixture(): lax.all_to_all(lax.all_to_all(outgoing, 'dp', split_axis=0, concat_axis=0...  28.2 us
    all_to_all x2, waiting for transfers between devices, mixture(): lax.all_to_all(lax.all_to_all(result, 'dp', split_axis=0, concat_axis=0,...  27.5 us
    all_to_all x2, waiting for transfers between devices, mixture(): lax.all_to_all(result, 'dp', split_axis=0, concat_axis=0, tiled=True)  23.1 us
    dot_general x1, matrix products, local(): jnp.einsum('kq,qcd->kcd', arriving.astype(jnp.bfloat16), incoming, prefer...  20.5 us
    all_to_all x2, starting transfers between devices, mixture(): lax.all_to_all(result, 'dp', split_axis=0, concat_axis=0, tiled=True)  14.8 us
  transfers between devices with their start and end apart: 11, of which 10 were waited for; matrix products, arithmetic and copies ran while one was open for 10% of the time, Pallas kernels for 0%

commit v1 on v0

v1 whole, which is shorter than its diff:
```python
import functools

import jax
import jax.numpy as jnp
from jax import lax
from jax.experimental import pallas as pl
from jax.experimental.pallas import tpu as pltpu
from jax.sharding import PartitionSpec as P

F32 = jnp.float32
BF16 = jnp.bfloat16
D = 7168
LAT = 512
KV = 576
FF = 1024
EXPERTS = 32
CAP = 3
N_DP = 16
N_EP = 8
SLICE = D // N_EP
META = 128
WIDE = SLICE + META
ROWS = 8
TOPK = 8
SLOTS = EXPERTS * CAP * N_EP
PER_DP = SLOTS // N_DP
HALF = SLOTS // 2
KVW = 768
KEYW = 640
SCALE = 192.0 ** (-0.5)
EPS = 1e-06
VMEM = pl.BlockSpec(memory_space=pltpu.VMEM)
ANY = pl.BlockSpec(memory_space=pl.ANY)
PARAMS = pltpu.CompilerParams(vmem_limit_bytes=48 * 1024 * 1024)


def cost(flops, nbytes):
    return pl.CostEstimate(flops=int(flops), bytes_accessed=int(nbytes), transcendentals=0)


def split3(v):
    hi = v.astype(BF16).astype(F32)
    mid = (v - hi).astype(BF16).astype(F32)
    lo = (v - hi - mid).astype(BF16).astype(F32)
    return hi, mid, lo


def pack_kernel(hidden_ref, ids_ref, gates_ref, out_ref):
    lane = lax.broadcasted_iota(jnp.int32, (ROWS, META), 1)
    rows = []
    metas = []
    for s in range(2):
        h = hidden_ref[s].astype(F32)
        scale = lax.rsqrt(jnp.mean(h * h, axis=-1, keepdims=True) + EPS)
        ids = ids_ref[s].astype(F32)
        parts = split3(gates_ref[s])
        meta = jnp.zeros((ROWS, META), F32)
        for k in range(TOPK):
            meta = jnp.where(lane == k, ids[:, k : k + 1], meta)
            for n, part in enumerate(parts):
                meta = jnp.where(lane == 8 + 8 * n + k, part[:, k : k + 1], meta)
        for n, part in enumerate(split3(scale)):
            meta = jnp.where(lane == 32 + n, part, meta)
        rows.append(h)
        metas.append(meta)
    meta = jnp.concatenate(metas, axis=0).astype(BF16)
    for j in range(N_EP):
        cut = slice(j * SLICE, (j + 1) * SLICE)
        both = jnp.concatenate([rows[0][:, cut], rows[1][:, cut]], axis=0)
        out_ref[j, :, :SLICE] = both.astype(BF16)
        out_ref[j, :, SLICE:] = meta


def unpack(r_ref, s):
    rows = r_ref[...].astype(F32)[:, 8 * s : 8 * s + 8, :].reshape(N_EP * ROWS, WIDE)
    n = N_EP * ROWS
    hid = rows[:, :SLICE]
    meta = rows[:, SLICE:]
    mt = meta.T
    ids = mt[0:8]
    gates = mt[8:16] + mt[16:24] + mt[24:32]
    scale = meta[:, 32:33] + meta[:, 33:34] + meta[:, 34:35]
    expert = lax.broadcasted_iota(jnp.int32, (EXPERTS, n), 0).astype(F32)
    onehot = jnp.zeros((EXPERTS, n), F32)
    gm = jnp.zeros((EXPERTS, n), F32)
    for k in range(TOPK):
        eq = expert == ids[k : k + 1]
        onehot = jnp.where(eq, 1.0, onehot)
        gm = jnp.where(eq, gates[k : k + 1], gm)
    p = lax.broadcasted_iota(jnp.int32, (n, n), 0)
    q = lax.broadcasted_iota(jnp.int32, (n, n), 1)
    earlier = jnp.where(((p >> 3) == (q >> 3)) & (p < q), 1.0, 0.0).astype(BF16)
    rank = jnp.dot(onehot.astype(BF16), earlier, preferred_element_type=F32)
    b = lax.broadcasted_iota(jnp.int32, (N_EP, n), 0)
    qq = lax.broadcasted_iota(jnp.int32, (N_EP, n), 1)
    block = jnp.where((qq >> 3) == b, 1.0, 0.0)

    def place(values):
        pieces = []
        for r in range(CAP):
            picked = jnp.where((rank == float(r)) & (onehot > 0.0), values, 0.0)
            pieces.append((picked[:, None, :] * block[None, :, :])[:, None])
        return jnp.concatenate(pieces, axis=1).reshape(SLOTS, n)

    return hid, scale, onehot, gm, place


def dispatch_kernel(r_ref, out0_ref, out1_ref):
    for s, out_ref in enumerate((out0_ref, out1_ref)):
        hid, scale, onehot, _, place = unpack(r_ref, s)
        normed = (hid * scale).astype(BF16)
        table = place(onehot).astype(BF16)
        out = jnp.dot(table, normed, preferred_element_type=F32)
        out_ref[...] = out.reshape(N_DP, PER_DP, SLICE).astype(BF16)


def gateup_kernel(at_ref, x_ref, wg_ref, wu_ref, keep_ref, send_ref):
    core = at_ref[1]
    for e in range(2):
        lhs = x_ref[:, 16 * e : 16 * e + 32, :].reshape(N_DP * 32, SLICE)
        halves = []
        for w_ref in (wg_ref, wu_ref):
            full = jnp.dot(lhs, w_ref[e], preferred_element_type=F32)
            full = full.reshape(N_DP, 32, 256)[:, 8 * e : 8 * e + 24, :].reshape(HALF, 256)
            halves.append((full[:, :128], full[:, 128:]))
        (g0, g1), (u0, u1) = halves
        first = core == 0
        keep_ref[0, e, :, :128] = jnp.where(first, g0, g1).astype(BF16)
        keep_ref[0, e, :, 128:] = jnp.where(first, u0, u1).astype(BF16)
        send_ref[0, e, :, :128] = jnp.where(first, g1, g0).astype(BF16)
        send_ref[0, e, :, 128:] = jnp.where(first, u1, u0).astype(BF16)


def gate_up(at, x, w_gate, w_up):
    wspec = pl.BlockSpec((2, SLICE, 256), lambda r, a: (0, 0, (a[0] + r) % 4))
    ospec = pl.BlockSpec((1, 2, HALF, 256), lambda r, a: (r, 0, 0, 0))
    shape = jax.ShapeDtypeStruct((4, 2, HALF, 256), BF16)
    return pl.pallas_call(
        gateup_kernel,
        grid_spec=pltpu.PrefetchScalarGridSpec(
            num_scalar_prefetch=1,
            grid=(4,),
            in_specs=[
                pl.BlockSpec((N_DP, PER_DP, SLICE), lambda r, a: (0, 0, 0)),
                wspec,
                wspec,
            ],
            out_specs=[ospec, ospec],
        ),
        out_shape=[shape, shape],
        compiler_params=PARAMS,
        cost_estimate=cost(4e9, 12e6),
        name="gate_up",
    )(at, x, w_gate, w_up)


def down_kernel(at_ref, *refs):
    acts = refs[:8]
    w_ref = refs[8]
    out_ref = refs[9]
    x = at_ref[0]
    first = at_ref[1] == 0
    results = []
    for e in range(2):
        total = jnp.zeros((HALF, SLICE), F32)
        for n, shift in enumerate((0, 3, 1, 2)):
            own = acts[n][e]
            other = acts[4 + n][e]
            low = jnp.where(first, own, other)
            high = jnp.where(first, other, own)
            lhs = jnp.concatenate([low, high], axis=1)
            chip = (x + shift) & 3
            rhs = w_ref[e, pl.ds(pl.multiple_of(chip * 256, 256), 256), :]
            total = total + jnp.dot(lhs, rhs, preferred_element_type=F32)
        results.append(total.reshape(N_DP, PER_DP // 2, SLICE))
    out_ref[...] = jnp.concatenate(results, axis=1).astype(BF16)


def down(at, acts, w_down):
    return pl.pallas_call(
        down_kernel,
        in_specs=[pl.BlockSpec(memory_space=pltpu.SMEM)] + [VMEM] * 9,
        out_specs=VMEM,
        out_shape=jax.ShapeDtypeStruct((N_DP, PER_DP, SLICE), BF16),
        compiler_params=PARAMS,
        cost_estimate=cost(2e9, 8e6),
        name="down",
    )(at, *acts, w_down)


def combine_kernel(s, r_ref, ret_ref, wl_ref, out_ref):
    hid, _, _, gm, place = unpack(r_ref, s)
    weights = place(gm)
    high = weights.astype(BF16)
    low = (weights - high.astype(F32)).astype(BF16)
    ret = ret_ref[...].reshape(SLOTS, SLICE)
    dims = (((0,), (0,)), ((), ()))
    mixed = lax.dot_general(high, ret, dims, preferred_element_type=F32)
    mixed = mixed + lax.dot_general(low, ret, dims, preferred_element_type=F32)
    resid = hid + mixed
    square = jnp.sum(resid * resid, axis=-1, keepdims=True)
    kv = lax.dot_general(
        resid.astype(BF16), wl_ref[...], (((1,), (1,)), ((), ())), preferred_element_type=F32
    )
    out_ref[:, :, :KV] = kv.reshape(N_EP, ROWS, KV)
    out_ref[:, :, KEYW:KVW] = jnp.broadcast_to(square, (N_EP * ROWS, KVW - KEYW)).reshape(
        N_EP, ROWS, KVW - KEYW
    )
    out_ref[:, :, KV:KEYW] = jnp.zeros((N_EP, ROWS, KEYW - KV), F32)
    out_ref[:, :, KVW:] = mixed.reshape(N_EP, ROWS, SLICE)


def key_kernel(z_ref, cos_ref, sin_ref, key_ref, mixed_ref):
    kv = jnp.sum(z_ref[:, :, :KVW], axis=0)
    for j in range(N_EP):
        mixed_ref[:, j * SLICE : (j + 1) * SLICE] = z_ref[j, :, KVW:].astype(BF16)
    raw = kv[:, :KEYW] * lax.rsqrt(kv[:, KEYW : KEYW + 1] * (1.0 / D) + EPS)
    latent = raw[:, :LAT]
    latent = latent * lax.rsqrt(jnp.mean(latent * latent, axis=-1, keepdims=True) + EPS)
    part = raw[:, LAT:]
    lane = lax.broadcasted_iota(jnp.int32, part.shape, 1)
    turned = jnp.where(lane < 32, -pltpu.roll(part, 96, 1), pltpu.roll(part, 32, 1))
    rotated = part * cos_ref[...] + turned * sin_ref[...]
    key_ref[:, :LAT] = latent.astype(BF16)
    key_ref[:, LAT:] = rotated.astype(BF16)


def old_attention(q, kt, count):
    scores = lax.dot_general(q, kt, (((0,), (0,)), ((), ())), preferred_element_type=F32) * SCALE
    lane = lax.broadcasted_iota(jnp.int32, scores.shape, 1)
    valid = lane < count
    scores = jnp.where(valid, scores, -1e30)
    top = jnp.max(scores, axis=1, keepdims=True)
    weights = jnp.where(valid, jnp.exp(scores - top), 0.0)
    total = jnp.sum(weights, axis=1, keepdims=True)
    out = lax.dot_general(
        weights.astype(BF16), kt[:LAT], (((1,), (1,)), ((), ())), preferred_element_type=F32
    )
    return out, top, total


def store_old(out_ref, stat_ref, parts):
    out, top, total = parts
    lane = lax.broadcasted_iota(jnp.int32, (128, 128), 1)
    out_ref[0] = out
    stat_ref[0] = jnp.where(lane == 0, top, total)


def old0_kernel(len_ref, q_ref, kt_ref, out_ref, stat_ref):
    count = len_ref[pl.program_id(0)]
    store_old(out_ref, stat_ref, old_attention(q_ref[0, 0], kt_ref[0], count))


def old1_kernel(tab_ref, q_ref, kt_ref, mig_ref, out_ref, stat_ref):
    t = pl.program_id(0)
    count = tab_ref[t]
    away = tab_ref[24 + t]

    @pl.when(away == 0)
    def _():
        store_old(out_ref, stat_ref, old_attention(q_ref[0, 0], kt_ref[0], count))

    @pl.when(away != 0)
    def _():
        store_old(out_ref, stat_ref, old_attention(q_ref[0, 0], mig_ref[0], count))


OLD_SHAPE = [
    jax.ShapeDtypeStruct((ROWS, 128, LAT), F32),
    jax.ShapeDtypeStruct((ROWS, 128, 128), F32),
]
OLD_SPECS = [
    pl.BlockSpec((1, 128, LAT), lambda t, a: (t, 0, 0)),
    pl.BlockSpec((1, 128, 128), lambda t, a: (t, 0, 0)),
]


def old0(lens, qt, cache_t):
    return pl.pallas_call(
        old0_kernel,
        grid_spec=pltpu.PrefetchScalarGridSpec(
            num_scalar_prefetch=1,
            grid=(ROWS,),
            in_specs=[
                pl.BlockSpec((1, 1, KV, 128), lambda t, a: (0, t, 0, 0)),
                pl.BlockSpec((1, KV, 512), lambda t, a: (t, 0, 0)),
            ],
            out_specs=OLD_SPECS,
        ),
        out_shape=OLD_SHAPE,
        compiler_params=PARAMS,
        cost_estimate=cost(5e9, 8e6),
        name="old0",
    )(lens, qt, cache_t)


def old1(table, qt, cache_t, moved):
    return pl.pallas_call(
        old1_kernel,
        grid_spec=pltpu.PrefetchScalarGridSpec(
            num_scalar_prefetch=1,
            grid=(ROWS,),
            in_specs=[
                pl.BlockSpec((1, 1, KV, 128), lambda t, a: (1, t, 0, 0)),
                pl.BlockSpec((1, KV, 512), lambda t, a: (a[8 + t], 0, 0)),
                pl.BlockSpec((1, KV, 512), lambda t, a: (a[16 + t], 0, 0)),
            ],
            out_specs=OLD_SPECS,
        ),
        out_shape=OLD_SHAPE,
        compiler_params=PARAMS,
        cost_estimate=cost(5e9, 8e6),
        name="old1",
    )(table, qt, cache_t, moved)


def merge_kernel(n_new, q_ref, old_ref, stat_ref, *refs):
    keys = refs[:n_new]
    out_ref = refs[-1]
    t = pl.program_id(0)
    lane = lax.broadcasted_iota(jnp.int32, (128, ROWS), 1)
    sub = lax.broadcasted_iota(jnp.int32, (ROWS, LAT), 0)
    top = stat_ref[0, :, 0:1]
    total = stat_ref[0, :, 1:2]
    q = q_ref[0, 0]
    scores = []
    values = []
    for key_ref in keys:
        both = lax.dot_general(
            q, key_ref[:, :KV], (((0,), (1,)), ((), ())), preferred_element_type=F32
        )
        scores.append(jnp.sum(jnp.where(lane == t, both, 0.0), axis=1, keepdims=True) * SCALE)
        latent = key_ref[:, :LAT].astype(F32)
        values.append(jnp.sum(jnp.where(sub == t, latent, 0.0), axis=0, keepdims=True))
    peak = top
    for s in scores:
        peak = jnp.maximum(peak, s)
    shrink = jnp.exp(top - peak)
    out = old_ref[0] * shrink
    total = total * shrink
    for s, v in zip(scores, values):
        w = jnp.exp(s - peak)
        total = total + w
        out = out + w * v
    out_ref[0, 0] = (out / total).astype(BF16)


def merge(step, qt, old, keys, buffer):
    n_new = len(keys)
    in_specs = [
        pl.BlockSpec((1, 1, KV, 128), lambda t: (step, t, 0, 0)),
        pl.BlockSpec((1, 128, LAT), lambda t: (t, 0, 0)),
        pl.BlockSpec((1, 128, 128), lambda t: (t, 0, 0)),
    ] + [pl.BlockSpec((ROWS, KEYW), lambda t: (0, 0))] * n_new
    args = [qt, *old, *keys]
    alias = {}
    if buffer is not None:
        in_specs.append(ANY)
        alias = {len(args): 0}
        args.append(buffer)
    return pl.pallas_call(
        functools.partial(merge_kernel, n_new),
        grid=(ROWS,),
        in_specs=in_specs,
        out_specs=pl.BlockSpec((1, 1, 128, LAT), lambda t: (step, t, 0, 0)),
        out_shape=jax.ShapeDtypeStruct((2, ROWS, 128, LAT), BF16),
        input_output_aliases=alias,
        compiler_params=PARAMS,
        cost_estimate=cost(1e8, 5e6),
        name="merge%d" % step,
    )(*args)


def forward_kernel(idx_ref, src_ref, out_ref, sem):
    copies = [
        pltpu.make_async_copy(src_ref.at[idx_ref[n]], out_ref.at[n], sem.at[n]) for n in range(2 * N_DP)
    ]
    for c in copies:
        c.start()
    for c in copies:
        c.wait()


def forward(idx, pieces):
    return pl.pallas_call(
        forward_kernel,
        in_specs=[pl.BlockSpec(memory_space=pltpu.SMEM), ANY],
        out_specs=ANY,
        out_shape=jax.ShapeDtypeStruct(pieces.shape, BF16),
        scratch_shapes=[pltpu.SemaphoreType.DMA((2 * N_DP,))],
        compiler_params=PARAMS,
        cost_estimate=cost(1e6, 3e6),
        name="forward",
    )(idx, pieces)


SIB = [(i, i ^ 1) for i in range(8)]
XP = [(i, (i + 2) % 8) for i in range(8)]
XM = [(i, (i - 2) % 8) for i in range(8)]
X2 = [(i, (i + 4) % 8) for i in range(8)]


def hop(v, pairs):
    return lax.ppermute(v, "ep", pairs)


def experts(at, arrived, w_gate, w_up, w_down):
    keep, send = gate_up(at, arrived, w_gate, w_up)
    got = hop(send, SIB)
    s1 = (keep[1].astype(F32) + got[1].astype(F32)).astype(BF16)
    s2 = (keep[2].astype(F32) + got[2].astype(F32)).astype(BF16)
    s3 = (keep[3].astype(F32) + got[3].astype(F32)).astype(BF16)
    a1 = hop(s1, XP)
    a2 = hop(s2, X2)
    a3 = hop(s3, XM)
    total = (
        keep[0].astype(F32)
        + got[0].astype(F32)
        + a1.astype(F32)
        + a2.astype(F32)
        + a3.astype(F32)
    )
    act = (jax.nn.silu(total[..., :128]) * total[..., 128:]).astype(BF16)
    b1 = hop(act, XP)
    b3 = hop(act, XM)
    b2 = hop(act, X2)
    own = [act, b1, b3, b2]
    other = [hop(v, SIB) for v in own]
    return down(at, own + other, w_down)


def local(
    hidden,
    expert_ids,
    expert_gates,
    w_gate,
    w_up,
    w_down,
    w_latent,
    queries,
    cache,
    lengths,
    came_from,
):
    my_dp = lax.axis_index("dp")
    my_ep = lax.axis_index("ep")
    my_dev = my_dp * N_EP + my_ep
    at = jnp.stack([my_ep // 2, my_ep % 2]).astype(jnp.int32)
    qt = jnp.swapaxes(queries, 2, 3)
    cache_t = jnp.swapaxes(cache, 1, 2)
    latent_t = w_latent.T

    packed = pl.pallas_call(
        pack_kernel,
        in_specs=[VMEM] * 3,
        out_specs=VMEM,
        out_shape=jax.ShapeDtypeStruct((N_EP, 2 * ROWS, WIDE), BF16),
        compiler_params=PARAMS,
        name="pack",
    )(hidden, expert_ids, expert_gates)
    gathered = lax.all_to_all(packed, "ep", split_axis=0, concat_axis=0, tiled=True)
    out_shape = jax.ShapeDtypeStruct((N_DP, PER_DP, SLICE), BF16)
    sends = pl.pallas_call(
        dispatch_kernel,
        in_specs=[VMEM],
        out_specs=[VMEM, VMEM],
        out_shape=[out_shape, out_shape],
        compiler_params=PARAMS,
        name="dispatch",
    )(gathered)

    table = lax.dynamic_index_in_dim(
        came_from.reshape(N_DP, N_EP, ROWS), my_ep, 1, keepdims=False
    )
    src_dp = table // (N_EP * ROWS)
    src_row = table % ROWS
    src_flat = (src_dp * ROWS + src_row).reshape(N_DP * ROWS)
    flat = lax.iota(jnp.int32, N_DP * ROWS)
    hit = src_flat[:, None] == flat[None, :]
    crosses = (flat // ROWS)[:, None] != (flat // ROWS)[None, :]
    away = jnp.any(hit & crosses, axis=0).reshape(N_DP, ROWS).astype(jnp.int32)
    rows_before = lax.iota(jnp.int32, ROWS)[:, None] < lax.iota(jnp.int32, ROWS)[None, :]
    label = jnp.sum(away[:, :, None] * rows_before[None], axis=1)
    label_of = jnp.sum(jnp.where(hit, label.reshape(1, -1), 0), axis=1).reshape(N_DP, ROWS)
    arriving = (src_dp != lax.iota(jnp.int32, N_DP)[:, None]).astype(jnp.int32)
    turn = jnp.sum(arriving[:, :, None] * rows_before[None], axis=1)
    source = src_dp * 2 + label_of
    pick = (turn[:, :, None] == lax.iota(jnp.int32, 2)) & (arriving[:, :, None] == 1)
    forward_idx = jnp.sum(jnp.where(pick, source[:, :, None], 0), axis=1).reshape(2 * N_DP)
    my_away = lax.dynamic_index_in_dim(away, my_dp, 0, keepdims=False)
    my_label = lax.dynamic_index_in_dim(label, my_dp, 0, keepdims=False)
    leave = (my_label[:, None] == lax.iota(jnp.int32, 2)) & (my_away[:, None] == 1)
    leaving = jnp.sum(jnp.where(leave, lax.iota(jnp.int32, ROWS)[:, None], 0), axis=0)
    my_src = lax.dynamic_index_in_dim(table, my_dp, 0, keepdims=False)
    my_src_flat = lax.dynamic_index_in_dim(
        src_flat.reshape(N_DP, ROWS), my_dp, 0, keepdims=False
    )
    my_arriving = lax.dynamic_index_in_dim(arriving, my_dp, 0, keepdims=False)
    my_turn = lax.dynamic_index_in_dim(turn, my_dp, 0, keepdims=False)
    own_len = lax.dynamic_slice_in_dim(lengths, my_dev * ROWS, ROWS)
    second_len = jnp.take(lengths, my_src)
    old_table = jnp.concatenate(
        [
            second_len,
            jnp.where(my_arriving == 1, 0, my_src % ROWS),
            jnp.where(my_arriving == 1, my_turn, 0),
            my_arriving,
        ]
    ).astype(jnp.int32)

    first_old = old0(own_len, qt, cache_t)

    two = jnp.concatenate(
        [lax.dynamic_slice_in_dim(cache_t, leaving[n], 1, 0) for n in range(2)], axis=0
    )
    pieces = two.reshape(2, 8, 72, 2, 256).transpose(1, 3, 0, 2, 4).reshape(N_DP, 2, 72, 256)
    spread = lax.all_to_all(pieces, "dp", split_axis=0, concat_axis=0, tiled=True)
    onward = forward(forward_idx, spread.reshape(2 * N_DP, 72, 256))

    positions = jnp.stack([own_len, second_len + 1]).astype(F32)
    freq = 10000.0 ** (-2.0 * jnp.arange(32, dtype=F32) / 64)
    angle = positions[:, :, None] * jnp.tile(freq, 4)[None, None, :]
    keep = jnp.arange(128) < 64
    cosine = jnp.where(keep, jnp.cos(angle), 0.0)
    sine = jnp.where(keep, jnp.sin(angle), 0.0)

    keys = []
    mixes = []
    arrived = [
        lax.all_to_all(sends[s], "dp", split_axis=0, concat_axis=0, tiled=True) for s in range(2)
    ]
    landed = lax.all_to_all(
        onward.reshape(N_DP, 2, 72, 256), "dp", split_axis=0, concat_axis=0, tiled=True
    )
    moved = landed.reshape(8, 2, 2, 72, 256).transpose(2, 0, 3, 1, 4).reshape(2, KV, 512)
    second_old = old1(old_table, qt, cache_t, moved)
    for s in range(2):
        result = experts(at, arrived[s], w_gate, w_up, w_down)
        returned = lax.all_to_all(result, "dp", split_axis=0, concat_axis=0, tiled=True)
        partial = pl.pallas_call(
            functools.partial(combine_kernel, s),
            in_specs=[VMEM] * 3,
            out_specs=VMEM,
            out_shape=jax.ShapeDtypeStruct((N_EP, ROWS, KVW + SLICE), F32),
            compiler_params=PARAMS,
            cost_estimate=cost(4e8, 4e6),
            name="combine%d" % s,
        )(gathered, returned, latent_t)
        summed = lax.all_to_all(partial, "ep", split_axis=0, concat_axis=0, tiled=True)
        key, mixed = pl.pallas_call(
            key_kernel,
            in_specs=[VMEM] * 3,
            out_specs=[VMEM, VMEM],
            out_shape=[
                jax.ShapeDtypeStruct((ROWS, KEYW), BF16),
                jax.ShapeDtypeStruct((ROWS, D), BF16),
            ],
            compiler_params=PARAMS,
            name="key%d" % s,
        )(summed, cosine[s], sine[s])
        keys.append(key)
        mixes.append(mixed)
    attended = merge(0, qt, first_old, [keys[0]], None)
    everyone = lax.all_to_all(
        jnp.broadcast_to(keys[0][None], (N_DP, ROWS, KEYW)),
        "dp",
        split_axis=0,
        concat_axis=0,
        tiled=True,
    ).reshape(N_DP * ROWS, KEYW)
    select = (my_src_flat[:, None] == flat[None, :]).astype(BF16)
    first_for_second = jnp.dot(select, everyone, preferred_element_type=F32).astype(BF16)
    attended = merge(1, qt, second_old, [first_for_second, keys[1]], attended)
    expert_out = jnp.stack(mixes)
    return (expert_out, attended)


def solution(mesh):
    in_specs = (
        P(None, ("dp", "ep"), None),
        P(None, ("dp", "ep"), None),
        P(None, ("dp", "ep"), None),
        P("dp", "ep", None),
        P("dp", "ep", None),
        P("dp", None, "ep"),
        P("ep", None),
        P(None, ("dp", "ep"), None, None),
        P(("dp", "ep"), None, None),
        P(),
        P(),
    )
    out_specs = (P(None, ("dp", "ep"), None), P(None, ("dp", "ep"), None, None))
    return jax.shard_map(local, mesh=mesh, in_specs=in_specs, out_specs=out_specs, check_vma=False)
```

time: 642 us -> 266 us (0.41)
  the two profiles are of different devices: /device:TPU:80 before, /device:TPU:0 now
where the time goes in v1:
time: 266 us; the launch traced here: 263 us
  waiting for transfers between devices  66.8 us (25%)
  starting transfers between devices  65.4 us (25%)
  Pallas kernels  63.5 us (24%)
  local copies, waits for them, and re-layouts  38.7 us (15%)
  blocking collectives  11.7 us (4%)
  other arithmetic  10.4 us (4%)
  between operations  4.98 us (2%)
    ppermute x22, waiting for transfers between devices, hop(): return lax.ppermute(v, 'ep', pairs)  34.3 us
    all_to_all x2, waiting for transfers between devices, local(): lax.all_to_all(sends[s], 'dp', split_axis=0, concat_axis=0, tiled=True)  19.7 us
    unnamed x48, local copies, waits for them, and re-layouts  19.2 us
    pallas_call x2, Pallas kernels, gate_up(): pl.pallas_call(gateup_kernel, grid_spec=pltpu.PrefetchScalarGridSpec(num_...  16.6 us
    ppermute x22, starting transfers between devices, hop(): return lax.ppermute(v, 'ep', pairs)  14.9 us
    all_to_all x2, starting transfers between devices, local(): lax.all_to_all(result, 'dp', split_axis=0, concat_axis=0, tiled=True)  14.3 us
    all_to_all x2, starting transfers between devices, local(): lax.all_to_all(sends[s], 'dp', split_axis=0, concat_axis=0, tiled=True)  11.8 us
    all_to_all x1, blocking collectives, local(): lax.all_to_all(packed, 'ep', split_axis=0, concat_axis=0, tiled=True)  11.7 us
  transfers between devices with their start and end apart: 31, of which 12 were waited for; matrix products, arithmetic and copies ran while one was open for 11% of the time, Pallas kernels for 21%

profile of v1, /device:TPU:0, one launch (start us, length us, event | category | flops | bytes accessed | tf_op | source)
XLA Modules:
  0.0 262.6 jit_solution(3684732409263196324)
XLA Ops:
  3.2 11.7 %all_to_all.50.r_ref = bf16[8,16,1024]{2,1,0:T(8,128)(2,1)S(1)} all-to-all(bf16[8,16,1024]{2,1,0:T(8,128)(2,1)S(1)} %pack.1), channel_id=1, replica_groups=mesh['dp'=16,'ep'=8] {'ep'}, dimensions={0} | all-to-all | bytes 524288 | tf_op jit(solution)/shard_map/all_to_all | solution.py:461
  17.2 8.0 %all-to-all-start.1 = ((bf16[16,48,896]{2,1,0:T(8,128)(2,1)}), bf16[16,48,896]{2,1,0:T(8,128)(2,1)S(1)}, u32[]{:S(2)}, u32[]{:S(2)}) async-start(bf16[16,48,896]{2,1,0:T(8,128)(2,1)} %get-tuple-element.16), calls=%async_computation.1 | async-start | bytes 2752512 | tf_op jit(solution)/shard_map/all_to_all | solution.py:530
  26.7 19.7 %all-to-all-done.1.x_ref = bf16[16,48,896]{2,1,0:T(8,128)(2,1)S(1)} async-done(((bf16[16,48,896]{2,1,0:T(8,128)(2,1)}), bf16[16,48,896]{2,1,0:T(8,128)(2,1)S(1)}, u32[]{:S(2)}, u32[]{:S(2)}) %all-to-all-start.1) | async-done | bytes 1376288 | tf_op jit(solution)/shard_map/all_to_all | solution.py:530
  47.5 3.7 %all-to-all-start.4 = ((bf16[16,48,896]{2,1,0:T(8,128)(2,1)}), bf16[16,48,896]{2,1,0:T(8,128)(2,1)S(1)}, u32[]{:S(2)}, u32[]{:S(2)}) async-start(bf16[16,48,896]{2,1,0:T(8,128)(2,1)} %get-tuple-element.20), calls=%async_computation.4 | async-start | bytes 2752512 | tf_op jit(solution)/shard_map/all_to_all | solution.py:530
  52.5 8.3 %gate_up.2 = (bf16[4,2,384,256]{3,2,1,0:T(8,128)(2,1)S(1)}, bf16[4,2,384,256]{3,2,1,0:T(8,128)(2,1)}) custom-call(s32[2]{0:T(128)S(1)} %pad_add_fusion.at_ref, bf16[16,48,896]{2,1,0:T(8,128)(2,1)S(1)} %copy-done.12, bf16[2,896,1024]{2,1,0:T(8,128)(2,1)} %wg_ref.3, bf16[2,896,1024]{2,1,0:T(8,128)(2,1)} %wu_ref.3), custom_call_target="tpu_custom_call" | custom-call | flops 4000000000 | bytes 12000000 | tf_op jit(solution)/shard_map/gate_up/pallas_call | solution.py:138
  69.1 3.7 %reshape.361 = bf16[2,8,72,2,256]{4,3,2,1,0:T(2,128)(2,1)} reshape(bf16[2,576,512]{2,1,0:T(8,128)(2,1)} %pad_maximum_fusion) | data formatting | bytes 2359296 | tf_op jit(solution)/shard_map/reshape | solution.py:516
  76.4 7.2 %all-to-all-start.7 = ((bf16[16,2,72,256]{3,2,1,0:T(8,128)(2,1)}), bf16[16,2,72,256]{3,2,1,0:T(8,128)(2,1)S(1)}, u32[]{:S(2)}, u32[]{:S(2)}) async-start(bf16[16,2,72,256]{3,2,1,0:T(8,128)(2,1)} %bitcast.113), calls=%async_computation.7 | async-start | bytes 2359296 | tf_op jit(solution)/shard_map/all_to_all | solution.py:517
  84.9 8.3 %gate_up.3 = (bf16[4,2,384,256]{3,2,1,0:T(8,128)(2,1)S(1)}, bf16[4,2,384,256]{3,2,1,0:T(8,128)(2,1)}) custom-call(s32[2]{0:T(128)S(1)} %pad_add_fusion.at_ref, bf16[16,48,896]{2,1,0:T(8,128)(2,1)S(1)} %copy-done.10, bf16[2,896,1024]{2,1,0:T(8,128)(2,1)} %wg_ref.3, bf16[2,896,1024]{2,1,0:T(8,128)(2,1)} %wu_ref.3), custom_call_target="tpu_custom_call" | custom-call | flops 4000000000 | bytes 12000000 | tf_op jit(solution)/shard_map/gate_up/pallas_call | solution.py:138
  99.4 4.2 %all-to-all-done.7 = bf16[16,2,72,256]{3,2,1,0:T(8,128)(2,1)S(1)} async-done(((bf16[16,2,72,256]{3,2,1,0:T(8,128)(2,1)}), bf16[16,2,72,256]{3,2,1,0:T(8,128)(2,1)S(1)}, u32[]{:S(2)}, u32[]{:S(2)}) %all-to-all-start.7) | async-done | bytes 1179680 | tf_op jit(solution)/shard_map/all_to_all | solution.py:517
  105.4 4.4 %all-to-all-start.8 = ((bf16[16,2,72,256]{3,2,1,0:T(8,128)(2,1)}), bf16[16,2,72,256]{3,2,1,0:T(8,128)(2,1)}, u32[]{:S(2)}, u32[]{:S(2)}) async-start(bf16[16,2,72,256]{3,2,1,0:T(8,128)(2,1)} %bitcast.34), calls=%async_computation.8 | async-start | bytes 2359296 | tf_op jit(solution)/shard_map/all_to_all | solution.py:532
  111.2 7.4 %collective-permute-done.1 = bf16[2,384,256]{2,1,0:T(8,128)(2,1)} collective-permute-done((bf16[2,384,256]{2,1,0:T(8,128)(2,1)}, bf16[2,384,256]{2,1,0:T(8,128)(2,1)}, u32[]{:S(2)}, u32[]{:S(2)}) %collective-permute-start.1) | collective-permute-done | bytes 393248 | tf_op jit(solution)/shard_map/ppermute | solution.py:404
  120.3 3.2 %collective-permute-start.5 = (bf16[2,384,128]{2,1,0:T(8,128)(2,1)S(1)}, bf16[2,384,128]{2,1,0:T(8,128)(2,1)S(1)}, u32[]{:S(2)}, u32[]{:S(2)}) collective-permute-start(bf16[2,384,128]{2,1,0:T(8,128)(2,1)S(1)} %fusion.11.refs_0_), channel_id=1, source_target_pairs={{0,6},{1,7},{2,0},{3,1},{4,2},{5,3},{6,4},{7,5},{8,14},{9,15},{10,... | collective-permute-start | bytes 589832 | tf_op jit(solution)/shard_map/ppermute | solution.py:404
  123.8 8.7 %collective-permute-done.4.refs_1_ = bf16[2,384,128]{2,1,0:T(8,128)(2,1)S(1)} collective-permute-done((bf16[2,384,128]{2,1,0:T(8,128)(2,1)S(1)}, bf16[2,384,128]{2,1,0:T(8,128)(2,1)S(1)}, u32[]{:S(2)}, u32[]{:S(2)}) %collective-permute-start.4) | collective-permute-done | bytes 196640 | tf_op jit(solution)/shard_map/ppermute | solution.py:404
  138.6 4.9 %down.2 = bf16[16,48,896]{2,1,0:T(8,128)(2,1)} custom-call(s32[2]{0:T(128)S(1)} %pad_add_fusion.at_ref, bf16[2,384,128]{2,1,0:T(8,128)(2,1)S(1)} %fusion.11.refs_0_, bf16[2,384,128]{2,1,0:T(8,128)(2,1)S(1)} %collective-permute-done.4.refs_1_, bf16[2,384,128]{2,1,0:T(8,128)(2,1)S(1)} %collective-permute-done.5.refs_2_, ...), custom_call_target="tpu_custom_call" | custom-call | flops 2000000000 | bytes 8000000 | tf_op jit(solution)/shard_map/down/pallas_call | solution.py:180
  143.5 7.1 %all-to-all-start.2 = ((bf16[16,48,896]{2,1,0:T(8,128)(2,1)}), bf16[16,48,896]{2,1,0:T(8,128)(2,1)}, u32[]{:S(2)}, u32[]{:S(2)}) async-start(bf16[16,48,896]{2,1,0:T(8,128)(2,1)} %down.2), calls=%async_computation.2 | async-start | bytes 2752512 | tf_op jit(solution)/shard_map/all_to_all | solution.py:539
  154.6 3.7 %collective-permute-done.12 = bf16[2,384,256]{2,1,0:T(8,128)(2,1)} collective-permute-done((bf16[2,384,256]{2,1,0:T(8,128)(2,1)S(1)}, bf16[2,384,256]{2,1,0:T(8,128)(2,1)}, u32[]{:S(2)}, u32[]{:S(2)}) %collective-permute-start.12) | collective-permute-done | bytes 393248 | tf_op jit(solution)/shard_map/ppermute | solution.py:404
  160.2 3.2 %collective-permute-start.16 = (bf16[2,384,128]{2,1,0:T(8,128)(2,1)S(1)}, bf16[2,384,128]{2,1,0:T(8,128)(2,1)S(1)}, u32[]{:S(2)}, u32[]{:S(2)}) collective-permute-start(bf16[2,384,128]{2,1,0:T(8,128)(2,1)S(1)} %fusion.10.refs_0_), channel_id=1, source_target_pairs={{0,6},{1,7},{2,0},{3,1},{4,2},{5,3},{6,4},{7,5},{8,14},{9,15},{10,... | collective-permute-start | bytes 589832 | tf_op jit(solution)/shard_map/ppermute | solution.py:404
  163.5 8.9 %collective-permute-done.15.refs_1_ = bf16[2,384,128]{2,1,0:T(8,128)(2,1)S(1)} collective-permute-done((bf16[2,384,128]{2,1,0:T(8,128)(2,1)S(1)}, bf16[2,384,128]{2,1,0:T(8,128)(2,1)S(1)}, u32[]{:S(2)}, u32[]{:S(2)}) %collective-permute-start.15) | collective-permute-done | bytes 196640 | tf_op jit(solution)/shard_map/ppermute | solution.py:404
  174.4 3.8 %down.3 = bf16[16,48,896]{2,1,0:T(8,128)(2,1)S(1)} custom-call(s32[2]{0:T(128)S(1)} %pad_add_fusion.at_ref, bf16[2,384,128]{2,1,0:T(8,128)(2,1)S(1)} %fusion.10.refs_0_, bf16[2,384,128]{2,1,0:T(8,128)(2,1)S(1)} %collective-permute-done.15.refs_1_, bf16[2,384,128]{2,1,0:T(8,128)(2,1)S(1)} %collective-permute-done.16.refs_2_, ...), custom_call_target="tpu_custom_call" | custom-call | flops 2000000000 | bytes 8000000 | tf_op jit(solution)/shard_map/down/pallas_call | solution.py:180
  179.3 7.1 %all-to-all-start.5 = ((bf16[16,48,896]{2,1,0:T(8,128)(2,1)}), bf16[16,48,896]{2,1,0:T(8,128)(2,1)}, u32[]{:S(2)}, u32[]{:S(2)}) async-start(bf16[16,48,896]{2,1,0:T(8,128)(2,1)} %copy-done.13), calls=%async_computation.5 | async-start | bytes 2752512 | tf_op jit(solution)/shard_map/all_to_all | solution.py:539
  186.6 8.0 %old0.1 = (f32[8,128,512]{2,1,0:T(8,128)S(1)}, f32[8,128,128]{2,1,0:T(8,128)S(1)}) custom-call(s32[8]{0:T(128)S(1)} %dynamic_slice.32.len_ref, bf16[2,8,576,128]{3,2,1,0:T(8,128)(2,1)S(1)} %bitcast.104, bf16[8,576,512]{2,1,0:T(8,128)(2,1)} %bitcast.115), custom_call_target="tpu_custom_call" | custom-call | flops 5000000000 | bytes 8000000 | tf_op jit(solution)/shard_map/old0/pallas_call | solution.py:279
  196.7 3.2 %combine0.1 = f32[8,8,1664]{2,1,0:T(8,128)} custom-call(bf16[8,16,1024]{2,1,0:T(8,128)(2,1)S(1)} %all_to_all.50.r_ref, bf16[16,48,896]{2,1,0:T(8,128)(2,1)} %all-to-all-done.2.ret_ref, bf16[576,896]{1,0:T(8,128)(2,1)S(1)} %bitcast.109), custom_call_target="tpu_custom_call" | custom-call | flops 400000000 | bytes 4000000 | tf_op jit(solution)/shard_map/combine0/pallas_call | solution.py:540
  200.0 8.6 %all-to-all-done.5.ret_ref = bf16[16,48,896]{2,1,0:T(8,128)(2,1)} async-done(((bf16[16,48,896]{2,1,0:T(8,128)(2,1)}), bf16[16,48,896]{2,1,0:T(8,128)(2,1)}, u32[]{:S(2)}, u32[]{:S(2)}) %all-to-all-start.5) | async-done | bytes 1376288 | tf_op jit(solution)/shard_map/all_to_all | solution.py:539
  208.6 4.0 %all-to-all-start.3 = ((f32[8,8,1664]{2,1,0:T(8,128)}), f32[8,8,1664]{2,1,0:T(8,128)S(1)}, u32[]{:S(2)}, u32[]{:S(2)}) async-start(f32[8,8,1664]{2,1,0:T(8,128)} %combine0.1), calls=%async_computation.3 | async-start | bytes 851968 | tf_op jit(solution)/shard_map/all_to_all | solution.py:549
  212.6 3.2 %copy.40 = bf16[2,8,72,2,256]{4,3,2,1,0:T(2,128)(2,1)} copy(bf16[2,8,72,2,256]{4,2,0,3,1:T(8,128)(2,1)} %bitcast.36) | data formatting | bytes 2359296 | tf_op jit(solution)/shard_map/transpose | solution.py:535
  215.8 3.9 %reshape.366.mig_ref = bf16[2,576,512]{2,1,0:T(8,128)(2,1)} reshape(bf16[2,8,72,2,256]{4,3,2,1,0:T(2,128)(2,1)} %copy.40) | data formatting | bytes 2359296 | tf_op jit(solution)/shard_map/reshape | solution.py:535
  220.9 3.2 %combine1.1 = f32[8,8,1664]{2,1,0:T(8,128)} custom-call(bf16[8,16,1024]{2,1,0:T(8,128)(2,1)S(1)} %all_to_all.50.r_ref, bf16[16,48,896]{2,1,0:T(8,128)(2,1)} %all-to-all-done.5.ret_ref, bf16[576,896]{1,0:T(8,128)(2,1)S(1)} %bitcast.110), custom_call_target="tpu_custom_call" | custom-call | flops 400000000 | bytes 4000000 | tf_op jit(solution)/shard_map/combine1/pallas_call | solution.py:540
  224.2 4.8 %all-to-all-start.6 = ((f32[8,8,1664]{2,1,0:T(8,128)}), f32[8,8,1664]{2,1,0:T(8,128)S(1)}, u32[]{:S(2)}, u32[]{:S(2)}) async-start(f32[8,8,1664]{2,1,0:T(8,128)} %combine1.1), calls=%async_computation.6 | async-start | bytes 851968 | tf_op jit(solution)/shard_map/all_to_all | solution.py:549
  230.2 8.0 %old1.1 = (f32[8,128,512]{2,1,0:T(8,128)S(1)}, f32[8,128,128]{2,1,0:T(8,128)S(1)}) custom-call(s32[32]{0:T(128)S(1)} %pad_add_fusion.1.tab_ref, bf16[2,8,576,128]{3,2,1,0:T(8,128)(2,1)S(1)} %bitcast.105, bf16[8,576,512]{2,1,0:T(8,128)(2,1)} %bitcast.116, bf16[2,576,512]{2,1,0:T(8,128)(2,1)S(1)} %copy-done.14), custom_call_target="tpu_custom_call" | custom-call | flops 5000000000 | bytes 8000000 | tf_op jit(solution)/shard_map/old1/pallas_call | solution.py:298
  241.2 4.2 %all-to-all-start.9 = ((bf16[16,8,640]{2,1,0:T(8,128)(2,1)}), bf16[16,8,640]{2,1,0:T(8,128)(2,1)}, u32[]{:S(2)}, u32[]{:S(2)}) async-start(bf16[16,8,640]{2,1,0:T(8,128)(2,1)} %broadcast_in_dim.92), calls=%async_computation.9 | async-start | bytes 327680 | tf_op jit(solution)/shard_map/all_to_all | solution.py:564
  248.9 5.3 %merge0.1.refs_2_ = bf16[2,8,128,512]{3,2,1,0:T(8,128)(2,1)} custom-call(bf16[2,8,576,128]{3,2,1,0:T(8,128)(2,1)S(1)} %bitcast.106, f32[8,128,512]{2,1,0:T(8,128)S(1)} %copy-done.4, f32[8,128,128]{2,1,0:T(8,128)S(1)} %copy-done.16, bf16[8,640]{1,0:T(8,128)(2,1)S(1)} %get-tuple-element.26.refs_0_), custom_call_target="tpu_custom_call" | custom-call | flops 100000000 | bytes 5000000 | tf_op jit(solution)/shard_map/merge0/pallas_call | solution.py:361
  256.9 5.7 %merge1.1 = bf16[2,8,128,512]{3,2,1,0:T(8,128)(2,1)} custom-call(bf16[2,8,576,128]{3,2,1,0:T(8,128)(2,1)S(1)} %bitcast.107, f32[8,128,512]{2,1,0:T(8,128)S(1)} %copy-done.6, f32[8,128,128]{2,1,0:T(8,128)S(1)} %copy-done.18, bf16[8,640]{1,0:T(8,128)(2,1)S(1)} %convolution_convert_fusion.refs_0_, ...), custom_call_target="tpu_custom_call", output_to_operand_aliasing={{}: (5, {})} | custom-call | flops 100000000 | bytes 5000000 | tf_op jit(solution)/shard_map/merge1/pallas_call | solution.py:361
  (156 shorter events, 58.2 us)
Async XLA Ops:
  17.2 29.2 %all-to-all-start.1 = ((bf16[16,48,896]{2,1,0:T(8,128)(2,1)}), bf16[16,48,896]{2,1,0:T(8,128)(2,1)S(1)}, u32[]{:S(2)}, u32[]{:S(2)}) async-start(bf16[16,48,896]{2,1,0:T(8,128)(2,1)} %get-tuple-element.16), calls=%async_computation.1 | async-start | bytes 2752512 | tf_op jit(solution)/shard_map/all_to_all | solution.py:530
  47.5 27.8 %all-to-all-start.4 = ((bf16[16,48,896]{2,1,0:T(8,128)(2,1)}), bf16[16,48,896]{2,1,0:T(8,128)(2,1)S(1)}, u32[]{:S(2)}, u32[]{:S(2)}) async-start(bf16[16,48,896]{2,1,0:T(8,128)(2,1)} %get-tuple-element.20), calls=%async_computation.4 | async-start | bytes 2752512 | tf_op jit(solution)/shard_map/all_to_all | solution.py:530
  60.9 32.5 %collective-permute-start = (bf16[4,2,384,256]{3,2,1,0:T(8,128)(2,1)}, bf16[4,2,384,256]{3,2,1,0:T(8,128)(2,1)}, u32[]{:S(2)}, u32[]{:S(2)}) collective-permute-start(bf16[4,2,384,256]{3,2,1,0:T(8,128)(2,1)} %get-tuple-element.18), channel_id=1, source_target_pairs={{0,1},{1,0},{2,3},{3,2},{4,5},{5,4},{6,7},{7,6},{8,9},{9,8},{10,11... | collective-permute-start | bytes 4718600 | tf_op jit(solution)/shard_map/ppermute | solution.py:404
  76.4 27.2 %all-to-all-start.7 = ((bf16[16,2,72,256]{3,2,1,0:T(8,128)(2,1)}), bf16[16,2,72,256]{3,2,1,0:T(8,128)(2,1)S(1)}, u32[]{:S(2)}, u32[]{:S(2)}) async-start(bf16[16,2,72,256]{3,2,1,0:T(8,128)(2,1)} %bitcast.113), calls=%async_computation.7 | async-start | bytes 2359296 | tf_op jit(solution)/shard_map/all_to_all | solution.py:517
  93.2 40.0 %collective-permute-start.11 = (bf16[4,2,384,256]{3,2,1,0:T(8,128)(2,1)}, bf16[4,2,384,256]{3,2,1,0:T(8,128)(2,1)}, u32[]{:S(2)}, u32[]{:S(2)}) collective-permute-start(bf16[4,2,384,256]{3,2,1,0:T(8,128)(2,1)} %get-tuple-element.22), channel_id=1, source_target_pairs={{0,1},{1,0},{2,3},{3,2},{4,5},{5,4},{6,7},{7,6},{8,9},{9,8},{10,11... | collective-permute-start | bytes 4718600 | tf_op jit(solution)/shard_map/ppermute | solution.py:404
  96.1 13.7 %collective-permute-start.3 = (bf16[2,384,256]{2,1,0:T(8,128)(2,1)}, bf16[2,384,256]{2,1,0:T(8,128)(2,1)}, u32[]{:S(2)}, u32[]{:S(2)}) collective-permute-start(bf16[2,384,256]{2,1,0:T(8,128)(2,1)} %get-tuple-element.39), channel_id=1, source_target_pairs={{0,6},{1,7},{2,0},{3,1},{4,2},{5,3},{6,4},{7,5},{8,14},{9,15},{10,... | collective-permute-start | bytes 1179656 | tf_op jit(solution)/shard_map/ppermute | solution.py:404
  97.3 13.8 %collective-permute-start.2 = (bf16[2,384,256]{2,1,0:T(8,128)(2,1)}, bf16[2,384,256]{2,1,0:T(8,128)(2,1)}, u32[]{:S(2)}, u32[]{:S(2)}) collective-permute-start(bf16[2,384,256]{2,1,0:T(8,128)(2,1)} %get-tuple-element.40), channel_id=1, source_target_pairs={{0,4},{1,5},{2,6},{3,7},{4,0},{5,1},{6,2},{7,3},{8,12},{9,13},{10,... | collective-permute-start | bytes 1179656 | tf_op jit(solution)/shard_map/ppermute | solution.py:404
  98.8 19.7 %collective-permute-start.1 = (bf16[2,384,256]{2,1,0:T(8,128)(2,1)}, bf16[2,384,256]{2,1,0:T(8,128)(2,1)}, u32[]{:S(2)}, u32[]{:S(2)}) collective-permute-start(bf16[2,384,256]{2,1,0:T(8,128)(2,1)} %get-tuple-element.38), channel_id=1, source_target_pairs={{0,2},{1,3},{2,4},{3,5},{4,6},{5,7},{6,0},{7,1},{8,10},{9,11},{10,... | collective-permute-start | bytes 1179656 | tf_op jit(solution)/shard_map/ppermute | solution.py:404
  105.4 38.1 %all-to-all-start.8 = ((bf16[16,2,72,256]{3,2,1,0:T(8,128)(2,1)}), bf16[16,2,72,256]{3,2,1,0:T(8,128)(2,1)}, u32[]{:S(2)}, u32[]{:S(2)}) async-start(bf16[16,2,72,256]{3,2,1,0:T(8,128)(2,1)} %bitcast.34), calls=%async_computation.8 | async-start | bytes 2359296 | tf_op jit(solution)/shard_map/all_to_all | solution.py:532
  109.8 23.3 %copy-start.8 = (bf16[4,2,384,256]{3,2,1,0:T(8,128)(2,1)S(1)}, bf16[4,2,384,256]{3,2,1,0:T(8,128)(2,1)}, u32[]{:S(2)}) copy-start(bf16[4,2,384,256]{3,2,1,0:T(8,128)(2,1)} %copy-done.7) | copy-start | bytes 4718596
  120.2 12.3 %collective-permute-start.4 = (bf16[2,384,128]{2,1,0:T(8,128)(2,1)S(1)}, bf16[2,384,128]{2,1,0:T(8,128)(2,1)S(1)}, u32[]{:S(2)}, u32[]{:S(2)}) collective-permute-start(bf16[2,384,128]{2,1,0:T(8,128)(2,1)S(1)} %fusion.11.refs_0_), channel_id=1, source_target_pairs={{0,2},{1,3},{2,4},{3,5},{4,6},{5,7},{6,0},{7,1},{8,10},{9,11},{10,... | collective-permute-start | bytes 589832 | tf_op jit(solution)/shard_map/ppermute | solution.py:404
  120.3 12.2 %collective-permute-start.5 = (bf16[2,384,128]{2,1,0:T(8,128)(2,1)S(1)}, bf16[2,384,128]{2,1,0:T(8,128)(2,1)S(1)}, u32[]{:S(2)}, u32[]{:S(2)}) collective-permute-start(bf16[2,384,128]{2,1,0:T(8,128)(2,1)S(1)} %fusion.11.refs_0_), channel_id=1, source_target_pairs={{0,6},{1,7},{2,0},{3,1},{4,2},{5,3},{6,4},{7,5},{8,14},{9,15},{10,... | collective-permute-start | bytes 589832 | tf_op jit(solution)/shard_map/ppermute | solution.py:404
  123.5 9.5 %collective-permute-start.6 = (bf16[2,384,128]{2,1,0:T(8,128)(2,1)S(1)}, bf16[2,384,128]{2,1,0:T(8,128)(2,1)S(1)}, u32[]{:S(2)}, u32[]{:S(2)}) collective-permute-start(bf16[2,384,128]{2,1,0:T(8,128)(2,1)S(1)} %fusion.11.refs_0_), channel_id=1, source_target_pairs={{0,4},{1,5},{2,6},{3,7},{4,0},{5,1},{6,2},{7,3},{8,12},{9,13},{10,... | collective-permute-start | bytes 589832 | tf_op jit(solution)/shard_map/ppermute | solution.py:404
  123.8 13.8 %collective-permute-start.7 = (bf16[2,384,128]{2,1,0:T(8,128)(2,1)S(1)}, bf16[2,384,128]{2,1,0:T(8,128)(2,1)S(1)}, u32[]{:S(2)}, u32[]{:S(2)}) collective-permute-start(bf16[2,384,128]{2,1,0:T(8,128)(2,1)S(1)} %fusion.11.refs_0_), channel_id=1, source_target_pairs={{0,1},{1,0},{2,3},{3,2},{4,5},{5,4},{6,7},{7,6},{8,9},{9,8},{10,11... | collective-permute-start | bytes 589832 | tf_op jit(solution)/shard_map/ppermute | solution.py:404
  132.5 5.1 %collective-permute-start.8 = (bf16[2,384,128]{2,1,0:T(8,128)(2,1)S(1)}, bf16[2,384,128]{2,1,0:T(8,128)(2,1)S(1)}, u32[]{:S(2)}, u32[]{:S(2)}) collective-permute-start(bf16[2,384,128]{2,1,0:T(8,128)(2,1)S(1)} %collective-permute-done.4.refs_1_), channel_id=1, source_target_pairs={{0,1},{1,0},{2,3},{3,2},{4,5},{5,4},{6,7},{7,6},{8,9},{9,8},{10,11... | collective-permute-start | bytes 589832 | tf_op jit(solution)/shard_map/ppermute | solution.py:404
  132.5 6.0 %collective-permute-start.9 = (bf16[2,384,128]{2,1,0:T(8,128)(2,1)S(1)}, bf16[2,384,128]{2,1,0:T(8,128)(2,1)S(1)}, u32[]{:S(2)}, u32[]{:S(2)}) collective-permute-start(bf16[2,384,128]{2,1,0:T(8,128)(2,1)S(1)} %collective-permute-done.5.refs_2_), channel_id=1, source_target_pairs={{0,1},{1,0},{2,3},{3,2},{4,5},{5,4},{6,7},{7,6},{8,9},{9,8},{10,11... | collective-permute-start | bytes 589832 | tf_op jit(solution)/shard_map/ppermute | solution.py:404
  133.1 5.5 %collective-permute-start.10 = (bf16[2,384,128]{2,1,0:T(8,128)(2,1)S(1)}, bf16[2,384,128]{2,1,0:T(8,128)(2,1)S(1)}, u32[]{:S(2)}, u32[]{:S(2)}) collective-permute-start(bf16[2,384,128]{2,1,0:T(8,128)(2,1)S(1)} %collective-permute-done.6.refs_3_), channel_id=1, source_target_pairs={{0,1},{1,0},{2,3},{3,2},{4,5},{5,4},{6,7},{7,6},{8,9},{9,8},{10,11... | collective-permute-start | bytes 589832 | tf_op jit(solution)/shard_map/ppermute | solution.py:404
  134.7 20.0 %collective-permute-start.14 = (bf16[2,384,256]{2,1,0:T(8,128)(2,1)S(1)}, bf16[2,384,256]{2,1,0:T(8,128)(2,1)}, u32[]{:S(2)}, u32[]{:S(2)}) collective-permute-start(bf16[2,384,256]{2,1,0:T(8,128)(2,1)S(1)} %get-tuple-element.42), channel_id=1, source_target_pairs={{0,6},{1,7},{2,0},{3,1},{4,2},{5,3},{6,4},{7,5},{8,14},{9,15},{10,... | collective-permute-start | bytes 1179656 | tf_op jit(solution)/shard_map/ppermute | solution.py:404
  137.6 17.0 %collective-permute-start.13 = (bf16[2,384,256]{2,1,0:T(8,128)(2,1)S(1)}, bf16[2,384,256]{2,1,0:T(8,128)(2,1)}, u32[]{:S(2)}, u32[]{:S(2)}) collective-permute-start(bf16[2,384,256]{2,1,0:T(8,128)(2,1)S(1)} %get-tuple-element.43), channel_id=1, source_target_pairs={{0,4},{1,5},{2,6},{3,7},{4,0},{5,1},{6,2},{7,3},{8,12},{9,13},{10,... | collective-permute-start | bytes 1179656 | tf_op jit(solution)/shard_map/ppermute | solution.py:404
  137.6 20.7 %collective-permute-start.12 = (bf16[2,384,256]{2,1,0:T(8,128)(2,1)S(1)}, bf16[2,384,256]{2,1,0:T(8,128)(2,1)}, u32[]{:S(2)}, u32[]{:S(2)}) collective-permute-start(bf16[2,384,256]{2,1,0:T(8,128)(2,1)S(1)} %get-tuple-element.41), channel_id=1, source_target_pairs={{0,2},{1,3},{2,4},{3,5},{4,6},{5,7},{6,0},{7,1},{8,10},{9,11},{10,... | collective-permute-start | bytes 1179656 | tf_op jit(solution)/shard_map/ppermute | solution.py:404
  143.5 35.8 %all-to-all-start.2 = ((bf16[16,48,896]{2,1,0:T(8,128)(2,1)}), bf16[16,48,896]{2,1,0:T(8,128)(2,1)}, u32[]{:S(2)}, u32[]{:S(2)}) async-start(bf16[16,48,896]{2,1,0:T(8,128)(2,1)} %down.2), calls=%async_computation.2 | async-start | bytes 2752512 | tf_op jit(solution)/shard_map/all_to_all | solution.py:539
  160.1 12.3 %collective-permute-start.15 = (bf16[2,384,128]{2,1,0:T(8,128)(2,1)S(1)}, bf16[2,384,128]{2,1,0:T(8,128)(2,1)S(1)}, u32[]{:S(2)}, u32[]{:S(2)}) collective-permute-start(bf16[2,384,128]{2,1,0:T(8,128)(2,1)S(1)} %fusion.10.refs_0_), channel_id=1, source_target_pairs={{0,2},{1,3},{2,4},{3,5},{4,6},{5,7},{6,0},{7,1},{8,10},{9,11},{10,... | collective-permute-start | bytes 589832 | tf_op jit(solution)/shard_map/ppermute | solution.py:404
  160.2 12.2 %collective-permute-start.16 = (bf16[2,384,128]{2,1,0:T(8,128)(2,1)S(1)}, bf16[2,384,128]{2,1,0:T(8,128)(2,1)S(1)}, u32[]{:S(2)}, u32[]{:S(2)}) collective-permute-start(bf16[2,384,128]{2,1,0:T(8,128)(2,1)S(1)} %fusion.10.refs_0_), channel_id=1, source_target_pairs={{0,6},{1,7},{2,0},{3,1},{4,2},{5,3},{6,4},{7,5},{8,14},{9,15},{10,... | collective-permute-start | bytes 589832 | tf_op jit(solution)/shard_map/ppermute | solution.py:404
  163.4 9.5 %collective-permute-start.17 = (bf16[2,384,128]{2,1,0:T(8,128)(2,1)S(1)}, bf16[2,384,128]{2,1,0:T(8,128)(2,1)S(1)}, u32[]{:S(2)}, u32[]{:S(2)}) collective-permute-start(bf16[2,384,128]{2,1,0:T(8,128)(2,1)S(1)} %fusion.10.refs_0_), channel_id=1, source_target_pairs={{0,4},{1,5},{2,6},{3,7},{4,0},{5,1},{6,2},{7,3},{8,12},{9,13},{10,... | collective-permute-start | bytes 589832 | tf_op jit(solution)/shard_map/ppermute | solution.py:404
  163.4 9.7 %collective-permute-start.18 = (bf16[2,384,128]{2,1,0:T(8,128)(2,1)S(1)}, bf16[2,384,128]{2,1,0:T(8,128)(2,1)S(1)}, u32[]{:S(2)}, u32[]{:S(2)}) collective-permute-start(bf16[2,384,128]{2,1,0:T(8,128)(2,1)S(1)} %fusion.10.refs_0_), channel_id=1, source_target_pairs={{0,1},{1,0},{2,3},{3,2},{4,5},{5,4},{6,7},{7,6},{8,9},{9,8},{10,11... | collective-permute-start | bytes 589832 | tf_op jit(solution)/shard_map/ppermute | solution.py:404
  172.4 1.4 collective-permute-start.19
  172.4 1.7 collective-permute-start.20
  172.9 1.5 collective-permute-start.21
  179.3 29.3 %all-to-all-start.5 = ((bf16[16,48,896]{2,1,0:T(8,128)(2,1)}), bf16[16,48,896]{2,1,0:T(8,128)(2,1)}, u32[]{:S(2)}, u32[]{:S(2)}) async-start(bf16[16,48,896]{2,1,0:T(8,128)(2,1)} %copy-done.13), calls=%async_computation.5 | async-start | bytes 2752512 | tf_op jit(solution)/shard_map/all_to_all | solution.py:539
  208.6 15.6 %all-to-all-start.3 = ((f32[8,8,1664]{2,1,0:T(8,128)}), f32[8,8,1664]{2,1,0:T(8,128)S(1)}, u32[]{:S(2)}, u32[]{:S(2)}) async-start(f32[8,8,1664]{2,1,0:T(8,128)} %combine0.1), calls=%async_computation.3 | async-start | bytes 851968 | tf_op jit(solution)/shard_map/all_to_all | solution.py:549
  224.2 16.3 %all-to-all-start.6 = ((f32[8,8,1664]{2,1,0:T(8,128)}), f32[8,8,1664]{2,1,0:T(8,128)S(1)}, u32[]{:S(2)}, u32[]{:S(2)}) async-start(f32[8,8,1664]{2,1,0:T(8,128)} %combine1.1), calls=%async_computation.6 | async-start | bytes 851968 | tf_op jit(solution)/shard_map/all_to_all | solution.py:549
  241.2 13.0 %all-to-all-start.9 = ((bf16[16,8,640]{2,1,0:T(8,128)(2,1)}), bf16[16,8,640]{2,1,0:T(8,128)(2,1)}, u32[]{:S(2)}, u32[]{:S(2)}) async-start(bf16[16,8,640]{2,1,0:T(8,128)(2,1)} %broadcast_in_dim.92), calls=%async_computation.9 | async-start | bytes 327680 | tf_op jit(solution)/shard_map/all_to_all | solution.py:564
  (23 other events, 63.8 us)

commit v2 on v1

--- a/solution.py
+++ b/solution.py
@@ -114,7 +114,7 @@
         out_ref[...] = out.reshape(N_DP, PER_DP, SLICE).astype(BF16)
 
 
-def gateup_kernel(at_ref, x_ref, wg_ref, wu_ref, keep_ref, send_ref):
+def gateup_kernel(at_ref, x_ref, wg_ref, wu_ref, after_ref, keep_ref, send_ref):
     core = at_ref[1]
     for e in range(2):
         lhs = x_ref[:, 16 * e : 16 * e + 32, :].reshape(N_DP * 32, SLICE)
@@ -131,7 +131,7 @@
         send_ref[0, e, :, 128:] = jnp.where(first, u1, u0).astype(BF16)
 
 
-def gate_up(at, x, w_gate, w_up):
+def gate_up(at, x, w_gate, w_up, after):
     wspec = pl.BlockSpec((2, SLICE, 256), lambda r, a: (0, 0, (a[0] + r) % 4))
     ospec = pl.BlockSpec((1, 2, HALF, 256), lambda r, a: (r, 0, 0, 0))
     shape = jax.ShapeDtypeStruct((4, 2, HALF, 256), BF16)
@@ -144,6 +144,7 @@
                 pl.BlockSpec((N_DP, PER_DP, SLICE), lambda r, a: (0, 0, 0)),
                 wspec,
                 wspec,
+                ANY,
             ],
             out_specs=[ospec, ospec],
         ),
@@ -151,7 +152,7 @@
         compiler_params=PARAMS,
         cost_estimate=cost(4e9, 12e6),
         name="gate_up",
-    )(at, x, w_gate, w_up)
+    )(at, x, w_gate, w_up, after)
 
 
 def down_kernel(at_ref, *refs):
@@ -188,7 +189,7 @@
     )(at, *acts, w_down)
 
 
-def combine_kernel(s, r_ref, ret_ref, wl_ref, out_ref):
+def combine_kernel(s, at_ref, r_ref, ret_ref, wl_ref, own_ref, other_ref, all_ref):
     hid, _, _, gm, place = unpack(r_ref, s)
     weights = place(gm)
     high = weights.astype(BF16)
@@ -202,18 +203,35 @@
     kv = lax.dot_general(
         resid.astype(BF16), wl_ref[...], (((1,), (1,)), ((), ())), preferred_element_type=F32
     )
-    out_ref[:, :, :KV] = kv.reshape(N_EP, ROWS, KV)
-    out_ref[:, :, KEYW:KVW] = jnp.broadcast_to(square, (N_EP * ROWS, KVW - KEYW)).reshape(
+    all_ref[:, :, :KV] = kv.reshape(N_EP, ROWS, KV)
+    all_ref[:, :, KEYW:KVW] = jnp.broadcast_to(square, (N_EP * ROWS, KVW - KEYW)).reshape(
         N_EP, ROWS, KVW - KEYW
     )
-    out_ref[:, :, KV:KEYW] = jnp.zeros((N_EP, ROWS, KEYW - KV), F32)
-    out_ref[:, :, KVW:] = mixed.reshape(N_EP, ROWS, SLICE)
-
-
-def key_kernel(z_ref, cos_ref, sin_ref, key_ref, mixed_ref):
-    kv = jnp.sum(z_ref[:, :, :KVW], axis=0)
-    for j in range(N_EP):
-        mixed_ref[:, j * SLICE : (j + 1) * SLICE] = z_ref[j, :, KVW:].astype(BF16)
+    all_ref[:, :, KV:KEYW] = jnp.zeros((N_EP, ROWS, KEYW - KV), F32)
+    all_ref[:, :, KVW:] = mixed.reshape(N_EP, ROWS, SLICE)
+    for r in range(4):
+        base = 2 * ((at_ref[0] - r) & 3)
+        own_ref[r] = all_ref[base + at_ref[1]]
+        other_ref[r] = all_ref[base + 1 - at_ref[1]]
+
+
+def fold_kernel(own_ref, got_ref, *out_refs):
+    for r, out_ref in enumerate(out_refs):
+        out_ref[:, :KVW] = own_ref[r, :, :KVW] + got_ref[r, :, :KVW]
+        out_ref[:, KVW : KVW + SLICE] = own_ref[r, :, KVW:]
+        out_ref[:, KVW + SLICE :] = got_ref[r, :, KVW:]
+
+
+def key_kernel(at_ref, u0_ref, u1_ref, u2_ref, u3_ref, cos_ref, sin_ref, key_ref, block_ref, mixed_ref):
+    parts = (u0_ref, u1_ref, u2_ref, u3_ref)
+    kv = sum(u[:, :KVW] for u in parts)
+    core = at_ref[1]
+    for r, u in enumerate(parts):
+        chip = (at_ref[0] + r) & 3
+        for which, j in enumerate((2 * chip + core, 2 * chip + 1 - core)):
+            lanes = pl.ds(pl.multiple_of(j * SLICE, SLICE), SLICE)
+            cut = slice(KVW + which * SLICE, KVW + (which + 1) * SLICE)
+            mixed_ref[:, lanes] = u[:, cut]
     raw = kv[:, :KEYW] * lax.rsqrt(kv[:, KEYW : KEYW + 1] * (1.0 / D) + EPS)
     latent = raw[:, :LAT]
     latent = latent * lax.rsqrt(jnp.mean(latent * latent, axis=-1, keepdims=True) + EPS)
@@ -221,8 +239,10 @@
     lane = lax.broadcasted_iota(jnp.int32, part.shape, 1)
     turned = jnp.where(lane < 32, -pltpu.roll(part, 96, 1), pltpu.roll(part, 32, 1))
     rotated = part * cos_ref[...] + turned * sin_ref[...]
-    key_ref[:, :LAT] = latent.astype(BF16)
-    key_ref[:, LAT:] = rotated.astype(BF16)
+    key = jnp.concatenate([latent, rotated], axis=1)
+    key_ref[...] = key.astype(BF16).astype(F32)
+    tiles = [key[:, 128 * n : 128 * n + 128] for n in range(5)] + [jnp.zeros((ROWS, 128), F32)]
+    block_ref[...] = jnp.concatenate(tiles, axis=0).astype(BF16)
 
 
 def old_attention(q, kt, count):
@@ -251,18 +271,9 @@
     store_old(out_ref, stat_ref, old_attention(q_ref[0, 0], kt_ref[0], count))
 
 
-def old1_kernel(tab_ref, q_ref, kt_ref, mig_ref, out_ref, stat_ref):
-    t = pl.program_id(0)
-    count = tab_ref[t]
-    away = tab_ref[24 + t]
-
-    @pl.when(away == 0)
-    def _():
-        store_old(out_ref, stat_ref, old_attention(q_ref[0, 0], kt_ref[0], count))
-
-    @pl.when(away != 0)
-    def _():
-        store_old(out_ref, stat_ref, old_attention(q_ref[0, 0], mig_ref[0], count))
+def old1_kernel(tab_ref, q_ref, kt_ref, after_ref, out_ref, stat_ref):
+    count = tab_ref[pl.program_id(0)]
+    store_old(out_ref, stat_ref, old_attention(q_ref[0, 0], kt_ref[0], count))
 
 
 OLD_SHAPE = [
@@ -294,7 +305,7 @@
     )(lens, qt, cache_t)
 
 
-def old1(table, qt, cache_t, moved):
+def old1(table, qt, cache_t, after):
     return pl.pallas_call(
         old1_kernel,
         grid_spec=pltpu.PrefetchScalarGridSpec(
@@ -303,7 +314,7 @@
             in_specs=[
                 pl.BlockSpec((1, 1, KV, 128), lambda t, a: (1, t, 0, 0)),
                 pl.BlockSpec((1, KV, 512), lambda t, a: (a[8 + t], 0, 0)),
-                pl.BlockSpec((1, KV, 512), lambda t, a: (a[16 + t], 0, 0)),
+                ANY,
             ],
             out_specs=OLD_SPECS,
         ),
@@ -311,58 +322,65 @@
         compiler_params=PARAMS,
         cost_estimate=cost(5e9, 8e6),
         name="old1",
-    )(table, qt, cache_t, moved)
-
-
-def merge_kernel(n_new, q_ref, old_ref, stat_ref, *refs):
-    keys = refs[:n_new]
-    out_ref = refs[-1]
-    t = pl.program_id(0)
+    )(table, qt, cache_t, after)
+
+
+def add_new(q, old, keys):
+    out, top, total = old
     lane = lax.broadcasted_iota(jnp.int32, (128, ROWS), 1)
     sub = lax.broadcasted_iota(jnp.int32, (ROWS, LAT), 0)
-    top = stat_ref[0, :, 0:1]
-    total = stat_ref[0, :, 1:2]
-    q = q_ref[0, 0]
     scores = []
     values = []
-    for key_ref in keys:
+    for key, row in keys:
         both = lax.dot_general(
-            q, key_ref[:, :KV], (((0,), (1,)), ((), ())), preferred_element_type=F32
+            q, key[:, :KV].astype(BF16), (((0,), (1,)), ((), ())), preferred_element_type=F32
         )
-        scores.append(jnp.sum(jnp.where(lane == t, both, 0.0), axis=1, keepdims=True) * SCALE)
-        latent = key_ref[:, :LAT].astype(F32)
-        values.append(jnp.sum(jnp.where(sub == t, latent, 0.0), axis=0, keepdims=True))
+        scores.append(jnp.sum(jnp.where(lane == row, both, 0.0), axis=1, keepdims=True) * SCALE)
+        values.append(jnp.sum(jnp.where(sub == row, key[:, :LAT], 0.0), axis=0, keepdims=True))
     peak = top
     for s in scores:
         peak = jnp.maximum(peak, s)
     shrink = jnp.exp(top - peak)
-    out = old_ref[0] * shrink
+    out = out * shrink
     total = total * shrink
     for s, v in zip(scores, values):
         w = jnp.exp(s - peak)
         total = total + w
         out = out + w * v
-    out_ref[0, 0] = (out / total).astype(BF16)
-
-
-def merge(step, qt, old, keys, buffer):
-    n_new = len(keys)
+    return (out / total).astype(BF16)
+
+
+def merge_kernel(step, tab_ref, q_ref, old_ref, stat_ref, *refs):
+    out_ref = refs[-1]
+    t = pl.program_id(0)
+    if step == 0:
+        keys = [(refs[0][...], t)]
+    else:
+        keys = [(refs[0][...], tab_ref[8 + t]), (refs[1][...], t)]
+    old = (old_ref[0], stat_ref[0, :, 0:1], stat_ref[0, :, 1:2])
+    out_ref[0, 0] = add_new(q_ref[0, 0], old, keys)
+
+
+def merge(step, table, qt, old, keys, buffer):
     in_specs = [
-        pl.BlockSpec((1, 1, KV, 128), lambda t: (step, t, 0, 0)),
-        pl.BlockSpec((1, 128, LAT), lambda t: (t, 0, 0)),
-        pl.BlockSpec((1, 128, 128), lambda t: (t, 0, 0)),
-    ] + [pl.BlockSpec((ROWS, KEYW), lambda t: (0, 0))] * n_new
-    args = [qt, *old, *keys]
+        pl.BlockSpec((1, 1, KV, 128), lambda t, a: (step, t, 0, 0)),
+        pl.BlockSpec((1, 128, LAT), lambda t, a: (t, 0, 0)),
+        pl.BlockSpec((1, 128, 128), lambda t, a: (t, 0, 0)),
+    ] + [pl.BlockSpec((ROWS, KEYW), lambda t, a: (0, 0))] * len(keys)
+    args = [table, qt, *old, *keys]
     alias = {}
     if buffer is not None:
         in_specs.append(ANY)
         alias = {len(args): 0}
         args.append(buffer)
     return pl.pallas_call(
-        functools.partial(merge_kernel, n_new),
-        grid=(ROWS,),
-        in_specs=in_specs,
-        out_specs=pl.BlockSpec((1, 1, 128, LAT), lambda t: (step, t, 0, 0)),
+        functools.partial(merge_kernel, step),
+        grid_spec=pltpu.PrefetchScalarGridSpec(
+            num_scalar_prefetch=1,
+            grid=(ROWS,),
+            in_specs=in_specs,
+            out_specs=pl.BlockSpec((1, 1, 128, LAT), lambda t, a: (step, t, 0, 0)),
+        ),
         out_shape=jax.ShapeDtypeStruct((2, ROWS, 128, LAT), BF16),
         input_output_aliases=alias,
         compiler_params=PARAMS,
@@ -371,27 +389,104 @@
     )(*args)
 
 
-def forward_kernel(idx_ref, src_ref, out_ref, sem):
-    copies = [
-        pltpu.make_async_copy(src_ref.at[idx_ref[n]], out_ref.at[n], sem.at[n]) for n in range(2 * N_DP)
-    ]
+def moved_kernel(tab_ref, q_ref, kv_ref, keys_ref, key1_ref, buffer_ref, out_ref, kt_ref):
+    k = pl.program_id(0)
+    slot = tab_ref[24 + k]
+    for j in range(N_DP):
+        f, l = j // 4, j % 4
+        kt_ref[144 * f : 144 * f + 144, 128 * l : 128 * l + 128] = kv_ref[j]
+    raw = keys_ref[...].astype(F32)
+    where = tab_ref[16 + k]
+    pick = lax.broadcasted_iota(jnp.int32, (N_DP, ROWS, 1), 0) * ROWS
+    pick = pick + lax.broadcasted_iota(jnp.int32, (N_DP, ROWS, 1), 1)
+    rows = []
+    for n in range(5):
+        tile = jnp.where(pick == where, raw[:, 8 * n : 8 * n + 8, :], 0.0)
+        rows.append(jnp.sum(jnp.sum(tile, axis=0), axis=0, keepdims=True))
+    first = jnp.broadcast_to(jnp.concatenate(rows, axis=1), (ROWS, KEYW))
+    q = q_ref[0, 0]
+    old = old_attention(q, kt_ref[...], tab_ref[slot])
+    out_ref[0, 0] = add_new(q, old, [(first, 0), (key1_ref[...], slot)])
+
+
+def moved_rows(table, qt, landed, key1, buffer):
+    return pl.pallas_call(
+        moved_kernel,
+        grid_spec=pltpu.PrefetchScalarGridSpec(
+            num_scalar_prefetch=1,
+            grid=(2,),
+            in_specs=[
+                pl.BlockSpec((1, 1, KV, 128), lambda k, a: (1, a[24 + k], 0, 0)),
+                pl.BlockSpec((N_DP, 144, 128), lambda k, a: (0, k, 0)),
+                pl.BlockSpec((N_DP, 48, 128), lambda k, a: (0, 6, 0)),
+                pl.BlockSpec((ROWS, KEYW), lambda k, a: (0, 0)),
+                ANY,
+            ],
+            out_specs=pl.BlockSpec((1, 1, 128, LAT), lambda k, a: (1, a[24 + k], 0, 0)),
+            scratch_shapes=[pltpu.VMEM((KV, 512), BF16)],
+        ),
+        out_shape=jax.ShapeDtypeStruct((2, ROWS, 128, LAT), BF16),
+        input_output_aliases={5: 0},
+        compiler_params=PARAMS,
+        cost_estimate=cost(6e8, 3e6),
+        name="moved_rows",
+    )(table, qt, landed, landed, key1, buffer)
+
+
+def run_copies(copies):
     for c in copies:
         c.start()
     for c in copies:
         c.wait()
 
 
-def forward(idx, pieces):
+def cut_kernel(leaving_ref, cache_ref, after_ref, out_ref, sem):
+    copies = []
+    for q in range(2):
+        row = leaving_ref[q]
+        for j in range(N_DP):
+            f, l = j // 4, j % 4
+            src = cache_ref.at[row, pl.ds(144 * f, 144), pl.ds(128 * l, 128)]
+            copies.append(pltpu.make_async_copy(src, out_ref.at[j, q], sem.at[q * N_DP + j]))
+    run_copies(copies)
+
+
+def cut_pieces(leaving, cache_t, after):
+    return pl.pallas_call(
+        cut_kernel,
+        in_specs=[pl.BlockSpec(memory_space=pltpu.SMEM), ANY, ANY],
+        out_specs=ANY,
+        out_shape=jax.ShapeDtypeStruct((N_DP, 2, 144, 128), BF16),
+        scratch_shapes=[pltpu.SemaphoreType.DMA((2 * N_DP,))],
+        compiler_params=PARAMS,
+        cost_estimate=cost(1e6, 3e6),
+        name="cut_pieces",
+    )(leaving, cache_t, after)
+
+
+def forward_kernel(idx_ref, src_ref, key_ref, out_ref, sem):
+    copies = []
+    for d in range(N_DP):
+        for k in range(2):
+            n = 2 * d + k
+            dst = out_ref.at[d, pl.ds(144 * k, 144)]
+            copies.append(pltpu.make_async_copy(src_ref.at[idx_ref[n]], dst, sem.at[n]))
+        dst = out_ref.at[d, pl.ds(288, 48)]
+        copies.append(pltpu.make_async_copy(key_ref, dst, sem.at[2 * N_DP + d]))
+    run_copies(copies)
+
+
+def forward(idx, pieces, key_block):
     return pl.pallas_call(
         forward_kernel,
-        in_specs=[pl.BlockSpec(memory_space=pltpu.SMEM), ANY],
+        in_specs=[pl.BlockSpec(memory_space=pltpu.SMEM), ANY, ANY],
         out_specs=ANY,
-        out_shape=jax.ShapeDtypeStruct(pieces.shape, BF16),
-        scratch_shapes=[pltpu.SemaphoreType.DMA((2 * N_DP,))],
+        out_shape=jax.ShapeDtypeStruct((N_DP, 336, 128), BF16),
+        scratch_shapes=[pltpu.SemaphoreType.DMA((3 * N_DP,))],
         compiler_params=PARAMS,
         cost_estimate=cost(1e6, 3e6),
         name="forward",
-    )(idx, pieces)
+    )(idx, pieces, key_block)
 
 
 SIB = [(i, i ^ 1) for i in range(8)]
@@ -404,29 +499,64 @@
     return lax.ppermute(v, "ep", pairs)
 
 
-def experts(at, arrived, w_gate, w_up, w_down):
-    keep, send = gate_up(at, arrived, w_gate, w_up)
+def pair_sum(keep, send):
     got = hop(send, SIB)
-    s1 = (keep[1].astype(F32) + got[1].astype(F32)).astype(BF16)
-    s2 = (keep[2].astype(F32) + got[2].astype(F32)).astype(BF16)
-    s3 = (keep[3].astype(F32) + got[3].astype(F32)).astype(BF16)
-    a1 = hop(s1, XP)
-    a2 = hop(s2, X2)
-    a3 = hop(s3, XM)
-    total = (
-        keep[0].astype(F32)
-        + got[0].astype(F32)
-        + a1.astype(F32)
-        + a2.astype(F32)
-        + a3.astype(F32)
-    )
+    parts = [(keep[r].astype(F32) + got[r].astype(F32)).astype(BF16) for r in (1, 2, 3)]
+    return keep[0].astype(F32) + got[0].astype(F32), parts
+
+
+def finish(at, own, parts, w_down):
+    a1 = hop(parts[0], XP)
+    a2 = hop(parts[1], X2)
+    a3 = hop(parts[2], XM)
+    total = own + a1.astype(F32) + a2.astype(F32) + a3.astype(F32)
     act = (jax.nn.silu(total[..., :128]) * total[..., 128:]).astype(BF16)
     b1 = hop(act, XP)
     b3 = hop(act, XM)
     b2 = hop(act, X2)
-    own = [act, b1, b3, b2]
-    other = [hop(v, SIB) for v in own]
-    return down(at, own + other, w_down)
+    ours = [act, b1, b3, b2]
+    theirs = [hop(v, SIB) for v in ours]
+    return down(at, ours + theirs, w_down)
+
+
+def make_keys(s, at, gathered, result, latent_t, cosine, sine):
+    returned = lax.all_to_all(result, "dp", split_axis=0, concat_axis=0, tiled=True)
+    smem = pl.BlockSpec(memory_space=pltpu.SMEM)
+    width = KVW + SLICE
+    shape = jax.ShapeDtypeStruct((4, ROWS, width), F32)
+    own, other = pl.pallas_call(
+        functools.partial(combine_kernel, s),
+        in_specs=[smem, VMEM, VMEM, VMEM],
+        out_specs=[VMEM, VMEM],
+        out_shape=[shape, shape],
+        scratch_shapes=[pltpu.VMEM((N_EP, ROWS, width), F32)],
+        compiler_params=PARAMS,
+        cost_estimate=cost(4e8, 4e6),
+        name="combine%d" % s,
+    )(at, gathered, returned, latent_t)
+    got = hop(other, SIB)
+    shape = jax.ShapeDtypeStruct((ROWS, width + SLICE), F32)
+    sums = pl.pallas_call(
+        fold_kernel,
+        in_specs=[VMEM, VMEM],
+        out_specs=[VMEM] * 4,
+        out_shape=[shape] * 4,
+        compiler_params=PARAMS,
+        name="fold%d" % s,
+    )(own, got)
+    parts = [sums[0], hop(sums[1], XM), hop(sums[2], X2), hop(sums[3], XP)]
+    return pl.pallas_call(
+        key_kernel,
+        in_specs=[smem] + [VMEM] * 6,
+        out_specs=[VMEM] * 3,
+        out_shape=[
+            jax.ShapeDtypeStruct((ROWS, KEYW), F32),
+            jax.ShapeDtypeStruct((48, 128), BF16),
+            jax.ShapeDtypeStruct((ROWS, D), F32),
+        ],
+        compiler_params=PARAMS,
+        name="key%d" % s,
+    )(at, *parts, cosine, sine)
 
 
 def local(
@@ -499,23 +629,22 @@
     my_turn = lax.dynamic_index_in_dim(turn, my_dp, 0, keepdims=False)
     own_len = lax.dynamic_slice_in_dim(lengths, my_dev * ROWS, ROWS)
     second_len = jnp.take(lengths, my_src)
+    order = (my_turn[:, None] == lax.iota(jnp.int32, 2)) & (my_arriving[:, None] == 1)
+    arrival_slot = jnp.sum(jnp.where(order, lax.iota(jnp.int32, ROWS)[:, None], 0), axis=0)
+    arrival_src = jnp.sum(jnp.where(order, my_src_flat[:, None], 0), axis=0)
+    pad = jnp.zeros((6,), jnp.int32)
     old_table = jnp.concatenate(
         [
             second_len,
             jnp.where(my_arriving == 1, 0, my_src % ROWS),
-            jnp.where(my_arriving == 1, my_turn, 0),
-            my_arriving,
+            arrival_src,
+            pad,
+            arrival_slot,
+            pad,
         ]
     ).astype(jnp.int32)
 
     first_old = old0(own_len, qt, cache_t)
-
-    two = jnp.concatenate(
-        [lax.dynamic_slice_in_dim(cache_t, leaving[n], 1, 0) for n in range(2)], axis=0
-    )
-    pieces = two.reshape(2, 8, 72, 2, 256).transpose(1, 3, 0, 2, 4).reshape(N_DP, 2, 72, 256)
-    spread = lax.all_to_all(pieces, "dp", split_axis=0, concat_axis=0, tiled=True)
-    onward = forward(forward_idx, spread.reshape(2 * N_DP, 72, 256))
 
     positions = jnp.stack([own_len, second_len + 1]).astype(F32)
     freq = 10000.0 ** (-2.0 * jnp.arange(32, dtype=F32) / 64)
@@ -524,54 +653,26 @@
     cosine = jnp.where(keep, jnp.cos(angle), 0.0)
     sine = jnp.where(keep, jnp.sin(angle), 0.0)
 
-    keys = []
-    mixes = []
     arrived = [
         lax.all_to_all(sends[s], "dp", split_axis=0, concat_axis=0, tiled=True) for s in range(2)
     ]
-    landed = lax.all_to_all(
-        onward.reshape(N_DP, 2, 72, 256), "dp", split_axis=0, concat_axis=0, tiled=True
-    )
-    moved = landed.reshape(8, 2, 2, 72, 256).transpose(2, 0, 3, 1, 4).reshape(2, KV, 512)
-    second_old = old1(old_table, qt, cache_t, moved)
-    for s in range(2):
-        result = experts(at, arrived[s], w_gate, w_up, w_down)
-        returned = lax.all_to_all(result, "dp", split_axis=0, concat_axis=0, tiled=True)
-        partial = pl.pallas_call(
-            functools.partial(combine_kernel, s),
-            in_specs=[VMEM] * 3,
-            out_specs=VMEM,
-            out_shape=jax.ShapeDtypeStruct((N_EP, ROWS, KVW + SLICE), F32),
-            compiler_params=PARAMS,
-            cost_estimate=cost(4e8, 4e6),
-            name="combine%d" % s,
-        )(gathered, returned, latent_t)
-        summed = lax.all_to_all(partial, "ep", split_axis=0, concat_axis=0, tiled=True)
-        key, mixed = pl.pallas_call(
-            key_kernel,
-            in_specs=[VMEM] * 3,
-            out_specs=[VMEM, VMEM],
-            out_shape=[
-                jax.ShapeDtypeStruct((ROWS, KEYW), BF16),
-                jax.ShapeDtypeStruct((ROWS, D), BF16),
-            ],
-            compiler_params=PARAMS,
-            name="key%d" % s,
-        )(summed, cosine[s], sine[s])
-        keys.append(key)
-        mixes.append(mixed)
-    attended = merge(0, qt, first_old, [keys[0]], None)
-    everyone = lax.all_to_all(
-        jnp.broadcast_to(keys[0][None], (N_DP, ROWS, KEYW)),
-        "dp",
-        split_axis=0,
-        concat_axis=0,
-        tiled=True,
-    ).reshape(N_DP * ROWS, KEYW)
-    select = (my_src_flat[:, None] == flat[None, :]).astype(BF16)
-    first_for_second = jnp.dot(select, everyone, preferred_element_type=F32).astype(BF16)
-    attended = merge(1, qt, second_old, [first_for_second, keys[1]], attended)
-    expert_out = jnp.stack(mixes)
+    keep, send = gate_up(at, arrived[0], w_gate, w_up, first_old[1])
+    own0, parts0 = pair_sum(keep, send)
+    second_old = old1(old_table, qt, cache_t, parts0[0])
+    keep, send = gate_up(at, arrived[1], w_gate, w_up, second_old[1])
+    own1, parts1 = pair_sum(keep, send)
+    pieces = cut_pieces(leaving.astype(jnp.int32), cache_t, arrived[1])
+    spread = lax.all_to_all(pieces, "dp", split_axis=0, concat_axis=0, tiled=True)
+    result0 = finish(at, own0, parts0, w_down)
+    result1 = finish(at, own1, parts1, w_down)
+    key0, block0, mixed0 = make_keys(0, at, gathered, result0, latent_t, cosine[0], sine[0])
+    attended = merge(0, old_table, qt, first_old, [key0], None)
+    onward = forward(forward_idx, spread.reshape(2 * N_DP, 144, 128), block0)
+    key1, _, mixed1 = make_keys(1, at, gathered, result1, latent_t, cosine[1], sine[1])
+    landed = lax.all_to_all(onward, "dp", split_axis=0, concat_axis=0, tiled=True)
+    attended = merge(1, old_table, qt, second_old, [key0, key1], attended)
+    attended = moved_rows(old_table, qt, landed, key1, attended)
+    expert_out = jnp.stack([mixed0, mixed1]).astype(BF16)
     return (expert_out, attended)
 
 

time: 266 us -> 308 us (1.16)
  Pallas kernels: 63.5 us -> 110 us
  waiting for transfers between devices: 66.8 us -> 91.4 us
  starting transfers between devices: 65.4 us -> 52.4 us
  local copies, waits for them, and re-layouts: 38.7 us -> 27.9 us
  between operations: 4.98 us -> 1.4 us
    pallas_call x6 -> x10, Pallas kernels: 17.8 us -> 64.9 us  [the longest x1 37.7 us: cut_pieces(): pl.pallas_call(cut_kernel, in_specs=[pl.BlockSpec(memory_space=pltpu.SMEM...]
    all_to_all x6 -> x3, starting transfers between devices: 31.6 us -> 13.5 us  [the longest x2 9 us: make_keys(): lax.all_to_all(result, 'dp', split_axis=0, concat_axis=0, tiled=True)]
    all_to_all x6 -> x3, waiting for transfers between devices: 8.61 us -> 20.2 us  [the longest x2 17.4 us: make_keys(): lax.all_to_all(result, 'dp', split_axis=0, concat_axis=0, tiled=True)]
    ppermute x22 -> x30, waiting for transfers between devices: 34.3 us -> 45 us  [hop(): return lax.ppermute(v, 'ep', pairs)]
    ppermute x22 -> x30, starting transfers between devices: 14.9 us -> 22.7 us  [hop(): return lax.ppermute(v, 'ep', pairs)]
    reshape x2 -> x0, local copies, waits for them, and re-layouts: 7.6 us -> none  [the longest x1 3.89 us: local(): landed.reshape(8, 2, 2, 72, 256).transpose(2, 0, 3, 1, 4)]
    transpose x2 -> x0, local copies, waits for them, and re-layouts: 5.71 us -> none  [the longest x1 3.22 us: local(): landed.reshape(8, 2, 2, 72, 256).transpose(2, 0, 3, 1, 4)]
    unnamed x48 -> x112, local copies, waits for them, and re-layouts: 19.2 us -> 23.9 us
  transfers between devices with their start and end apart: 31 -> 36, of which waited for: 12 -> 16; matrix products, arithmetic and copies ran while one was open for 11% -> 5% of each run, Pallas kernels for 21% -> 29%
where the time goes in v2:
time: 308 us; the launch traced here: 306 us
  Pallas kernels  110 us (36%)
  waiting for transfers between devices  91.4 us (30%)
  starting transfers between devices  52.4 us (17%)
  local copies, waits for them, and re-layouts  27.9 us (9%)
  blocking collectives  11.7 us (4%)
  other arithmetic  11.1 us (4%)
    ppermute x30, waiting for transfers between devices, hop(): return lax.ppermute(v, 'ep', pairs)  45 us
    pallas_call x1, Pallas kernels, cut_pieces(): pl.pallas_call(cut_kernel, in_specs=[pl.BlockSpec(memory_space=pltpu.SMEM...  37.7 us
    unnamed x112, local copies, waits for them, and re-layouts  23.9 us
    ppermute x30, starting transfers between devices, hop(): return lax.ppermute(v, 'ep', pairs)  22.7 us
    all_to_all x2, waiting for transfers between devices, local(): lax.all_to_all(sends[s], 'dp', split_axis=0, concat_axis=0, tiled=True)  18.9 us
    all_to_all x2, waiting for transfers between devices, make_keys(): lax.all_to_all(result, 'dp', split_axis=0, concat_axis=0, tiled=True)  17.4 us
    pallas_call x2, Pallas kernels, gate_up(): pl.pallas_call(gateup_kernel, grid_spec=pltpu.PrefetchScalarGridSpec(num_...  16.6 us
    all_to_all x2, starting transfers between devices, local(): lax.all_to_all(sends[s], 'dp', split_axis=0, concat_axis=0, tiled=True)  12.5 us
  transfers between devices with their start and end apart: 36, of which 16 were waited for; matrix products, arithmetic and copies ran while one was open for 5% of the time, Pallas kernels for 29%

profile of v2, /device:TPU:0, one launch (start us, length us, event | category | flops | bytes accessed | tf_op | source)
XLA Modules:
  0.0 305.7 jit_solution(15283745704476914709)
XLA Ops:
  3.2 11.7 %all_to_all.35.r_ref = bf16[8,16,1024]{2,1,0:T(8,128)(2,1)S(1)} all-to-all(bf16[8,16,1024]{2,1,0:T(8,128)(2,1)S(1)} %pack.1), channel_id=1, replica_groups=mesh['dp'=16,'ep'=8] {'ep'}, dimensions={0} | all-to-all | bytes 524288 | tf_op jit(solution)/shard_map/all_to_all | solution.py:591
  18.3 8.1 %all-to-all-start.1 = ((bf16[16,48,896]{2,1,0:T(8,128)(2,1)}), bf16[16,48,896]{2,1,0:T(8,128)(2,1)}, u32[]{:S(2)}, u32[]{:S(2)}) async-start(bf16[16,48,896]{2,1,0:T(8,128)(2,1)} %copy-done.12), calls=%async_computation.1 | async-start | bytes 2752512 | tf_op jit(solution)/shard_map/all_to_all | solution.py:657
  29.2 8.0 %old0.1 = (f32[8,128,512]{2,1,0:T(8,128)S(1)}, f32[8,128,128]{2,1,0:T(8,128)S(1)}) custom-call(s32[8]{0:T(128)S(1)} %dynamic_slice.26.len_ref, bf16[2,8,576,128]{3,2,1,0:T(8,128)(2,1)S(1)} %bitcast.67, bf16[8,576,512]{2,1,0:T(8,128)(2,1)} %bitcast.75), custom_call_target="tpu_custom_call" | custom-call | flops 5000000000 | bytes 8000000 | tf_op jit(solution)/shard_map/old0/pallas_call | solution.py:290
  38.5 9.2 %all-to-all-done.1.x_ref = bf16[16,48,896]{2,1,0:T(8,128)(2,1)} async-done(((bf16[16,48,896]{2,1,0:T(8,128)(2,1)}), bf16[16,48,896]{2,1,0:T(8,128)(2,1)}, u32[]{:S(2)}, u32[]{:S(2)}) %all-to-all-start.1) | async-done | bytes 1376288 | tf_op jit(solution)/shard_map/all_to_all | solution.py:657
  47.6 8.8 %gate_up.2 = (bf16[4,2,384,256]{3,2,1,0:T(8,128)(2,1)S(1)}, bf16[4,2,384,256]{3,2,1,0:T(8,128)(2,1)}) custom-call(s32[2]{0:T(128)S(1)} %pad_add_fusion.at_ref, bf16[16,48,896]{2,1,0:T(8,128)(2,1)} %all-to-all-done.1.x_ref, bf16[2,896,1024]{2,1,0:T(8,128)(2,1)} %wg_ref.3, bf16[2,896,1024]{2,1,0:T(8,128)(2,1)} %wu_ref.3, ...), custom_call_target="tpu_custom_call" | custom-call | flops 4000000000 | bytes 12000000 | tf_op jit(solution)/shard_map/gate_up/pallas_call | solution.py:138
  58.7 4.4 %all-to-all-start.3 = ((bf16[16,48,896]{2,1,0:T(8,128)(2,1)}), bf16[16,48,896]{2,1,0:T(8,128)(2,1)}, u32[]{:S(2)}, u32[]{:S(2)}) async-start(bf16[16,48,896]{2,1,0:T(8,128)(2,1)} %copy-done.10), calls=%async_computation.3 | async-start | bytes 2752512 | tf_op jit(solution)/shard_map/all_to_all | solution.py:657
  67.1 7.9 %old1.1 = (f32[8,128,512]{2,1,0:T(8,128)S(1)}, f32[8,128,128]{2,1,0:T(8,128)S(1)}) custom-call(s32[32]{0:T(128)S(1)} %concatenate.7.tab_ref, bf16[2,8,576,128]{3,2,1,0:T(8,128)(2,1)S(1)} %bitcast.68, bf16[8,576,512]{2,1,0:T(8,128)(2,1)} %bitcast.76, bf16[2,384,256]{2,1,0:T(8,128)(2,1)S(1)} %get-tuple-element.69.after_ref), custom_call_target="tpu_custom_call" | custom-call | flops 5000000000 | bytes 8000000 | tf_op jit(solution)/shard_map/old1/pallas_call | solution.py:309
  76.3 9.7 %all-to-all-done.3.x_ref.after_ref = bf16[16,48,896]{2,1,0:T(8,128)(2,1)} async-done(((bf16[16,48,896]{2,1,0:T(8,128)(2,1)}), bf16[16,48,896]{2,1,0:T(8,128)(2,1)}, u32[]{:S(2)}, u32[]{:S(2)}) %all-to-all-start.3) | async-done | bytes 1376288 | tf_op jit(solution)/shard_map/all_to_all | solution.py:657
  86.1 7.8 %gate_up.3 = (bf16[4,2,384,256]{3,2,1,0:T(8,128)(2,1)S(1)}, bf16[4,2,384,256]{3,2,1,0:T(8,128)(2,1)S(1)}) custom-call(s32[2]{0:T(128)S(1)} %pad_add_fusion.at_ref, bf16[16,48,896]{2,1,0:T(8,128)(2,1)} %all-to-all-done.3.x_ref.after_ref, bf16[2,896,1024]{2,1,0:T(8,128)(2,1)} %wg_ref.3, bf16[2,896,1024]{2,1,0:T(8,128)(2,1)} %wu_ref.3, ...), custom_call_target="tpu_custom_call" | custom-call | flops 4000000000 | bytes 12000000 | tf_op jit(solution)/shard_map/gate_up/pallas_call | solution.py:138
  97.4 10.2 %collective-permute-done.2 = bf16[2,384,256]{2,1,0:T(8,128)(2,1)S(1)} collective-permute-done((bf16[2,384,256]{2,1,0:T(8,128)(2,1)S(1)}, bf16[2,384,256]{2,1,0:T(8,128)(2,1)S(1)}, u32[]{:S(2)}, u32[]{:S(2)}) %collective-permute-start.2) | collective-permute-done | bytes 393248 | tf_op jit(solution)/shard_map/ppermute | solution.py:499
  107.6 6.4 %collective-permute-done.3 = bf16[2,384,256]{2,1,0:T(8,128)(2,1)S(1)} collective-permute-done((bf16[2,384,256]{2,1,0:T(8,128)(2,1)S(1)}, bf16[2,384,256]{2,1,0:T(8,128)(2,1)S(1)}, u32[]{:S(2)}, u32[]{:S(2)}) %collective-permute-start.3) | collective-permute-done | bytes 393248 | tf_op jit(solution)/shard_map/ppermute | solution.py:499
  120.3 6.0 %collective-permute-done.6.refs_3_ = bf16[2,384,128]{2,1,0:T(8,128)(2,1)S(1)} collective-permute-done((bf16[2,384,128]{2,1,0:T(8,128)(2,1)S(1)}, bf16[2,384,128]{2,1,0:T(8,128)(2,1)S(1)}, u32[]{:S(2)}, u32[]{:S(2)}) %collective-permute-start.6) | collective-permute-done | bytes 196640 | tf_op jit(solution)/shard_map/ppermute | solution.py:499
  131.5 2.8 collective-permute-start.18
  134.3 3.8 %down.2 = bf16[16,48,896]{2,1,0:T(8,128)(2,1)S(1)} custom-call(s32[2]{0:T(128)S(1)} %pad_add_fusion.at_ref, bf16[2,384,128]{2,1,0:T(8,128)(2,1)S(1)} %fusion.11.refs_0_, bf16[2,384,128]{2,1,0:T(8,128)(2,1)S(1)} %collective-permute-done.4.refs_1_, bf16[2,384,128]{2,1,0:T(8,128)(2,1)S(1)} %collective-permute-done.5.refs_2_, ...), custom_call_target="tpu_custom_call" | custom-call | flops 2000000000 | bytes 8000000 | tf_op jit(solution)/shard_map/down/pallas_call | solution.py:181
  139.2 4.6 %all-to-all-start.2 = ((bf16[16,48,896]{2,1,0:T(8,128)(2,1)}), bf16[16,48,896]{2,1,0:T(8,128)(2,1)}, u32[]{:S(2)}, u32[]{:S(2)}) async-start(bf16[16,48,896]{2,1,0:T(8,128)(2,1)} %copy-done.11), calls=%async_computation.2 | async-start | bytes 2752512 | tf_op jit(solution)/shard_map/all_to_all | solution.py:523
  143.8 8.6 %collective-permute-done.16 = bf16[2,384,256]{2,1,0:T(8,128)(2,1)} collective-permute-done((bf16[2,384,256]{2,1,0:T(8,128)(2,1)}, bf16[2,384,256]{2,1,0:T(8,128)(2,1)}, u32[]{:S(2)}, u32[]{:S(2)}) %collective-permute-start.16) | collective-permute-done | bytes 393248 | tf_op jit(solution)/shard_map/ppermute | solution.py:499
  154.9 3.0 collective-permute-start.20
  158.5 5.2 %collective-permute-done.21.refs_3_ = bf16[2,384,128]{2,1,0:T(8,128)(2,1)S(1)} collective-permute-done((bf16[2,384,128]{2,1,0:T(8,128)(2,1)S(1)}, bf16[2,384,128]{2,1,0:T(8,128)(2,1)S(1)}, u32[]{:S(2)}, u32[]{:S(2)}) %collective-permute-start.21) | collective-permute-done | bytes 196640 | tf_op jit(solution)/shard_map/ppermute | solution.py:499
  163.7 2.9 collective-permute-done.20.refs_2_
  168.5 4.2 %down.3 = bf16[16,48,896]{2,1,0:T(8,128)(2,1)S(1)} custom-call(s32[2]{0:T(128)S(1)} %pad_add_fusion.at_ref, bf16[2,384,128]{2,1,0:T(8,128)(2,1)S(1)} %fusion.10.refs_0_, bf16[2,384,128]{2,1,0:T(8,128)(2,1)S(1)} %collective-permute-done.19.refs_1_, bf16[2,384,128]{2,1,0:T(8,128)(2,1)S(1)} %collective-permute-done.20.refs_2_, ...), custom_call_target="tpu_custom_call" | custom-call | flops 2000000000 | bytes 8000000 | tf_op jit(solution)/shard_map/down/pallas_call | solution.py:181
  173.8 4.4 %all-to-all-start.4 = ((bf16[16,48,896]{2,1,0:T(8,128)(2,1)}), bf16[16,48,896]{2,1,0:T(8,128)(2,1)}, u32[]{:S(2)}, u32[]{:S(2)}) async-start(bf16[16,48,896]{2,1,0:T(8,128)(2,1)} %copy-done.13), calls=%async_computation.4 | async-start | bytes 2752512 | tf_op jit(solution)/shard_map/all_to_all | solution.py:523
  183.4 17.4 %all-to-all-done.4.ret_ref = bf16[16,48,896]{2,1,0:T(8,128)(2,1)} async-done(((bf16[16,48,896]{2,1,0:T(8,128)(2,1)}), bf16[16,48,896]{2,1,0:T(8,128)(2,1)}, u32[]{:S(2)}, u32[]{:S(2)}) %all-to-all-start.4) | async-done | bytes 1376288 | tf_op jit(solution)/shard_map/all_to_all | solution.py:523
  202.1 3.2 %combine1.1 = (f32[4,8,1664]{2,1,0:T(8,128)S(1)}, f32[4,8,1664]{2,1,0:T(8,128)}) custom-call(s32[2]{0:T(128)S(1)} %copy-done.32, bf16[8,16,1024]{2,1,0:T(8,128)(2,1)S(1)} %all_to_all.35.r_ref, bf16[16,48,896]{2,1,0:T(8,128)(2,1)} %all-to-all-done.4.ret_ref, bf16[576,896]{1,0:T(8,128)(2,1)S(1)} %bitcast.74), custom_call_target="tpu_custom_call" | custom-call | flops 400000000 | bytes 4000000 | tf_op jit(solution)/shard_map/combine1/pallas_call | solution.py:527
  211.4 37.7 %cut_pieces.1 = bf16[16,2,144,128]{3,2,1,0:T(8,128)(2,1)} custom-call(s32[2]{0:T(128)S(1)} %fusion.23.leaving_ref, bf16[8,576,512]{2,1,0:T(8,128)(2,1)} %bitcast.77, bf16[16,48,896]{2,1,0:T(8,128)(2,1)} %all-to-all-done.3.x_ref.after_ref), custom_call_target="tpu_custom_call" | custom-call | flops 1000000 | bytes 3000000 | tf_op jit(solution)/shard_map/cut_pieces/pallas_call | solution.py:455
  249.1 3.7 %all-to-all-start.5 = ((bf16[16,2,144,128]{3,2,1,0:T(8,128)(2,1)}), bf16[16,2,144,128]{3,2,1,0:T(8,128)(2,1)S(1)}, u32[]{:S(2)}, u32[]{:S(2)}) async-start(bf16[16,2,144,128]{3,2,1,0:T(8,128)(2,1)} %cut_pieces.1), calls=%async_computation.5 | async-start | bytes 2359296 | tf_op jit(solution)/shard_map/all_to_all | solution.py:665
  265.2 7.2 %all-to-all-done.5 = bf16[16,2,144,128]{3,2,1,0:T(8,128)(2,1)S(1)} async-done(((bf16[16,2,144,128]{3,2,1,0:T(8,128)(2,1)}), bf16[16,2,144,128]{3,2,1,0:T(8,128)(2,1)S(1)}, u32[]{:S(2)}, u32[]{:S(2)}) %all-to-all-start.5) | async-done | bytes 1179680 | tf_op jit(solution)/shard_map/all_to_all | solution.py:665
  273.8 2.9 forward.1
  277.9 4.5 %all-to-all-start.6 = ((bf16[16,336,128]{2,1,0:T(8,128)(2,1)}), bf16[16,336,128]{2,1,0:T(8,128)(2,1)}, u32[]{:S(2)}, u32[]{:S(2)}) async-start(bf16[16,336,128]{2,1,0:T(8,128)(2,1)} %copy-done.1), calls=%async_computation.6 | async-start | bytes 2752512 | tf_op jit(solution)/shard_map/all_to_all | solution.py:672
  284.0 5.9 %merge0.1.refs_2_ = bf16[2,8,128,512]{3,2,1,0:T(8,128)(2,1)} custom-call(s32[32]{0:T(128)S(1)} %copy-done.36, bf16[2,8,576,128]{3,2,1,0:T(8,128)(2,1)S(1)} %bitcast.69, f32[8,128,512]{2,1,0:T(8,128)S(1)} %copy-done.5, f32[8,128,128]{2,1,0:T(8,128)S(1)} %copy-done.15, f32[8,640]{1,0:T(8,128)S(1)} %copy-done.22), custom_call_target="tpu_custom_call" | custom-call | flops 100000000 | bytes 5000000 | tf_op jit(solution)/shard_map/merge0/pallas_call | solution.py:376
  291.7 6.3 %merge1.1.buffer_ref = bf16[2,8,128,512]{3,2,1,0:T(8,128)(2,1)} custom-call(s32[32]{0:T(128)S(1)} %copy-done.36, bf16[2,8,576,128]{3,2,1,0:T(8,128)(2,1)S(1)} %bitcast.70, f32[8,128,512]{2,1,0:T(8,128)S(1)} %copy-done.7, f32[8,128,128]{2,1,0:T(8,128)S(1)} %copy-done.17, f32[8,640]{1,0:T(8,128)S(1)} %copy-done.22, ...), custom_call_target="tpu_custom_call", output_to_operand_aliasing={{}: (6, {})} | custom-call | flops 100000000 | bytes 5000000 | tf_op jit(solution)/shard_map/merge1/pallas_call | solution.py:376
  298.7 2.8 all-to-all-done.6.kv_ref.keys_ref
  301.5 4.2 %moved_rows.1 = bf16[2,8,128,512]{3,2,1,0:T(8,128)(2,1)} custom-call(s32[32]{0:T(128)S(1)} %copy-done.36, bf16[2,8,576,128]{3,2,1,0:T(8,128)(2,1)S(1)} %bitcast.71, bf16[16,336,128]{2,1,0:T(8,128)(2,1)} %all-to-all-done.6.kv_ref.keys_ref, bf16[16,336,128]{2,1,0:T(8,128)(2,1)} %all-to-all-done.6.kv_ref.keys_ref, ...), custom_call_target="tpu_custom_call", output_to_operand_aliasing={{}: (5, {})} | custom-call | flops 600000000 | bytes 3000000 | tf_op jit(solution)/shard_map/moved_rows/pallas_call | solution.py:413
  (230 shorter events, 70.6 us)
Async XLA Ops:
  18.3 29.3 %all-to-all-start.1 = ((bf16[16,48,896]{2,1,0:T(8,128)(2,1)}), bf16[16,48,896]{2,1,0:T(8,128)(2,1)}, u32[]{:S(2)}, u32[]{:S(2)}) async-start(bf16[16,48,896]{2,1,0:T(8,128)(2,1)} %copy-done.12), calls=%async_computation.1 | async-start | bytes 2752512 | tf_op jit(solution)/shard_map/all_to_all | solution.py:657
  57.6 6.5 %collective-permute-start = (bf16[4,2,384,256]{3,2,1,0:T(8,128)(2,1)}, bf16[4,2,384,256]{3,2,1,0:T(8,128)(2,1)}, u32[]{:S(2)}, u32[]{:S(2)}) collective-permute-start(bf16[4,2,384,256]{3,2,1,0:T(8,128)(2,1)} %get-tuple-element.32), channel_id=1, source_target_pairs={{0,1},{1,0},{2,3},{3,2},{4,5},{5,4},{6,7},{7,6},{8,9},{9,8},{10,11... | collective-permute-start | bytes 4718600 | tf_op jit(solution)/shard_map/ppermute | solution.py:499
  58.7 27.4 %all-to-all-start.3 = ((bf16[16,48,896]{2,1,0:T(8,128)(2,1)}), bf16[16,48,896]{2,1,0:T(8,128)(2,1)}, u32[]{:S(2)}, u32[]{:S(2)}) async-start(bf16[16,48,896]{2,1,0:T(8,128)(2,1)} %copy-done.10), calls=%async_computation.3 | async-start | bytes 2752512 | tf_op jit(solution)/shard_map/all_to_all | solution.py:657
  93.9 35.7 %collective-permute-start.15 = (bf16[4,2,384,256]{3,2,1,0:T(8,128)(2,1)S(1)}, bf16[4,2,384,256]{3,2,1,0:T(8,128)(2,1)S(1)}, u32[]{:S(2)}, u32[]{:S(2)}) collective-permute-start(bf16[4,2,384,256]{3,2,1,0:T(8,128)(2,1)S(1)} %get-tuple-element.43), channel_id=1, source_target_pairs={{0,1},{1,0},{2,3},{3,2},{4,5},{5,4},{6,7},{7,6},{8,9},{9,8},{10,11... | collective-permute-start | bytes 4718600 | tf_op jit(solution)/shard_map/ppermute | solution.py:499
  94.0 13.5 %collective-permute-start.2 = (bf16[2,384,256]{2,1,0:T(8,128)(2,1)S(1)}, bf16[2,384,256]{2,1,0:T(8,128)(2,1)S(1)}, u32[]{:S(2)}, u32[]{:S(2)}) collective-permute-start(bf16[2,384,256]{2,1,0:T(8,128)(2,1)S(1)} %copy-done.42), channel_id=1, source_target_pairs={{0,4},{1,5},{2,6},{3,7},{4,0},{5,1},{6,2},{7,3},{8,12},{9,13},{10,... | collective-permute-start | bytes 1179656 | tf_op jit(solution)/shard_map/ppermute | solution.py:499
  94.9 19.1 %collective-permute-start.3 = (bf16[2,384,256]{2,1,0:T(8,128)(2,1)S(1)}, bf16[2,384,256]{2,1,0:T(8,128)(2,1)S(1)}, u32[]{:S(2)}, u32[]{:S(2)}) collective-permute-start(bf16[2,384,256]{2,1,0:T(8,128)(2,1)S(1)} %copy-done.41), channel_id=1, source_target_pairs={{0,6},{1,7},{2,0},{3,1},{4,2},{5,3},{6,4},{7,5},{8,14},{9,15},{10,... | collective-permute-start | bytes 1179656 | tf_op jit(solution)/shard_map/ppermute | solution.py:499
  97.4 18.1 %collective-permute-start.1 = (bf16[2,384,256]{2,1,0:T(8,128)(2,1)S(1)}, bf16[2,384,256]{2,1,0:T(8,128)(2,1)S(1)}, u32[]{:S(2)}, u32[]{:S(2)}) collective-permute-start(bf16[2,384,256]{2,1,0:T(8,128)(2,1)S(1)} %get-tuple-element.69.after_ref), channel_id=1, source_target_pairs={{0,2},{1,3},{2,4},{3,5},{4,6},{5,7},{6,0},{7,1},{8,10},{9,11},{10,... | collective-permute-start | bytes 1179656 | tf_op jit(solution)/shard_map/ppermute | solution.py:499
  117.0 9.3 %collective-permute-start.6 = (bf16[2,384,128]{2,1,0:T(8,128)(2,1)S(1)}, bf16[2,384,128]{2,1,0:T(8,128)(2,1)S(1)}, u32[]{:S(2)}, u32[]{:S(2)}) collective-permute-start(bf16[2,384,128]{2,1,0:T(8,128)(2,1)S(1)} %fusion.11.refs_0_), channel_id=1, source_target_pairs={{0,4},{1,5},{2,6},{3,7},{4,0},{5,1},{6,2},{7,3},{8,12},{9,13},{10,... | collective-permute-start | bytes 589832 | tf_op jit(solution)/shard_map/ppermute | solution.py:499
  118.3 9.9 %collective-permute-start.5 = (bf16[2,384,128]{2,1,0:T(8,128)(2,1)S(1)}, bf16[2,384,128]{2,1,0:T(8,128)(2,1)S(1)}, u32[]{:S(2)}, u32[]{:S(2)}) collective-permute-start(bf16[2,384,128]{2,1,0:T(8,128)(2,1)S(1)} %fusion.11.refs_0_), channel_id=1, source_target_pairs={{0,6},{1,7},{2,0},{3,1},{4,2},{5,3},{6,4},{7,5},{8,14},{9,15},{10,... | collective-permute-start | bytes 589832 | tf_op jit(solution)/shard_map/ppermute | solution.py:499
  120.0 9.6 %collective-permute-start.4 = (bf16[2,384,128]{2,1,0:T(8,128)(2,1)S(1)}, bf16[2,384,128]{2,1,0:T(8,128)(2,1)S(1)}, u32[]{:S(2)}, u32[]{:S(2)}) collective-permute-start(bf16[2,384,128]{2,1,0:T(8,128)(2,1)S(1)} %fusion.11.refs_0_), channel_id=1, source_target_pairs={{0,2},{1,3},{2,4},{3,5},{4,6},{5,7},{6,0},{7,1},{8,10},{9,11},{10,... | collective-permute-start | bytes 589832 | tf_op jit(solution)/shard_map/ppermute | solution.py:499
  120.3 11.2 %collective-permute-start.7 = (bf16[2,384,128]{2,1,0:T(8,128)(2,1)S(1)}, bf16[2,384,128]{2,1,0:T(8,128)(2,1)S(1)}, u32[]{:S(2)}, u32[]{:S(2)}) collective-permute-start(bf16[2,384,128]{2,1,0:T(8,128)(2,1)S(1)} %fusion.11.refs_0_), channel_id=1, source_target_pairs={{0,1},{1,0},{2,3},{3,2},{4,5},{5,4},{6,7},{7,6},{8,9},{9,8},{10,11... | collective-permute-start | bytes 589832 | tf_op jit(solution)/shard_map/ppermute | solution.py:499
  126.3 7.9 %collective-permute-start.10 = (bf16[2,384,128]{2,1,0:T(8,128)(2,1)S(1)}, bf16[2,384,128]{2,1,0:T(8,128)(2,1)S(1)}, u32[]{:S(2)}, u32[]{:S(2)}) collective-permute-start(bf16[2,384,128]{2,1,0:T(8,128)(2,1)S(1)} %collective-permute-done.6.refs_3_), channel_id=1, source_target_pairs={{0,1},{1,0},{2,3},{3,2},{4,5},{5,4},{6,7},{7,6},{8,9},{9,8},{10,11... | collective-permute-start | bytes 589832 | tf_op jit(solution)/shard_map/ppermute | solution.py:499
  128.2 6.1 %collective-permute-start.9 = (bf16[2,384,128]{2,1,0:T(8,128)(2,1)S(1)}, bf16[2,384,128]{2,1,0:T(8,128)(2,1)S(1)}, u32[]{:S(2)}, u32[]{:S(2)}) collective-permute-start(bf16[2,384,128]{2,1,0:T(8,128)(2,1)S(1)} %collective-permute-done.5.refs_2_), channel_id=1, source_target_pairs={{0,1},{1,0},{2,3},{3,2},{4,5},{5,4},{6,7},{7,6},{8,9},{9,8},{10,11... | collective-permute-start | bytes 589832 | tf_op jit(solution)/shard_map/ppermute | solution.py:499
  131.0 21.5 %collective-permute-start.16 = (bf16[2,384,256]{2,1,0:T(8,128)(2,1)}, bf16[2,384,256]{2,1,0:T(8,128)(2,1)}, u32[]{:S(2)}, u32[]{:S(2)}) collective-permute-start(bf16[2,384,256]{2,1,0:T(8,128)(2,1)} %get-tuple-element.70), channel_id=1, source_target_pairs={{0,2},{1,3},{2,4},{3,5},{4,6},{5,7},{6,0},{7,1},{8,10},{9,11},{10,... | collective-permute-start | bytes 1179656 | tf_op jit(solution)/shard_map/ppermute | solution.py:499
  131.5 21.0 %collective-permute-start.18 = (bf16[2,384,256]{2,1,0:T(8,128)(2,1)}, bf16[2,384,256]{2,1,0:T(8,128)(2,1)}, u32[]{:S(2)}, u32[]{:S(2)}) collective-permute-start(bf16[2,384,256]{2,1,0:T(8,128)(2,1)} %get-tuple-element.71), channel_id=1, source_target_pairs={{0,6},{1,7},{2,0},{3,1},{4,2},{5,3},{6,4},{7,5},{8,14},{9,15},{10,... | collective-permute-start | bytes 1179656 | tf_op jit(solution)/shard_map/ppermute | solution.py:499
  134.2 18.2 %collective-permute-start.17 = (bf16[2,384,256]{2,1,0:T(8,128)(2,1)S(1)}, bf16[2,384,256]{2,1,0:T(8,128)(2,1)}, u32[]{:S(2)}, u32[]{:S(2)}) collective-permute-start(bf16[2,384,256]{2,1,0:T(8,128)(2,1)S(1)} %get-tuple-element.72), channel_id=1, source_target_pairs={{0,4},{1,5},{2,6},{3,7},{4,0},{5,1},{6,2},{7,3},{8,12},{9,13},{10,... | collective-permute-start | bytes 1179656 | tf_op jit(solution)/shard_map/ppermute | solution.py:499
  139.2 34.6 %all-to-all-start.2 = ((bf16[16,48,896]{2,1,0:T(8,128)(2,1)}), bf16[16,48,896]{2,1,0:T(8,128)(2,1)}, u32[]{:S(2)}, u32[]{:S(2)}) async-start(bf16[16,48,896]{2,1,0:T(8,128)(2,1)} %copy-done.11), calls=%async_computation.2 | async-start | bytes 2752512 | tf_op jit(solution)/shard_map/all_to_all | solution.py:523
  154.3 9.4 %collective-permute-start.21 = (bf16[2,384,128]{2,1,0:T(8,128)(2,1)S(1)}, bf16[2,384,128]{2,1,0:T(8,128)(2,1)S(1)}, u32[]{:S(2)}, u32[]{:S(2)}) collective-permute-start(bf16[2,384,128]{2,1,0:T(8,128)(2,1)S(1)} %fusion.10.refs_0_), channel_id=1, source_target_pairs={{0,4},{1,5},{2,6},{3,7},{4,0},{5,1},{6,2},{7,3},{8,12},{9,13},{10,... | collective-permute-start | bytes 589832 | tf_op jit(solution)/shard_map/ppermute | solution.py:499
  154.9 11.7 %collective-permute-start.20 = (bf16[2,384,128]{2,1,0:T(8,128)(2,1)S(1)}, bf16[2,384,128]{2,1,0:T(8,128)(2,1)S(1)}, u32[]{:S(2)}, u32[]{:S(2)}) collective-permute-start(bf16[2,384,128]{2,1,0:T(8,128)(2,1)S(1)} %fusion.10.refs_0_), channel_id=1, source_target_pairs={{0,6},{1,7},{2,0},{3,1},{4,2},{5,3},{6,4},{7,5},{8,14},{9,15},{10,... | collective-permute-start | bytes 589832 | tf_op jit(solution)/shard_map/ppermute | solution.py:499
  157.9 8.7 %collective-permute-start.19 = (bf16[2,384,128]{2,1,0:T(8,128)(2,1)S(1)}, bf16[2,384,128]{2,1,0:T(8,128)(2,1)S(1)}, u32[]{:S(2)}, u32[]{:S(2)}) collective-permute-start(bf16[2,384,128]{2,1,0:T(8,128)(2,1)S(1)} %fusion.10.refs_0_), channel_id=1, source_target_pairs={{0,2},{1,3},{2,4},{3,5},{4,6},{5,7},{6,0},{7,1},{8,10},{9,11},{10,... | collective-permute-start | bytes 589832 | tf_op jit(solution)/shard_map/ppermute | solution.py:499
  158.5 9.3 %collective-permute-start.22 = (bf16[2,384,128]{2,1,0:T(8,128)(2,1)S(1)}, bf16[2,384,128]{2,1,0:T(8,128)(2,1)}, u32[]{:S(2)}, u32[]{:S(2)}) collective-permute-start(bf16[2,384,128]{2,1,0:T(8,128)(2,1)S(1)} %fusion.10.refs_0_), channel_id=1, source_target_pairs={{0,1},{1,0},{2,3},{3,2},{4,5},{5,4},{6,7},{7,6},{8,9},{9,8},{10,11... | collective-permute-start | bytes 589832 | tf_op jit(solution)/shard_map/ppermute | solution.py:499
  173.8 27.0 %all-to-all-start.4 = ((bf16[16,48,896]{2,1,0:T(8,128)(2,1)}), bf16[16,48,896]{2,1,0:T(8,128)(2,1)}, u32[]{:S(2)}, u32[]{:S(2)}) async-start(bf16[16,48,896]{2,1,0:T(8,128)(2,1)} %copy-done.13), calls=%async_computation.4 | async-start | bytes 2752512 | tf_op jit(solution)/shard_map/all_to_all | solution.py:523
  182.3 24.3 %collective-permute-start.11 = (f32[4,8,1664]{2,1,0:T(8,128)S(1)}, f32[4,8,1664]{2,1,0:T(8,128)S(1)}, u32[]{:S(2)}, u32[]{:S(2)}) collective-permute-start(f32[4,8,1664]{2,1,0:T(8,128)S(1)} %get-tuple-element.34), channel_id=1, source_target_pairs={{0,1},{1,0},{2,3},{3,2},{4,5},{5,4},{6,7},{7,6},{8,9},{9,8},{10,11... | collective-permute-start | bytes 638984 | tf_op jit(solution)/shard_map/ppermute | solution.py:499
  205.9 50.7 %collective-permute-start.26 = (f32[4,8,1664]{2,1,0:T(8,128)}, f32[4,8,1664]{2,1,0:T(8,128)}, u32[]{:S(2)}, u32[]{:S(2)}) collective-permute-start(f32[4,8,1664]{2,1,0:T(8,128)} %get-tuple-element.45), channel_id=1, source_target_pairs={{0,1},{1,0},{2,3},{3,2},{4,5},{5,4},{6,7},{7,6},{8,9},{9,8},{10,11... | collective-permute-start | bytes 638984 | tf_op jit(solution)/shard_map/ppermute | solution.py:499
  208.0 44.8 %collective-permute-start.12 = (f32[8,2560]{1,0:T(8,128)}, f32[8,2560]{1,0:T(8,128)}, u32[]{:S(2)}, u32[]{:S(2)}) collective-permute-start(f32[8,2560]{1,0:T(8,128)} %get-tuple-element.36), channel_id=1, source_target_pairs={{0,6},{1,7},{2,0},{3,1},{4,2},{5,3},{6,4},{7,5},{8,14},{9,15},{10,... | collective-permute-start | bytes 245768 | tf_op jit(solution)/shard_map/ppermute | solution.py:499
  210.4 42.4 %collective-permute-start.13 = (f32[8,2560]{1,0:T(8,128)}, f32[8,2560]{1,0:T(8,128)}, u32[]{:S(2)}, u32[]{:S(2)}) collective-permute-start(f32[8,2560]{1,0:T(8,128)} %get-tuple-element.37), channel_id=1, source_target_pairs={{0,4},{1,5},{2,6},{3,7},{4,0},{5,1},{6,2},{7,3},{8,12},{9,13},{10,... | collective-permute-start | bytes 245768 | tf_op jit(solution)/shard_map/ppermute | solution.py:499
  210.4 42.4 %collective-permute-start.14 = (f32[8,2560]{1,0:T(8,128)}, f32[8,2560]{1,0:T(8,128)}, u32[]{:S(2)}, u32[]{:S(2)}) collective-permute-start(f32[8,2560]{1,0:T(8,128)} %get-tuple-element.38), channel_id=1, source_target_pairs={{0,2},{1,3},{2,4},{3,5},{4,6},{5,7},{6,0},{7,1},{8,10},{9,11},{10,... | collective-permute-start | bytes 245768 | tf_op jit(solution)/shard_map/ppermute | solution.py:499
  249.1 23.4 %all-to-all-start.5 = ((bf16[16,2,144,128]{3,2,1,0:T(8,128)(2,1)}), bf16[16,2,144,128]{3,2,1,0:T(8,128)(2,1)S(1)}, u32[]{:S(2)}, u32[]{:S(2)}) async-start(bf16[16,2,144,128]{3,2,1,0:T(8,128)(2,1)} %cut_pieces.1), calls=%async_computation.5 | async-start | bytes 2359296 | tf_op jit(solution)/shard_map/all_to_all | solution.py:665
  259.8 30.1 %collective-permute-start.27 = (f32[8,2560]{1,0:T(8,128)}, f32[8,2560]{1,0:T(8,128)}, u32[]{:S(2)}, u32[]{:S(2)}) collective-permute-start(f32[8,2560]{1,0:T(8,128)} %get-tuple-element.47), channel_id=1, source_target_pairs={{0,6},{1,7},{2,0},{3,1},{4,2},{5,3},{6,4},{7,5},{8,14},{9,15},{10,... | collective-permute-start | bytes 245768 | tf_op jit(solution)/shard_map/ppermute | solution.py:499
  262.2 27.7 %collective-permute-start.28 = (f32[8,2560]{1,0:T(8,128)}, f32[8,2560]{1,0:T(8,128)}, u32[]{:S(2)}, u32[]{:S(2)}) collective-permute-start(f32[8,2560]{1,0:T(8,128)} %get-tuple-element.48), channel_id=1, source_target_pairs={{0,4},{1,5},{2,6},{3,7},{4,0},{5,1},{6,2},{7,3},{8,12},{9,13},{10,... | collective-permute-start | bytes 245768 | tf_op jit(solution)/shard_map/ppermute | solution.py:499
  264.5 25.4 %collective-permute-start.29 = (f32[8,2560]{1,0:T(8,128)}, f32[8,2560]{1,0:T(8,128)}, u32[]{:S(2)}, u32[]{:S(2)}) collective-permute-start(f32[8,2560]{1,0:T(8,128)} %get-tuple-element.49), channel_id=1, source_target_pairs={{0,2},{1,3},{2,4},{3,5},{4,6},{5,7},{6,0},{7,1},{8,10},{9,11},{10,... | collective-permute-start | bytes 245768 | tf_op jit(solution)/shard_map/ppermute | solution.py:499
  277.9 23.6 %all-to-all-start.6 = ((bf16[16,336,128]{2,1,0:T(8,128)(2,1)}), bf16[16,336,128]{2,1,0:T(8,128)(2,1)}, u32[]{:S(2)}, u32[]{:S(2)}) async-start(bf16[16,336,128]{2,1,0:T(8,128)(2,1)} %copy-done.1), calls=%async_computation.6 | async-start | bytes 2752512 | tf_op jit(solution)/shard_map/all_to_all | solution.py:672
  (60 other events, 470.6 us)

commit v3 on v2

--- a/solution.py
+++ b/solution.py
@@ -2,6 +2,7 @@
 
 import jax
 import jax.numpy as jnp
+import numpy as np
 from jax import lax
 from jax.experimental import pallas as pl
 from jax.experimental.pallas import tpu as pltpu
@@ -114,7 +115,79 @@
         out_ref[...] = out.reshape(N_DP, PER_DP, SLICE).astype(BF16)
 
 
-def gateup_kernel(at_ref, x_ref, wg_ref, wu_ref, after_ref, keep_ref, send_ref):
+def total(values, axis):
+    return jnp.sum(values, axis=axis, keepdims=True)
+
+
+def table_kernel(me_ref, from_ref, len_ref, freq_ref, tab_ref, cos_ref, sin_ref, hold_ref):
+    n = N_DP * ROWS
+    my_dp, my_ep = me_ref[0], me_ref[1]
+    sub = lax.broadcasted_iota(jnp.int32, (n, n), 0)
+    lane = lax.broadcasted_iota(jnp.int32, (n, n), 1)
+    lane64 = lax.broadcasted_iota(jnp.int32, (n, 64), 1)
+    sub64 = lax.broadcasted_iota(jnp.int32, (n, 64), 0)
+    wanted = lane64 == my_ep * ROWS + (sub64 & 7)
+
+    def column(ref):
+        wide = jnp.broadcast_to(ref[...][:, None, :], (N_DP, ROWS, 64)).reshape(n, 64)
+        return total(jnp.where(wanted, wide, 0), 1)
+
+    def as_row(col):
+        return total(jnp.where(sub == lane, col, 0), 0)
+
+    came = column(from_ref)
+    lens = column(len_ref)
+    src_dp = came >> 6
+    src = src_dp * ROWS + (came & 7)
+    home = lax.broadcasted_iota(jnp.int32, (n, 1), 0)
+    arriving = src_dp != (home >> 3)
+    arriving_row = as_row(arriving.astype(jnp.int32))
+    hit = src == lane
+    away_row = total(jnp.where(hit & arriving, 1, 0), 0)
+    label = total(jnp.where(((src >> 3) == (lane >> 3)) & (lane < src), away_row, 0), 1)
+    turn = total(jnp.where(((sub >> 3) == (lane >> 3)) & (lane < sub), arriving_row, 0), 1)
+    second = total(jnp.where(hit, as_row(lens), 0), 1)
+    mine = sub == my_dp * ROWS + lane
+    here = ((sub >> 3) == my_dp) & arriving & (turn == lane)
+    onward = ((sub >> 3) == (lane >> 1)) & arriving & (turn == (lane & 1)) & (lane < 2 * N_DP)
+    gone = ((src >> 3) == my_dp) & arriving & (label == lane)
+    lane_row = lax.broadcasted_iota(jnp.int32, (1, n), 1)
+    spot = jnp.where(lane_row == 0, my_ep >> 1, jnp.where(lane_row == 1, my_ep & 1, 0))
+    rows = [
+        total(jnp.where(mine, second, 0), 0),
+        total(jnp.where(mine & ~arriving, src & 7, 0), 0),
+        total(jnp.where(here, src, 0), 0),
+        total(jnp.where(here, home & 7, 0), 0),
+        total(jnp.where(onward, src_dp * 2 + label, 0), 0),
+        total(jnp.where(gone, src & 7, 0), 0),
+        total(jnp.where(mine, lens, 0), 0),
+        spot,
+    ]
+    tab_ref[...] = jnp.concatenate(rows, axis=0)
+    hold_ref[0] = lens.astype(F32)
+    hold_ref[1] = (second + 1).astype(F32)
+    live = lax.broadcasted_iota(jnp.int32, (ROWS, 128), 1) < 64
+    for s in range(2):
+        angle = hold_ref[s, pl.ds(pl.multiple_of(my_dp * ROWS, ROWS), ROWS), :] * freq_ref[...]
+        cos_ref[s] = jnp.where(live, jnp.cos(angle), 0.0)
+        sin_ref[s] = jnp.where(live, jnp.sin(angle), 0.0)
+
+
+def make_table(me, came_from, lengths):
+    freq = jnp.asarray(np.tile(10000.0 ** (-2.0 * np.arange(32) / 64), 4)[None], F32)
+    wave = jax.ShapeDtypeStruct((2, ROWS, 128), F32)
+    return pl.pallas_call(
+        table_kernel,
+        in_specs=[pl.BlockSpec(memory_space=pltpu.SMEM)] + [VMEM] * 3,
+        out_specs=[VMEM] * 3,
+        out_shape=[jax.ShapeDtypeStruct((8, 128), jnp.int32), wave, wave],
+        scratch_shapes=[pltpu.VMEM((2, N_DP * ROWS, 1), F32)],
+        compiler_params=PARAMS,
+        name="table",
+    )(me, came_from.reshape(N_DP, 64), lengths.reshape(N_DP, 64), freq)
+
+
+def gateup_kernel(at_ref, x_ref, wg_ref, wu_ref, after_ref, also_ref, keep_ref, send_ref):
     core = at_ref[1]
     for e in range(2):
         lhs = x_ref[:, 16 * e : 16 * e + 32, :].reshape(N_DP * 32, SLICE)
@@ -131,7 +204,7 @@
         send_ref[0, e, :, 128:] = jnp.where(first, u1, u0).astype(BF16)
 
 
-def gate_up(at, x, w_gate, w_up, after):
+def gate_up(at, x, w_gate, w_up, after, also):
     wspec = pl.BlockSpec((2, SLICE, 256), lambda r, a: (0, 0, (a[0] + r) % 4))
     ospec = pl.BlockSpec((1, 2, HALF, 256), lambda r, a: (r, 0, 0, 0))
     shape = jax.ShapeDtypeStruct((4, 2, HALF, 256), BF16)
@@ -145,6 +218,7 @@
                 wspec,
                 wspec,
                 ANY,
+                ANY,
             ],
             out_specs=[ospec, ospec],
         ),
@@ -152,13 +226,13 @@
         compiler_params=PARAMS,
         cost_estimate=cost(4e9, 12e6),
         name="gate_up",
-    )(at, x, w_gate, w_up, after)
+    )(at, x, w_gate, w_up, after, also)
 
 
 def down_kernel(at_ref, *refs):
     acts = refs[:8]
     w_ref = refs[8]
-    out_ref = refs[9]
+    out_ref = refs[-1]
     x = at_ref[0]
     first = at_ref[1] == 0
     results = []
@@ -177,19 +251,19 @@
     out_ref[...] = jnp.concatenate(results, axis=1).astype(BF16)
 
 
-def down(at, acts, w_down):
+def down(at, acts, w_down, after):
     return pl.pallas_call(
         down_kernel,
-        in_specs=[pl.BlockSpec(memory_space=pltpu.SMEM)] + [VMEM] * 9,
+        in_specs=[pl.BlockSpec(memory_space=pltpu.SMEM)] + [VMEM] * 9 + [ANY],
         out_specs=VMEM,
         out_shape=jax.ShapeDtypeStruct((N_DP, PER_DP, SLICE), BF16),
         compiler_params=PARAMS,
         cost_estimate=cost(2e9, 8e6),
         name="down",
-    )(at, *acts, w_down)
-
-
-def combine_kernel(s, at_ref, r_ref, ret_ref, wl_ref, own_ref, other_ref, all_ref):
+    )(at, *acts, w_down, after)
+
+
+def combine_kernel(s, at_ref, r_ref, ret_ref, wl_ref, after_ref, own_ref, other_ref, all_ref):
     hid, _, _, gm, place = unpack(r_ref, s)
     weights = place(gm)
     high = weights.astype(BF16)
@@ -267,12 +341,12 @@
 
 
 def old0_kernel(len_ref, q_ref, kt_ref, out_ref, stat_ref):
-    count = len_ref[pl.program_id(0)]
+    count = len_ref[6, pl.program_id(0)]
     store_old(out_ref, stat_ref, old_attention(q_ref[0, 0], kt_ref[0], count))
 
 
 def old1_kernel(tab_ref, q_ref, kt_ref, after_ref, out_ref, stat_ref):
-    count = tab_ref[pl.program_id(0)]
+    count = tab_ref[0, pl.program_id(0)]
     store_old(out_ref, stat_ref, old_attention(q_ref[0, 0], kt_ref[0], count))
 
 
@@ -313,7 +387,7 @@
             grid=(ROWS,),
             in_specs=[
                 pl.BlockSpec((1, 1, KV, 128), lambda t, a: (1, t, 0, 0)),
-                pl.BlockSpec((1, KV, 512), lambda t, a: (a[8 + t], 0, 0)),
+                pl.BlockSpec((1, KV, 512), lambda t, a: (a[1, t], 0, 0)),
                 ANY,
             ],
             out_specs=OLD_SPECS,
@@ -332,9 +406,7 @@
     scores = []
     values = []
     for key, row in keys:
-        both = lax.dot_general(
-            q, key[:, :KV].astype(BF16), (((0,), (1,)), ((), ())), preferred_element_type=F32
-        )
+        both = jnp.dot(key[:, :KV].astype(BF16), q, preferred_element_type=F32).T
         scores.append(jnp.sum(jnp.where(lane == row, both, 0.0), axis=1, keepdims=True) * SCALE)
         values.append(jnp.sum(jnp.where(sub == row, key[:, :LAT], 0.0), axis=0, keepdims=True))
     peak = top
@@ -356,7 +428,7 @@
     if step == 0:
         keys = [(refs[0][...], t)]
     else:
-        keys = [(refs[0][...], tab_ref[8 + t]), (refs[1][...], t)]
+        keys = [(refs[0][...], tab_ref[1, t]), (refs[1][...], t)]
     old = (old_ref[0], stat_ref[0, :, 0:1], stat_ref[0, :, 1:2])
     out_ref[0, 0] = add_new(q_ref[0, 0], old, keys)
 
@@ -391,12 +463,12 @@
 
 def moved_kernel(tab_ref, q_ref, kv_ref, keys_ref, key1_ref, buffer_ref, out_ref, kt_ref):
     k = pl.program_id(0)
-    slot = tab_ref[24 + k]
+    slot = tab_ref[3, k]
     for j in range(N_DP):
         f, l = j // 4, j % 4
         kt_ref[144 * f : 144 * f + 144, 128 * l : 128 * l + 128] = kv_ref[j]
     raw = keys_ref[...].astype(F32)
-    where = tab_ref[16 + k]
+    where = tab_ref[2, k]
     pick = lax.broadcasted_iota(jnp.int32, (N_DP, ROWS, 1), 0) * ROWS
     pick = pick + lax.broadcasted_iota(jnp.int32, (N_DP, ROWS, 1), 1)
     rows = []
@@ -405,7 +477,7 @@
         rows.append(jnp.sum(jnp.sum(tile, axis=0), axis=0, keepdims=True))
     first = jnp.broadcast_to(jnp.concatenate(rows, axis=1), (ROWS, KEYW))
     q = q_ref[0, 0]
-    old = old_attention(q, kt_ref[...], tab_ref[slot])
+    old = old_attention(q, kt_ref[...], tab_ref[0, slot])
     out_ref[0, 0] = add_new(q, old, [(first, 0), (key1_ref[...], slot)])
 
 
@@ -416,13 +488,13 @@
             num_scalar_prefetch=1,
             grid=(2,),
             in_specs=[
-                pl.BlockSpec((1, 1, KV, 128), lambda k, a: (1, a[24 + k], 0, 0)),
+                pl.BlockSpec((1, 1, KV, 128), lambda k, a: (1, a[3, k], 0, 0)),
                 pl.BlockSpec((N_DP, 144, 128), lambda k, a: (0, k, 0)),
                 pl.BlockSpec((N_DP, 48, 128), lambda k, a: (0, 6, 0)),
                 pl.BlockSpec((ROWS, KEYW), lambda k, a: (0, 0)),
                 ANY,
             ],
-            out_specs=pl.BlockSpec((1, 1, 128, LAT), lambda k, a: (1, a[24 + k], 0, 0)),
+            out_specs=pl.BlockSpec((1, 1, 128, LAT), lambda k, a: (1, a[3, k], 0, 0)),
             scratch_shapes=[pltpu.VMEM((KV, 512), BF16)],
         ),
         out_shape=jax.ShapeDtypeStruct((2, ROWS, 128, LAT), BF16),
@@ -443,7 +515,7 @@
 def cut_kernel(leaving_ref, cache_ref, after_ref, out_ref, sem):
     copies = []
     for q in range(2):
-        row = leaving_ref[q]
+        row = leaving_ref[5, q]
         for j in range(N_DP):
             f, l = j // 4, j % 4
             src = cache_ref.at[row, pl.ds(144 * f, 144), pl.ds(128 * l, 128)]
@@ -455,7 +527,7 @@
     return pl.pallas_call(
         cut_kernel,
         in_specs=[pl.BlockSpec(memory_space=pltpu.SMEM), ANY, ANY],
-        out_specs=ANY,
+        out_specs=VMEM,
         out_shape=jax.ShapeDtypeStruct((N_DP, 2, 144, 128), BF16),
         scratch_shapes=[pltpu.SemaphoreType.DMA((2 * N_DP,))],
         compiler_params=PARAMS,
@@ -470,7 +542,7 @@
         for k in range(2):
             n = 2 * d + k
             dst = out_ref.at[d, pl.ds(144 * k, 144)]
-            copies.append(pltpu.make_async_copy(src_ref.at[idx_ref[n]], dst, sem.at[n]))
+            copies.append(pltpu.make_async_copy(src_ref.at[idx_ref[4, n]], dst, sem.at[n]))
         dst = out_ref.at[d, pl.ds(288, 48)]
         copies.append(pltpu.make_async_copy(key_ref, dst, sem.at[2 * N_DP + d]))
     run_copies(copies)
@@ -479,8 +551,8 @@
 def forward(idx, pieces, key_block):
     return pl.pallas_call(
         forward_kernel,
-        in_specs=[pl.BlockSpec(memory_space=pltpu.SMEM), ANY, ANY],
-        out_specs=ANY,
+        in_specs=[pl.BlockSpec(memory_space=pltpu.SMEM), VMEM, VMEM],
+        out_specs=VMEM,
         out_shape=jax.ShapeDtypeStruct((N_DP, 336, 128), BF16),
         scratch_shapes=[pltpu.SemaphoreType.DMA((3 * N_DP,))],
         compiler_params=PARAMS,
@@ -495,6 +567,10 @@
 X2 = [(i, (i + 4) % 8) for i in range(8)]
 
 
+def to_dp(v):
+    return lax.all_to_all(v, "dp", split_axis=0, concat_axis=0, tiled=True)
+
+
 def hop(v, pairs):
     return lax.ppermute(v, "ep", pairs)
 
@@ -505,35 +581,37 @@
     return keep[0].astype(F32) + got[0].astype(F32), parts
 
 
-def finish(at, own, parts, w_down):
+def activate(own, parts):
     a1 = hop(parts[0], XP)
     a2 = hop(parts[1], X2)
     a3 = hop(parts[2], XM)
     total = own + a1.astype(F32) + a2.astype(F32) + a3.astype(F32)
-    act = (jax.nn.silu(total[..., :128]) * total[..., 128:]).astype(BF16)
+    return (jax.nn.silu(total[..., :128]) * total[..., 128:]).astype(BF16)
+
+
+def finish(at, act, w_down, after):
     b1 = hop(act, XP)
     b3 = hop(act, XM)
     b2 = hop(act, X2)
     ours = [act, b1, b3, b2]
     theirs = [hop(v, SIB) for v in ours]
-    return down(at, ours + theirs, w_down)
-
-
-def make_keys(s, at, gathered, result, latent_t, cosine, sine):
-    returned = lax.all_to_all(result, "dp", split_axis=0, concat_axis=0, tiled=True)
+    return down(at, ours + theirs, w_down, after)
+
+
+def make_keys(s, at, gathered, returned, latent_t, cosine, sine, after):
     smem = pl.BlockSpec(memory_space=pltpu.SMEM)
     width = KVW + SLICE
     shape = jax.ShapeDtypeStruct((4, ROWS, width), F32)
     own, other = pl.pallas_call(
         functools.partial(combine_kernel, s),
-        in_specs=[smem, VMEM, VMEM, VMEM],
+        in_specs=[smem, VMEM, VMEM, VMEM, ANY],
         out_specs=[VMEM, VMEM],
         out_shape=[shape, shape],
         scratch_shapes=[pltpu.VMEM((N_EP, ROWS, width), F32)],
         compiler_params=PARAMS,
         cost_estimate=cost(4e8, 4e6),
         name="combine%d" % s,
-    )(at, gathered, returned, latent_t)
+    )(at, gathered, returned, latent_t, after)
     got = hop(other, SIB)
     shape = jax.ShapeDtypeStruct((ROWS, width + SLICE), F32)
     sums = pl.pallas_call(
@@ -574,8 +652,9 @@
 ):
     my_dp = lax.axis_index("dp")
     my_ep = lax.axis_index("ep")
-    my_dev = my_dp * N_EP + my_ep
+    me = jnp.stack([my_dp, my_ep]).astype(jnp.int32)
     at = jnp.stack([my_ep // 2, my_ep % 2]).astype(jnp.int32)
+    table, cosine, sine = make_table(me, came_from, lengths)
     qt = jnp.swapaxes(queries, 2, 3)
     cache_t = jnp.swapaxes(cache, 1, 2)
     latent_t = w_latent.T
@@ -599,79 +678,29 @@
         name="dispatch",
     )(gathered)
 
-    table = lax.dynamic_index_in_dim(
-        came_from.reshape(N_DP, N_EP, ROWS), my_ep, 1, keepdims=False
-    )
-    src_dp = table // (N_EP * ROWS)
-    src_row = table % ROWS
-    src_flat = (src_dp * ROWS + src_row).reshape(N_DP * ROWS)
-    flat = lax.iota(jnp.int32, N_DP * ROWS)
-    hit = src_flat[:, None] == flat[None, :]
-    crosses = (flat // ROWS)[:, None] != (flat // ROWS)[None, :]
-    away = jnp.any(hit & crosses, axis=0).reshape(N_DP, ROWS).astype(jnp.int32)
-    rows_before = lax.iota(jnp.int32, ROWS)[:, None] < lax.iota(jnp.int32, ROWS)[None, :]
-    label = jnp.sum(away[:, :, None] * rows_before[None], axis=1)
-    label_of = jnp.sum(jnp.where(hit, label.reshape(1, -1), 0), axis=1).reshape(N_DP, ROWS)
-    arriving = (src_dp != lax.iota(jnp.int32, N_DP)[:, None]).astype(jnp.int32)
-    turn = jnp.sum(arriving[:, :, None] * rows_before[None], axis=1)
-    source = src_dp * 2 + label_of
-    pick = (turn[:, :, None] == lax.iota(jnp.int32, 2)) & (arriving[:, :, None] == 1)
-    forward_idx = jnp.sum(jnp.where(pick, source[:, :, None], 0), axis=1).reshape(2 * N_DP)
-    my_away = lax.dynamic_index_in_dim(away, my_dp, 0, keepdims=False)
-    my_label = lax.dynamic_index_in_dim(label, my_dp, 0, keepdims=False)
-    leave = (my_label[:, None] == lax.iota(jnp.int32, 2)) & (my_away[:, None] == 1)
-    leaving = jnp.sum(jnp.where(leave, lax.iota(jnp.int32, ROWS)[:, None], 0), axis=0)
-    my_src = lax.dynamic_index_in_dim(table, my_dp, 0, keepdims=False)
-    my_src_flat = lax.dynamic_index_in_dim(
-        src_flat.reshape(N_DP, ROWS), my_dp, 0, keepdims=False
-    )
-    my_arriving = lax.dynamic_index_in_dim(arriving, my_dp, 0, keepdims=False)
-    my_turn = lax.dynamic_index_in_dim(turn, my_dp, 0, keepdims=False)
-    own_len = lax.dynamic_slice_in_dim(lengths, my_dev * ROWS, ROWS)
-    second_len = jnp.take(lengths, my_src)
-    order = (my_turn[:, None] == lax.iota(jnp.int32, 2)) & (my_arriving[:, None] == 1)
-    arrival_slot = jnp.sum(jnp.where(order, lax.iota(jnp.int32, ROWS)[:, None], 0), axis=0)
-    arrival_src = jnp.sum(jnp.where(order, my_src_flat[:, None], 0), axis=0)
-    pad = jnp.zeros((6,), jnp.int32)
-    old_table = jnp.concatenate(
-        [
-            second_len,
-            jnp.where(my_arriving == 1, 0, my_src % ROWS),
-            arrival_src,
-            pad,
-            arrival_slot,
-            pad,
-        ]
-    ).astype(jnp.int32)
-
-    first_old = old0(own_len, qt, cache_t)
-
-    positions = jnp.stack([own_len, second_len + 1]).astype(F32)
-    freq = 10000.0 ** (-2.0 * jnp.arange(32, dtype=F32) / 64)
-    angle = positions[:, :, None] * jnp.tile(freq, 4)[None, None, :]
-    keep = jnp.arange(128) < 64
-    cosine = jnp.where(keep, jnp.cos(angle), 0.0)
-    sine = jnp.where(keep, jnp.sin(angle), 0.0)
-
-    arrived = [
-        lax.all_to_all(sends[s], "dp", split_axis=0, concat_axis=0, tiled=True) for s in range(2)
-    ]
-    keep, send = gate_up(at, arrived[0], w_gate, w_up, first_old[1])
+    first_old = old0(table, qt, cache_t)
+
+    arrived = [to_dp(sends[s]) for s in range(2)]
+    keep, send = gate_up(at, arrived[0], w_gate, w_up, first_old[1], cosine)
     own0, parts0 = pair_sum(keep, send)
-    second_old = old1(old_table, qt, cache_t, parts0[0])
-    keep, send = gate_up(at, arrived[1], w_gate, w_up, second_old[1])
+    second_old = old1(table, qt, cache_t, parts0[0])
+    act0 = activate(own0, parts0)
+    keep, send = gate_up(at, arrived[1], w_gate, w_up, second_old[1], act0)
     own1, parts1 = pair_sum(keep, send)
-    pieces = cut_pieces(leaving.astype(jnp.int32), cache_t, arrived[1])
-    spread = lax.all_to_all(pieces, "dp", split_axis=0, concat_axis=0, tiled=True)
-    result0 = finish(at, own0, parts0, w_down)
-    result1 = finish(at, own1, parts1, w_down)
-    key0, block0, mixed0 = make_keys(0, at, gathered, result0, latent_t, cosine[0], sine[0])
-    attended = merge(0, old_table, qt, first_old, [key0], None)
-    onward = forward(forward_idx, spread.reshape(2 * N_DP, 144, 128), block0)
-    key1, _, mixed1 = make_keys(1, at, gathered, result1, latent_t, cosine[1], sine[1])
-    landed = lax.all_to_all(onward, "dp", split_axis=0, concat_axis=0, tiled=True)
-    attended = merge(1, old_table, qt, second_old, [key0, key1], attended)
-    attended = moved_rows(old_table, qt, landed, key1, attended)
+    pieces = cut_pieces(table, cache_t, arrived[1])
+    spread = to_dp(pieces)
+    result0 = finish(at, act0, w_down, spread)
+    back0 = to_dp(result0)
+    act1 = activate(own1, parts1)
+    result1 = finish(at, act1, w_down, spread)
+    back1 = to_dp(result1)
+    key0, block0, mixed0 = make_keys(0, at, gathered, back0, latent_t, cosine[0], sine[0], table)
+    onward = forward(table, spread.reshape(2 * N_DP, 144, 128), block0)
+    attended = merge(0, table, qt, first_old, [key0], None)
+    key1, _, mixed1 = make_keys(1, at, gathered, back1, latent_t, cosine[1], sine[1], onward)
+    landed = to_dp(onward)
+    attended = merge(1, table, qt, second_old, [key0, key1], attended)
+    attended = moved_rows(table, qt, landed, key1, attended)
     expert_out = jnp.stack([mixed0, mixed1]).astype(BF16)
     return (expert_out, attended)
 

time: 308 us -> 242 us (0.79)
  waiting for transfers between devices: 91.4 us -> 54.5 us
  Pallas kernels: 110 us -> 73.2 us
  starting transfers between devices: 52.4 us -> 61.2 us
    pallas_call x1, Pallas kernels: 37.7 us -> 2.15 us  [cut_pieces(): pl.pallas_call(cut_kernel, in_specs=[pl.BlockSpec(memory_space=pltpu.SMEM...]
    all_to_all x6, waiting for transfers between devices: 46.3 us -> 13.6 us  [to_dp(): return lax.all_to_all(v, 'dp', split_axis=0, concat_axis=0, tiled=True)]
    all_to_all x6, starting transfers between devices: 29.7 us -> 40.5 us  [to_dp(): return lax.all_to_all(v, 'dp', split_axis=0, concat_axis=0, tiled=True)]
    unnamed x112 -> x90, local copies, waits for them, and re-layouts: 23.9 us -> 29.6 us
    ppermute x30, waiting for transfers between devices: 45 us -> 41 us  [hop(): return lax.ppermute(v, 'ep', pairs)]
  transfers between devices with their start and end apart: 36 -> 36, of which waited for: 16 -> 14; matrix products, arithmetic and copies ran while one was open for 5% -> 4% of each run, Pallas kernels for 29% -> 19%
where the time goes in v3:
time: 242 us; the launch traced here: 240 us
  Pallas kernels  73.2 us (30%)
  starting transfers between devices  61.2 us (25%)
  waiting for transfers between devices  54.5 us (23%)
  local copies, waits for them, and re-layouts  29.7 us (12%)
  blocking collectives  11.7 us (5%)
  other arithmetic  8.8 us (4%)
    ppermute x30, waiting for transfers between devices, hop(): return lax.ppermute(v, 'ep', pairs)  41 us
    all_to_all x6, starting transfers between devices, to_dp(): return lax.all_to_all(v, 'dp', split_axis=0, concat_axis=0, tiled=True)  40.5 us
    unnamed x90, local copies, waits for them, and re-layouts  29.6 us
    ppermute x30, starting transfers between devices, hop(): return lax.ppermute(v, 'ep', pairs)  20.7 us
    pallas_call x2, Pallas kernels, gate_up(): pl.pallas_call(gateup_kernel, grid_spec=pltpu.PrefetchScalarGridSpec(num_...  17.5 us
    all_to_all x6, waiting for transfers between devices, to_dp(): return lax.all_to_all(v, 'dp', split_axis=0, concat_axis=0, tiled=True)  13.6 us
    pallas_call x2, Pallas kernels, merge(): pl.pallas_call(functools.partial(merge_kernel, step), grid_spec=pltpu.Pre...  11.9 us
    all_to_all x1, blocking collectives, local(): lax.all_to_all(packed, 'ep', split_axis=0, concat_axis=0, tiled=True)  11.7 us
  transfers between devices with their start and end apart: 36, of which 14 were waited for; matrix products, arithmetic and copies ran while one was open for 4% of the time, Pallas kernels for 19%

profile of v3, /device:TPU:0, one launch (start us, length us, event | category | flops | bytes accessed | tf_op | source)
XLA Modules:
  0.0 240.3 jit_solution(6406755886855328579)
XLA Ops:
  3.2 11.7 %all_to_all.35.r_ref = bf16[8,16,1024]{2,1,0:T(8,128)(2,1)S(1)} all-to-all(bf16[8,16,1024]{2,1,0:T(8,128)(2,1)S(1)} %pack.1), channel_id=1, replica_groups=mesh['dp'=16,'ep'=8] {'ep'}, dimensions={0} | all-to-all | bytes 524288 | tf_op jit(solution)/shard_map/all_to_all | solution.py:670
  19.0 8.1 %all-to-all-start.1 = ((bf16[16,48,896]{2,1,0:T(8,128)(2,1)}), bf16[16,48,896]{2,1,0:T(8,128)(2,1)}, u32[]{:S(2)}, u32[]{:S(2)}) async-start(bf16[16,48,896]{2,1,0:T(8,128)(2,1)} %copy-done.18), calls=%async_computation.1 | async-start | bytes 2752512 | tf_op jit(solution)/shard_map/all_to_all | solution.py:571
  29.0 8.0 %old0.1 = (f32[8,128,512]{2,1,0:T(8,128)S(1)}, f32[8,128,128]{2,1,0:T(8,128)S(1)}) custom-call(s32[8,128]{1,0:T(8,128)S(1)} %get-tuple-element.33.len_ref.leaving_ref.after_ref.tab_ref.idx_ref, bf16[2,8,576,128]{3,2,1,0:T(8,128)(2,1)S(1)} %bitcast.44, bf16[8,576,512]{2,1,0:T(8,128)(2,1)} %bitcast.52), custom_call_target="tpu_custom_call" | custom-call | flops 5000000000 | bytes 8000000 | tf_op jit(solution)/shard_map/old0/pallas_call | solution.py:364
  38.4 10.0 %all-to-all-done.1.x_ref = bf16[16,48,896]{2,1,0:T(8,128)(2,1)} async-done(((bf16[16,48,896]{2,1,0:T(8,128)(2,1)}), bf16[16,48,896]{2,1,0:T(8,128)(2,1)}, u32[]{:S(2)}, u32[]{:S(2)}) %all-to-all-start.1) | async-done | bytes 1376288 | tf_op jit(solution)/shard_map/all_to_all | solution.py:571
  48.4 8.8 %gate_up.2 = (bf16[4,2,384,256]{3,2,1,0:T(8,128)(2,1)S(1)}, bf16[4,2,384,256]{3,2,1,0:T(8,128)(2,1)}) custom-call(s32[2]{0:T(128)S(1)} %pad_add_fusion.at_ref, bf16[16,48,896]{2,1,0:T(8,128)(2,1)} %all-to-all-done.1.x_ref, bf16[2,896,1024]{2,1,0:T(8,128)(2,1)} %wg_ref.3, bf16[2,896,1024]{2,1,0:T(8,128)(2,1)} %wu_ref.3, ...), custom_call_target="tpu_custom_call" | custom-call | flops 4000000000 | bytes 12000000 | tf_op jit(solution)/shard_map/gate_up/pallas_call | solution.py:211
  58.4 4.4 %all-to-all-start.2 = ((bf16[16,48,896]{2,1,0:T(8,128)(2,1)}), bf16[16,48,896]{2,1,0:T(8,128)(2,1)}, u32[]{:S(2)}, u32[]{:S(2)}) async-start(bf16[16,48,896]{2,1,0:T(8,128)(2,1)} %copy-done.17), calls=%async_computation.2 | async-start | bytes 2752512 | tf_op jit(solution)/shard_map/all_to_all | solution.py:571
  67.4 8.1 %old1.1 = (f32[8,128,512]{2,1,0:T(8,128)S(1)}, f32[8,128,128]{2,1,0:T(8,128)S(1)}) custom-call(s32[8,128]{1,0:T(8,128)S(1)} %get-tuple-element.33.len_ref.leaving_ref.after_ref.tab_ref.idx_ref, bf16[2,8,576,128]{3,2,1,0:T(8,128)(2,1)S(1)} %bitcast.45, bf16[8,576,512]{2,1,0:T(8,128)(2,1)} %bitcast.53, bf16[2,384,256]{2,1,0:T(8,128)(2,1)S(1)} %get-tuple-element.67.after_ref), custom_call_target="tpu_custom_call" | custom-call | flops 5000000000 | bytes 8000000 | tf_op jit(solution)/shard_map/old1/pallas_call | solution.py:383
  76.7 2.6 %collective-permute-done.2 = bf16[2,384,256]{2,1,0:T(8,128)(2,1)S(1)} collective-permute-done((bf16[2,384,256]{2,1,0:T(8,128)(2,1)S(1)}, bf16[2,384,256]{2,1,0:T(8,128)(2,1)S(1)}, u32[]{:S(2)}, u32[]{:S(2)}) %collective-permute-start.2) | collective-permute-done | bytes 393248 | tf_op jit(solution)/shard_map/ppermute | solution.py:575
  79.4 7.7 %collective-permute-done.1 = bf16[2,384,256]{2,1,0:T(8,128)(2,1)S(1)} collective-permute-done((bf16[2,384,256]{2,1,0:T(8,128)(2,1)S(1)}, bf16[2,384,256]{2,1,0:T(8,128)(2,1)S(1)}, u32[]{:S(2)}, u32[]{:S(2)}) %collective-permute-start.1) | collective-permute-done | bytes 393248 | tf_op jit(solution)/shard_map/ppermute | solution.py:575
  88.6 8.8 %gate_up.3 = (bf16[4,2,384,256]{3,2,1,0:T(8,128)(2,1)S(1)}, bf16[4,2,384,256]{3,2,1,0:T(8,128)(2,1)}) custom-call(s32[2]{0:T(128)S(1)} %pad_add_fusion.at_ref, bf16[16,48,896]{2,1,0:T(8,128)(2,1)} %all-to-all-done.2.after_ref.x_ref, bf16[2,896,1024]{2,1,0:T(8,128)(2,1)} %wg_ref.3, bf16[2,896,1024]{2,1,0:T(8,128)(2,1)} %wu_ref.3, ...), custom_call_target="tpu_custom_call" | custom-call | flops 4000000000 | bytes 12000000 | tf_op jit(solution)/shard_map/gate_up/pallas_call | solution.py:211
  101.7 6.8 %all-to-all-start.3 = ((bf16[16,2,144,128]{3,2,1,0:T(8,128)(2,1)}), bf16[16,2,144,128]{3,2,1,0:T(8,128)(2,1)S(1)}, u32[]{:S(2)}, u32[]{:S(2)}) async-start(bf16[16,2,144,128]{3,2,1,0:T(8,128)(2,1)} %copy-done.5), calls=%async_computation.3 | async-start | bytes 2359296 | tf_op jit(solution)/shard_map/all_to_all | solution.py:571
  108.6 3.2 %collective-permute-start.5 = (bf16[2,384,128]{2,1,0:T(8,128)(2,1)}, bf16[2,384,128]{2,1,0:T(8,128)(2,1)}, u32[]{:S(2)}, u32[]{:S(2)}) collective-permute-start(bf16[2,384,128]{2,1,0:T(8,128)(2,1)} %copy-done.19), channel_id=1, source_target_pairs={{0,6},{1,7},{2,0},{3,1},{4,2},{5,3},{6,4},{7,5},{8,14},{9,15},{10,... | collective-permute-start | bytes 589832 | tf_op jit(solution)/shard_map/ppermute | solution.py:575
  112.0 9.2 %collective-permute-done.4.refs_1_ = bf16[2,384,128]{2,1,0:T(8,128)(2,1)S(1)} collective-permute-done((bf16[2,384,128]{2,1,0:T(8,128)(2,1)}, bf16[2,384,128]{2,1,0:T(8,128)(2,1)S(1)}, u32[]{:S(2)}, u32[]{:S(2)}) %collective-permute-start.4) | collective-permute-done | bytes 196640 | tf_op jit(solution)/shard_map/ppermute | solution.py:575
  121.8 2.8 %fusion.7 = (bf16[2,384,256]{2,1,0:T(8,128)(2,1)}, bf16[2,384,256]{2,1,0:T(8,128)(2,1)}, bf16[2,384,256]{2,1,0:T(8,128)(2,1)}) fusion(bf16[4,2,384,256]{3,2,1,0:T(8,128)(2,1)} %collective-permute-done.15, bf16[4,2,384,256]{3,2,1,0:T(8,128)(2,1)} %copy-done.15), kind=kLoop, calls=%fused_computation.15 | loop fusion | flops 2359296 | bytes 3538944 | tf_op jit(solution)/shard_map/convert_element_type | solution.py:580
  124.6 3.0 %collective-permute-start.18 = (bf16[2,384,256]{2,1,0:T(8,128)(2,1)}, bf16[2,384,256]{2,1,0:T(8,128)(2,1)}, u32[]{:S(2)}, u32[]{:S(2)}) collective-permute-start(bf16[2,384,256]{2,1,0:T(8,128)(2,1)} %get-tuple-element.63), channel_id=1, source_target_pairs={{0,6},{1,7},{2,0},{3,1},{4,2},{5,3},{6,4},{7,5},{8,14},{9,15},{10,... | collective-permute-start | bytes 1179656 | tf_op jit(solution)/shard_map/ppermute | solution.py:575
  133.5 4.2 %down.2 = bf16[16,48,896]{2,1,0:T(8,128)(2,1)S(1)} custom-call(s32[2]{0:T(128)S(1)} %pad_add_fusion.at_ref, bf16[2,384,128]{2,1,0:T(8,128)(2,1)S(1)} %copy-done.20, bf16[2,384,128]{2,1,0:T(8,128)(2,1)S(1)} %copy-done.29, bf16[2,384,128]{2,1,0:T(8,128)(2,1)} %collective-permute-done.5.refs_2_, bf16[2,384,128]{2,1,0:T(8,128)(2,1)} %collective-permute-done.6.refs_3_, ...), custom_call_target="tpu_custom_call" | custom-call | flops 2000000000 | bytes 8000000 | tf_op jit(solution)/shard_map/down/pallas_call | solution.py:255
  138.9 6.9 %all-to-all-start.4 = ((bf16[16,48,896]{2,1,0:T(8,128)(2,1)}), bf16[16,48,896]{2,1,0:T(8,128)(2,1)}, u32[]{:S(2)}, u32[]{:S(2)}) async-start(bf16[16,48,896]{2,1,0:T(8,128)(2,1)} %copy-done.3), calls=%async_computation.4 | async-start | bytes 2752512 | tf_op jit(solution)/shard_map/all_to_all | solution.py:571
  145.8 3.4 %collective-permute-done.16 = bf16[2,384,256]{2,1,0:T(8,128)(2,1)} collective-permute-done((bf16[2,384,256]{2,1,0:T(8,128)(2,1)}, bf16[2,384,256]{2,1,0:T(8,128)(2,1)}, u32[]{:S(2)}, u32[]{:S(2)}) %collective-permute-start.16) | collective-permute-done | bytes 393248 | tf_op jit(solution)/shard_map/ppermute | solution.py:575
  151.1 3.2 %collective-permute-start.20 = (bf16[2,384,128]{2,1,0:T(8,128)(2,1)S(1)}, bf16[2,384,128]{2,1,0:T(8,128)(2,1)S(1)}, u32[]{:S(2)}, u32[]{:S(2)}) collective-permute-start(bf16[2,384,128]{2,1,0:T(8,128)(2,1)S(1)} %fusion.10.refs_0_), channel_id=1, source_target_pairs={{0,6},{1,7},{2,0},{3,1},{4,2},{5,3},{6,4},{7,5},{8,14},{9,15},{10,... | collective-permute-start | bytes 589832 | tf_op jit(solution)/shard_map/ppermute | solution.py:575
  154.4 9.0 %collective-permute-done.19.refs_1_ = bf16[2,384,128]{2,1,0:T(8,128)(2,1)S(1)} collective-permute-done((bf16[2,384,128]{2,1,0:T(8,128)(2,1)S(1)}, bf16[2,384,128]{2,1,0:T(8,128)(2,1)S(1)}, u32[]{:S(2)}, u32[]{:S(2)}) %collective-permute-start.19) | collective-permute-done | bytes 196640 | tf_op jit(solution)/shard_map/ppermute | solution.py:575
  165.4 3.8 %down.3 = bf16[16,48,896]{2,1,0:T(8,128)(2,1)S(1)} custom-call(s32[2]{0:T(128)S(1)} %pad_add_fusion.at_ref, bf16[2,384,128]{2,1,0:T(8,128)(2,1)S(1)} %fusion.10.refs_0_, bf16[2,384,128]{2,1,0:T(8,128)(2,1)S(1)} %collective-permute-done.19.refs_1_, bf16[2,384,128]{2,1,0:T(8,128)(2,1)S(1)} %collective-permute-done.20.refs_2_, ...), custom_call_target="tpu_custom_call" | custom-call | flops 2000000000 | bytes 8000000 | tf_op jit(solution)/shard_map/down/pallas_call | solution.py:255
  170.4 6.9 %all-to-all-start.5 = ((bf16[16,48,896]{2,1,0:T(8,128)(2,1)}), bf16[16,48,896]{2,1,0:T(8,128)(2,1)}, u32[]{:S(2)}, u32[]{:S(2)}) async-start(bf16[16,48,896]{2,1,0:T(8,128)(2,1)} %copy-done.4), calls=%async_computation.5 | async-start | bytes 2752512 | tf_op jit(solution)/shard_map/all_to_all | solution.py:571
  183.6 2.8 %collective-permute-start.12 = (f32[8,2560]{1,0:T(8,128)S(1)}, f32[8,2560]{1,0:T(8,128)S(1)}, u32[]{:S(2)}, u32[]{:S(2)}) collective-permute-start(f32[8,2560]{1,0:T(8,128)S(1)} %get-tuple-element.42), channel_id=1, source_target_pairs={{0,6},{1,7},{2,0},{3,1},{4,2},{5,3},{6,4},{7,5},{8,14},{9,15},{10,... | collective-permute-start | bytes 245768 | tf_op jit(solution)/shard_map/ppermute | solution.py:575
  187.3 2.8 %collective-permute-done.12.u1_ref = f32[8,2560]{1,0:T(8,128)S(1)} collective-permute-done((f32[8,2560]{1,0:T(8,128)S(1)}, f32[8,2560]{1,0:T(8,128)S(1)}, u32[]{:S(2)}, u32[]{:S(2)}) %collective-permute-start.12) | collective-permute-done | bytes 81952 | tf_op jit(solution)/shard_map/ppermute | solution.py:575
  190.1 2.8 %collective-permute-done.13.u2_ref = f32[8,2560]{1,0:T(8,128)S(1)} collective-permute-done((f32[8,2560]{1,0:T(8,128)S(1)}, f32[8,2560]{1,0:T(8,128)S(1)}, u32[]{:S(2)}, u32[]{:S(2)}) %collective-permute-start.13) | collective-permute-done | bytes 81952 | tf_op jit(solution)/shard_map/ppermute | solution.py:575
  195.5 3.0 %forward.1.after_ref = bf16[16,336,128]{2,1,0:T(8,128)(2,1)S(1)} custom-call(s32[8,128]{1,0:T(8,128)S(1)} %get-tuple-element.33.len_ref.leaving_ref.after_ref.tab_ref.idx_ref, bf16[32,144,128]{2,1,0:T(8,128)(2,1)S(1)} %bitcast.49, bf16[48,128]{1,0:T(8,128)(2,1)S(1)} %get-tuple-element.50.key_ref), custom_call_target="tpu_custom_call" | custom-call | flops 1000000 | bytes 3000000 | tf_op jit(solution)/shard_map/forward/pallas_call | solution.py:552
  203.1 3.2 %combine1.1 = (f32[4,8,1664]{2,1,0:T(8,128)S(1)}, f32[4,8,1664]{2,1,0:T(8,128)}) custom-call(s32[2]{0:T(128)S(1)} %pad_add_fusion.at_ref, bf16[8,16,1024]{2,1,0:T(8,128)(2,1)S(1)} %copy-done.8, bf16[16,48,896]{2,1,0:T(8,128)(2,1)} %all-to-all-done.5.ret_ref, bf16[576,896]{1,0:T(8,128)(2,1)S(1)} %bitcast.51, bf16[16,336,128]{2,1,0:T(8,128)(2,1)S(1)} %copy-done.2), custom_call_target="tpu_custom_call" | custom-call | flops 400000000 | bytes 4000000 | tf_op jit(solution)/shard_map/combine1/pallas_call | solution.py:605
  206.3 7.4 %all-to-all-start.6 = ((bf16[16,336,128]{2,1,0:T(8,128)(2,1)}), bf16[16,336,128]{2,1,0:T(8,128)(2,1)}, u32[]{:S(2)}, u32[]{:S(2)}) async-start(bf16[16,336,128]{2,1,0:T(8,128)(2,1)} %copy-done.1), calls=%async_computation.6 | async-start | bytes 2752512 | tf_op jit(solution)/shard_map/all_to_all | solution.py:571
  218.4 5.8 %merge0.1.refs_2_ = bf16[2,8,128,512]{3,2,1,0:T(8,128)(2,1)} custom-call(s32[8,128]{1,0:T(8,128)S(1)} %get-tuple-element.33.len_ref.leaving_ref.after_ref.tab_ref.idx_ref, bf16[2,8,576,128]{3,2,1,0:T(8,128)(2,1)S(1)} %bitcast.46, f32[8,128,512]{2,1,0:T(8,128)S(1)} %copy-done.14, f32[8,128,128]{2,1,0:T(8,128)S(1)} %copy-done.24, f32[8,640]{1,0:T(8,128)S(1)} %copy-done.35), custom_call_target="tpu_custom_call" | custom-call | flops 100000000 | bytes 5000000 | tf_op jit(solution)/shard_map/merge0/pallas_call | solution.py:448
  225.6 6.1 %merge1.1.buffer_ref = bf16[2,8,128,512]{3,2,1,0:T(8,128)(2,1)} custom-call(s32[8,128]{1,0:T(8,128)S(1)} %get-tuple-element.33.len_ref.leaving_ref.after_ref.tab_ref.idx_ref, bf16[2,8,576,128]{3,2,1,0:T(8,128)(2,1)S(1)} %bitcast.47, f32[8,128,512]{2,1,0:T(8,128)S(1)} %copy-done.12, f32[8,128,128]{2,1,0:T(8,128)S(1)} %copy-done.22, ...), custom_call_target="tpu_custom_call", output_to_operand_aliasing={{}: (6, {})} | custom-call | flops 100000000 | bytes 5000000 | tf_op jit(solution)/shard_map/merge1/pallas_call | solution.py:448
  232.4 3.6 %all-to-all-done.6.kv_ref.keys_ref = bf16[16,336,128]{2,1,0:T(8,128)(2,1)} async-done(((bf16[16,336,128]{2,1,0:T(8,128)(2,1)}), bf16[16,336,128]{2,1,0:T(8,128)(2,1)}, u32[]{:S(2)}, u32[]{:S(2)}) %all-to-all-start.6) | async-done | bytes 1376288 | tf_op jit(solution)/shard_map/all_to_all | solution.py:571
  236.0 4.3 %moved_rows.1 = bf16[2,8,128,512]{3,2,1,0:T(8,128)(2,1)} custom-call(s32[8,128]{1,0:T(8,128)S(1)} %get-tuple-element.33.len_ref.leaving_ref.after_ref.tab_ref.idx_ref, bf16[2,8,576,128]{3,2,1,0:T(8,128)(2,1)S(1)} %bitcast.48, bf16[16,336,128]{2,1,0:T(8,128)(2,1)} %all-to-all-done.6.kv_ref.keys_ref, ...), custom_call_target="tpu_custom_call", output_to_operand_aliasing={{}: (5, {})} | custom-call | flops 600000000 | bytes 3000000 | tf_op jit(solution)/shard_map/moved_rows/pallas_call | solution.py:485
  (165 shorter events, 56.9 us)
Async XLA Ops:
  19.0 29.3 %all-to-all-start.1 = ((bf16[16,48,896]{2,1,0:T(8,128)(2,1)}), bf16[16,48,896]{2,1,0:T(8,128)(2,1)}, u32[]{:S(2)}, u32[]{:S(2)}) async-start(bf16[16,48,896]{2,1,0:T(8,128)(2,1)} %copy-done.18), calls=%async_computation.1 | async-start | bytes 2752512 | tf_op jit(solution)/shard_map/all_to_all | solution.py:571
  58.4 4.4 %collective-permute-start = (bf16[4,2,384,256]{3,2,1,0:T(8,128)(2,1)}, bf16[4,2,384,256]{3,2,1,0:T(8,128)(2,1)}, u32[]{:S(2)}, u32[]{:S(2)}) collective-permute-start(bf16[4,2,384,256]{3,2,1,0:T(8,128)(2,1)} %get-tuple-element.37), channel_id=1, source_target_pairs={{0,1},{1,0},{2,3},{3,2},{4,5},{5,4},{6,7},{7,6},{8,9},{9,8},{10,11... | collective-permute-start | bytes 4718600 | tf_op jit(solution)/shard_map/ppermute | solution.py:575
  58.4 30.2 %all-to-all-start.2 = ((bf16[16,48,896]{2,1,0:T(8,128)(2,1)}), bf16[16,48,896]{2,1,0:T(8,128)(2,1)}, u32[]{:S(2)}, u32[]{:S(2)}) async-start(bf16[16,48,896]{2,1,0:T(8,128)(2,1)} %copy-done.17), calls=%async_computation.2 | async-start | bytes 2752512 | tf_op jit(solution)/shard_map/all_to_all | solution.py:571
  64.6 12.1 %collective-permute-start.3 = (bf16[2,384,256]{2,1,0:T(8,128)(2,1)S(1)}, bf16[2,384,256]{2,1,0:T(8,128)(2,1)S(1)}, u32[]{:S(2)}, u32[]{:S(2)}) collective-permute-start(bf16[2,384,256]{2,1,0:T(8,128)(2,1)S(1)} %get-tuple-element.66), channel_id=1, source_target_pairs={{0,6},{1,7},{2,0},{3,1},{4,2},{5,3},{6,4},{7,5},{8,14},{9,15},{10,... | collective-permute-start | bytes 1179656 | tf_op jit(solution)/shard_map/ppermute | solution.py:575
  65.9 13.5 %collective-permute-start.2 = (bf16[2,384,256]{2,1,0:T(8,128)(2,1)S(1)}, bf16[2,384,256]{2,1,0:T(8,128)(2,1)S(1)}, u32[]{:S(2)}, u32[]{:S(2)}) collective-permute-start(bf16[2,384,256]{2,1,0:T(8,128)(2,1)S(1)} %get-tuple-element.65), channel_id=1, source_target_pairs={{0,4},{1,5},{2,6},{3,7},{4,0},{5,1},{6,2},{7,3},{8,12},{9,13},{10,... | collective-permute-start | bytes 1179656 | tf_op jit(solution)/shard_map/ppermute | solution.py:575
  67.4 19.7 %collective-permute-start.1 = (bf16[2,384,256]{2,1,0:T(8,128)(2,1)S(1)}, bf16[2,384,256]{2,1,0:T(8,128)(2,1)S(1)}, u32[]{:S(2)}, u32[]{:S(2)}) collective-permute-start(bf16[2,384,256]{2,1,0:T(8,128)(2,1)S(1)} %get-tuple-element.67.after_ref), channel_id=1, source_target_pairs={{0,2},{1,3},{2,4},{3,5},{4,6},{5,7},{6,0},{7,1},{8,10},{9,11},{10,... | collective-permute-start | bytes 1179656 | tf_op jit(solution)/shard_map/ppermute | solution.py:575
  98.5 23.3 %collective-permute-start.15 = (bf16[4,2,384,256]{3,2,1,0:T(8,128)(2,1)}, bf16[4,2,384,256]{3,2,1,0:T(8,128)(2,1)}, u32[]{:S(2)}, u32[]{:S(2)}) collective-permute-start(bf16[4,2,384,256]{3,2,1,0:T(8,128)(2,1)} %get-tuple-element.49), channel_id=1, source_target_pairs={{0,1},{1,0},{2,3},{3,2},{4,5},{5,4},{6,7},{7,6},{8,9},{9,8},{10,11... | collective-permute-start | bytes 4718600 | tf_op jit(solution)/shard_map/ppermute | solution.py:575
  101.7 28.1 %all-to-all-start.3 = ((bf16[16,2,144,128]{3,2,1,0:T(8,128)(2,1)}), bf16[16,2,144,128]{3,2,1,0:T(8,128)(2,1)S(1)}, u32[]{:S(2)}, u32[]{:S(2)}) async-start(bf16[16,2,144,128]{3,2,1,0:T(8,128)(2,1)} %copy-done.5), calls=%async_computation.3 | async-start | bytes 2359296 | tf_op jit(solution)/shard_map/all_to_all | solution.py:571
  108.5 12.7 %collective-permute-start.4 = (bf16[2,384,128]{2,1,0:T(8,128)(2,1)}, bf16[2,384,128]{2,1,0:T(8,128)(2,1)S(1)}, u32[]{:S(2)}, u32[]{:S(2)}) collective-permute-start(bf16[2,384,128]{2,1,0:T(8,128)(2,1)} %copy-done.19), channel_id=1, source_target_pairs={{0,2},{1,3},{2,4},{3,5},{4,6},{5,7},{6,0},{7,1},{8,10},{9,11},{10,... | collective-permute-start | bytes 589832 | tf_op jit(solution)/shard_map/ppermute | solution.py:575
  108.6 12.6 %collective-permute-start.5 = (bf16[2,384,128]{2,1,0:T(8,128)(2,1)}, bf16[2,384,128]{2,1,0:T(8,128)(2,1)}, u32[]{:S(2)}, u32[]{:S(2)}) collective-permute-start(bf16[2,384,128]{2,1,0:T(8,128)(2,1)} %copy-done.19), channel_id=1, source_target_pairs={{0,6},{1,7},{2,0},{3,1},{4,2},{5,3},{6,4},{7,5},{8,14},{9,15},{10,... | collective-permute-start | bytes 589832 | tf_op jit(solution)/shard_map/ppermute | solution.py:575
  111.8 9.9 %collective-permute-start.6 = (bf16[2,384,128]{2,1,0:T(8,128)(2,1)}, bf16[2,384,128]{2,1,0:T(8,128)(2,1)}, u32[]{:S(2)}, u32[]{:S(2)}) collective-permute-start(bf16[2,384,128]{2,1,0:T(8,128)(2,1)} %copy-done.19), channel_id=1, source_target_pairs={{0,4},{1,5},{2,6},{3,7},{4,0},{5,1},{6,2},{7,3},{8,12},{9,13},{10,... | collective-permute-start | bytes 589832 | tf_op jit(solution)/shard_map/ppermute | solution.py:575
  112.0 15.5 %collective-permute-start.7 = (bf16[2,384,128]{2,1,0:T(8,128)(2,1)}, bf16[2,384,128]{2,1,0:T(8,128)(2,1)S(1)}, u32[]{:S(2)}, u32[]{:S(2)}) collective-permute-start(bf16[2,384,128]{2,1,0:T(8,128)(2,1)} %copy-done.19), channel_id=1, source_target_pairs={{0,1},{1,0},{2,3},{3,2},{4,5},{5,4},{6,7},{7,6},{8,9},{9,8},{10,11... | collective-permute-start | bytes 589832 | tf_op jit(solution)/shard_map/ppermute | solution.py:575
  121.2 7.0 %collective-permute-start.8 = (bf16[2,384,128]{2,1,0:T(8,128)(2,1)S(1)}, bf16[2,384,128]{2,1,0:T(8,128)(2,1)S(1)}, u32[]{:S(2)}, u32[]{:S(2)}) collective-permute-start(bf16[2,384,128]{2,1,0:T(8,128)(2,1)S(1)} %collective-permute-done.4.refs_1_), channel_id=1, source_target_pairs={{0,1},{1,0},{2,3},{3,2},{4,5},{5,4},{6,7},{7,6},{8,9},{9,8},{10,11... | collective-permute-start | bytes 589832 | tf_op jit(solution)/shard_map/ppermute | solution.py:575
  121.2 8.6 %collective-permute-start.9 = (bf16[2,384,128]{2,1,0:T(8,128)(2,1)}, bf16[2,384,128]{2,1,0:T(8,128)(2,1)}, u32[]{:S(2)}, u32[]{:S(2)}) collective-permute-start(bf16[2,384,128]{2,1,0:T(8,128)(2,1)} %collective-permute-done.5.refs_2_), channel_id=1, source_target_pairs={{0,1},{1,0},{2,3},{3,2},{4,5},{5,4},{6,7},{7,6},{8,9},{9,8},{10,11... | collective-permute-start | bytes 589832 | tf_op jit(solution)/shard_map/ppermute | solution.py:575
  121.7 8.1 %collective-permute-start.10 = (bf16[2,384,128]{2,1,0:T(8,128)(2,1)}, bf16[2,384,128]{2,1,0:T(8,128)(2,1)}, u32[]{:S(2)}, u32[]{:S(2)}) collective-permute-start(bf16[2,384,128]{2,1,0:T(8,128)(2,1)} %collective-permute-done.6.refs_3_), channel_id=1, source_target_pairs={{0,1},{1,0},{2,3},{3,2},{4,5},{5,4},{6,7},{7,6},{8,9},{9,8},{10,11... | collective-permute-start | bytes 589832 | tf_op jit(solution)/shard_map/ppermute | solution.py:575
  124.6 21.2 %collective-permute-start.18 = (bf16[2,384,256]{2,1,0:T(8,128)(2,1)}, bf16[2,384,256]{2,1,0:T(8,128)(2,1)}, u32[]{:S(2)}, u32[]{:S(2)}) collective-permute-start(bf16[2,384,256]{2,1,0:T(8,128)(2,1)} %get-tuple-element.63), channel_id=1, source_target_pairs={{0,6},{1,7},{2,0},{3,1},{4,2},{5,3},{6,4},{7,5},{8,14},{9,15},{10,... | collective-permute-start | bytes 1179656 | tf_op jit(solution)/shard_map/ppermute | solution.py:575
  128.2 17.6 %collective-permute-start.17 = (bf16[2,384,256]{2,1,0:T(8,128)(2,1)}, bf16[2,384,256]{2,1,0:T(8,128)(2,1)}, u32[]{:S(2)}, u32[]{:S(2)}) collective-permute-start(bf16[2,384,256]{2,1,0:T(8,128)(2,1)} %get-tuple-element.64), channel_id=1, source_target_pairs={{0,4},{1,5},{2,6},{3,7},{4,0},{5,1},{6,2},{7,3},{8,12},{9,13},{10,... | collective-permute-start | bytes 1179656 | tf_op jit(solution)/shard_map/ppermute | solution.py:575
  128.9 20.3 %collective-permute-start.16 = (bf16[2,384,256]{2,1,0:T(8,128)(2,1)}, bf16[2,384,256]{2,1,0:T(8,128)(2,1)}, u32[]{:S(2)}, u32[]{:S(2)}) collective-permute-start(bf16[2,384,256]{2,1,0:T(8,128)(2,1)} %get-tuple-element.62), channel_id=1, source_target_pairs={{0,2},{1,3},{2,4},{3,5},{4,6},{5,7},{6,0},{7,1},{8,10},{9,11},{10,... | collective-permute-start | bytes 1179656 | tf_op jit(solution)/shard_map/ppermute | solution.py:575
  138.9 31.5 %all-to-all-start.4 = ((bf16[16,48,896]{2,1,0:T(8,128)(2,1)}), bf16[16,48,896]{2,1,0:T(8,128)(2,1)}, u32[]{:S(2)}, u32[]{:S(2)}) async-start(bf16[16,48,896]{2,1,0:T(8,128)(2,1)} %copy-done.3), calls=%async_computation.4 | async-start | bytes 2752512 | tf_op jit(solution)/shard_map/all_to_all | solution.py:571
  151.1 12.3 %collective-permute-start.19 = (bf16[2,384,128]{2,1,0:T(8,128)(2,1)S(1)}, bf16[2,384,128]{2,1,0:T(8,128)(2,1)S(1)}, u32[]{:S(2)}, u32[]{:S(2)}) collective-permute-start(bf16[2,384,128]{2,1,0:T(8,128)(2,1)S(1)} %fusion.10.refs_0_), channel_id=1, source_target_pairs={{0,2},{1,3},{2,4},{3,5},{4,6},{5,7},{6,0},{7,1},{8,10},{9,11},{10,... | collective-permute-start | bytes 589832 | tf_op jit(solution)/shard_map/ppermute | solution.py:575
  151.1 12.2 %collective-permute-start.20 = (bf16[2,384,128]{2,1,0:T(8,128)(2,1)S(1)}, bf16[2,384,128]{2,1,0:T(8,128)(2,1)S(1)}, u32[]{:S(2)}, u32[]{:S(2)}) collective-permute-start(bf16[2,384,128]{2,1,0:T(8,128)(2,1)S(1)} %fusion.10.refs_0_), channel_id=1, source_target_pairs={{0,6},{1,7},{2,0},{3,1},{4,2},{5,3},{6,4},{7,5},{8,14},{9,15},{10,... | collective-permute-start | bytes 589832 | tf_op jit(solution)/shard_map/ppermute | solution.py:575
  154.4 9.5 %collective-permute-start.21 = (bf16[2,384,128]{2,1,0:T(8,128)(2,1)S(1)}, bf16[2,384,128]{2,1,0:T(8,128)(2,1)S(1)}, u32[]{:S(2)}, u32[]{:S(2)}) collective-permute-start(bf16[2,384,128]{2,1,0:T(8,128)(2,1)S(1)} %fusion.10.refs_0_), channel_id=1, source_target_pairs={{0,4},{1,5},{2,6},{3,7},{4,0},{5,1},{6,2},{7,3},{8,12},{9,13},{10,... | collective-permute-start | bytes 589832 | tf_op jit(solution)/shard_map/ppermute | solution.py:575
  154.4 9.6 %collective-permute-start.22 = (bf16[2,384,128]{2,1,0:T(8,128)(2,1)S(1)}, bf16[2,384,128]{2,1,0:T(8,128)(2,1)S(1)}, u32[]{:S(2)}, u32[]{:S(2)}) collective-permute-start(bf16[2,384,128]{2,1,0:T(8,128)(2,1)S(1)} %fusion.10.refs_0_), channel_id=1, source_target_pairs={{0,1},{1,0},{2,3},{3,2},{4,5},{5,4},{6,7},{7,6},{8,9},{9,8},{10,11... | collective-permute-start | bytes 589832 | tf_op jit(solution)/shard_map/ppermute | solution.py:575
  170.4 29.2 %all-to-all-start.5 = ((bf16[16,48,896]{2,1,0:T(8,128)(2,1)}), bf16[16,48,896]{2,1,0:T(8,128)(2,1)}, u32[]{:S(2)}, u32[]{:S(2)}) async-start(bf16[16,48,896]{2,1,0:T(8,128)(2,1)} %copy-done.4), calls=%async_computation.5 | async-start | bytes 2752512 | tf_op jit(solution)/shard_map/all_to_all | solution.py:571
  183.6 6.5 %collective-permute-start.12 = (f32[8,2560]{1,0:T(8,128)S(1)}, f32[8,2560]{1,0:T(8,128)S(1)}, u32[]{:S(2)}, u32[]{:S(2)}) collective-permute-start(f32[8,2560]{1,0:T(8,128)S(1)} %get-tuple-element.42), channel_id=1, source_target_pairs={{0,6},{1,7},{2,0},{3,1},{4,2},{5,3},{6,4},{7,5},{8,14},{9,15},{10,... | collective-permute-start | bytes 245768 | tf_op jit(solution)/shard_map/ppermute | solution.py:575
  186.3 6.6 %collective-permute-start.13 = (f32[8,2560]{1,0:T(8,128)S(1)}, f32[8,2560]{1,0:T(8,128)S(1)}, u32[]{:S(2)}, u32[]{:S(2)}) collective-permute-start(f32[8,2560]{1,0:T(8,128)S(1)} %get-tuple-element.43), channel_id=1, source_target_pairs={{0,4},{1,5},{2,6},{3,7},{4,0},{5,1},{6,2},{7,3},{8,12},{9,13},{10,... | collective-permute-start | bytes 245768 | tf_op jit(solution)/shard_map/ppermute | solution.py:575
  186.4 7.2 %collective-permute-start.14 = (f32[8,2560]{1,0:T(8,128)S(1)}, f32[8,2560]{1,0:T(8,128)S(1)}, u32[]{:S(2)}, u32[]{:S(2)}) collective-permute-start(f32[8,2560]{1,0:T(8,128)S(1)} %get-tuple-element.44), channel_id=1, source_target_pairs={{0,2},{1,3},{2,4},{3,5},{4,6},{5,7},{6,0},{7,1},{8,10},{9,11},{10,... | collective-permute-start | bytes 245768 | tf_op jit(solution)/shard_map/ppermute | solution.py:575
  206.3 7.4 %collective-permute-start.26 = (f32[4,8,1664]{2,1,0:T(8,128)}, f32[4,8,1664]{2,1,0:T(8,128)S(1)}, u32[]{:S(2)}, u32[]{:S(2)}) collective-permute-start(f32[4,8,1664]{2,1,0:T(8,128)} %get-tuple-element.52), channel_id=1, source_target_pairs={{0,1},{1,0},{2,3},{3,2},{4,5},{5,4},{6,7},{7,6},{8,9},{9,8},{10,11... | collective-permute-start | bytes 638984 | tf_op jit(solution)/shard_map/ppermute | solution.py:575
  206.3 29.7 %all-to-all-start.6 = ((bf16[16,336,128]{2,1,0:T(8,128)(2,1)}), bf16[16,336,128]{2,1,0:T(8,128)(2,1)}, u32[]{:S(2)}, u32[]{:S(2)}) async-start(bf16[16,336,128]{2,1,0:T(8,128)(2,1)} %copy-done.1), calls=%async_computation.6 | async-start | bytes 2752512 | tf_op jit(solution)/shard_map/all_to_all | solution.py:571
  213.8 10.5 %collective-permute-start.27 = (f32[8,2560]{1,0:T(8,128)S(1)}, f32[8,2560]{1,0:T(8,128)S(1)}, u32[]{:S(2)}, u32[]{:S(2)}) collective-permute-start(f32[8,2560]{1,0:T(8,128)S(1)} %get-tuple-element.54), channel_id=1, source_target_pairs={{0,6},{1,7},{2,0},{3,1},{4,2},{5,3},{6,4},{7,5},{8,14},{9,15},{10,... | collective-permute-start | bytes 245768 | tf_op jit(solution)/shard_map/ppermute | solution.py:575
  214.7 9.5 %collective-permute-start.28 = (f32[8,2560]{1,0:T(8,128)S(1)}, f32[8,2560]{1,0:T(8,128)S(1)}, u32[]{:S(2)}, u32[]{:S(2)}) collective-permute-start(f32[8,2560]{1,0:T(8,128)S(1)} %get-tuple-element.55), channel_id=1, source_target_pairs={{0,4},{1,5},{2,6},{3,7},{4,0},{5,1},{6,2},{7,3},{8,12},{9,13},{10,... | collective-permute-start | bytes 245768 | tf_op jit(solution)/shard_map/ppermute | solution.py:575
  215.0 9.3 %collective-permute-start.29 = (f32[8,2560]{1,0:T(8,128)S(1)}, f32[8,2560]{1,0:T(8,128)S(1)}, u32[]{:S(2)}, u32[]{:S(2)}) collective-permute-start(f32[8,2560]{1,0:T(8,128)S(1)} %get-tuple-element.56), channel_id=1, source_target_pairs={{0,2},{1,3},{2,4},{3,5},{4,6},{5,7},{6,0},{7,1},{8,10},{9,11},{10,... | collective-permute-start | bytes 245768 | tf_op jit(solution)/shard_map/ppermute | solution.py:575
  (49 other events, 198.6 us)

commit v4 on v3

--- a/solution.py
+++ b/solution.py
@@ -33,6 +33,17 @@
 VMEM = pl.BlockSpec(memory_space=pltpu.VMEM)
 ANY = pl.BlockSpec(memory_space=pl.ANY)
 PARAMS = pltpu.CompilerParams(vmem_limit_bytes=48 * 1024 * 1024)
+
+
+FULL = pltpu.CompilerParams(vmem_limit_bytes=60 * 1024 * 1024)
+
+
+def in_hbm(*shape):
+    return pltpu.HBM(shape, BF16)
+
+
+def whole(*shape):
+    return pl.BlockSpec(shape, lambda *_: (0,) * len(shape))
 
 
 def cost(flops, nbytes):
@@ -254,10 +265,13 @@
 def down(at, acts, w_down, after):
     return pl.pallas_call(
         down_kernel,
-        in_specs=[pl.BlockSpec(memory_space=pltpu.SMEM)] + [VMEM] * 9 + [ANY],
-        out_specs=VMEM,
-        out_shape=jax.ShapeDtypeStruct((N_DP, PER_DP, SLICE), BF16),
-        compiler_params=PARAMS,
+        grid=(1,),
+        in_specs=[pl.BlockSpec(memory_space=pltpu.SMEM)]
+        + [whole(2, HALF, 128)] * 8
+        + [whole(2, FF, SLICE), ANY],
+        out_specs=whole(N_DP, PER_DP, SLICE),
+        out_shape=in_hbm(N_DP, PER_DP, SLICE),
+        compiler_params=FULL,
         cost_estimate=cost(2e9, 8e6),
         name="down",
     )(at, *acts, w_down, after)
@@ -661,20 +675,22 @@
 
     packed = pl.pallas_call(
         pack_kernel,
-        in_specs=[VMEM] * 3,
-        out_specs=VMEM,
-        out_shape=jax.ShapeDtypeStruct((N_EP, 2 * ROWS, WIDE), BF16),
-        compiler_params=PARAMS,
+        grid=(1,),
+        in_specs=[whole(2, ROWS, D), whole(2, ROWS, TOPK), whole(2, ROWS, TOPK)],
+        out_specs=whole(N_EP, 2 * ROWS, WIDE),
+        out_shape=in_hbm(N_EP, 2 * ROWS, WIDE),
+        compiler_params=FULL,
         name="pack",
     )(hidden, expert_ids, expert_gates)
     gathered = lax.all_to_all(packed, "ep", split_axis=0, concat_axis=0, tiled=True)
-    out_shape = jax.ShapeDtypeStruct((N_DP, PER_DP, SLICE), BF16)
+    out_shape = in_hbm(N_DP, PER_DP, SLICE)
     sends = pl.pallas_call(
         dispatch_kernel,
-        in_specs=[VMEM],
-        out_specs=[VMEM, VMEM],
+        grid=(1,),
+        in_specs=[whole(N_EP, 2 * ROWS, WIDE)],
+        out_specs=[whole(N_DP, PER_DP, SLICE)] * 2,
         out_shape=[out_shape, out_shape],
-        compiler_params=PARAMS,
+        compiler_params=FULL,
         name="dispatch",
     )(gathered)
 

time: 242 us -> 240 us (level)
  local copies, waits for them, and re-layouts: 29.7 us -> 17.4 us
  Pallas kernels: 73.2 us -> 80.2 us
  waiting for transfers between devices: 54.5 us -> 58.4 us
    unnamed x90 -> x84, local copies, waits for them, and re-layouts: 29.6 us -> 17.3 us
    pallas_call x4, Pallas kernels: 9.45 us -> 16.4 us  [the longest x2 11.1 us: down(): pl.pallas_call(down_kernel, grid=(1,), in_specs=[pl.BlockSpec(memory_spac...]
    ppermute x30, waiting for transfers between devices: 41 us -> 43.4 us  [hop(): return lax.ppermute(v, 'ep', pairs)]
  transfers between devices with their start and end apart: 36 -> 36, of which waited for: 14 -> 16; matrix products, arithmetic and copies ran while one was open for 4% -> 4% of each run, Pallas kernels for 19% -> 21%
where the time goes in v4:
time: 240 us; the launch traced here: 238 us
  Pallas kernels  80.2 us (33%)
  starting transfers between devices  60 us (25%)
  waiting for transfers between devices  58.4 us (24%)
  local copies, waits for them, and re-layouts  17.4 us (7%)
  blocking collectives  12 us (5%)
  other arithmetic  8.8 us (4%)
    ppermute x30, waiting for transfers between devices, hop(): return lax.ppermute(v, 'ep', pairs)  43.4 us
    all_to_all x6, starting transfers between devices, to_dp(): return lax.all_to_all(v, 'dp', split_axis=0, concat_axis=0, tiled=True)  39.3 us
    ppermute x30, starting transfers between devices, hop(): return lax.ppermute(v, 'ep', pairs)  20.8 us
    pallas_call x2, Pallas kernels, gate_up(): pl.pallas_call(gateup_kernel, grid_spec=pltpu.PrefetchScalarGridSpec(num_...  17.6 us
    unnamed x84, local copies, waits for them, and re-layouts  17.3 us
    all_to_all x6, waiting for transfers between devices, to_dp(): return lax.all_to_all(v, 'dp', split_axis=0, concat_axis=0, tiled=True)  14.9 us
    all_to_all x1, blocking collectives, local(): lax.all_to_all(packed, 'ep', split_axis=0, concat_axis=0, tiled=True)  12 us
    pallas_call x2, Pallas kernels, merge(): pl.pallas_call(functools.partial(merge_kernel, step), grid_spec=pltpu.Pre...  11.9 us
  transfers between devices with their start and end apart: 36, of which 16 were waited for; matrix products, arithmetic and copies ran while one was open for 4% of the time, Pallas kernels for 21%

profile of v4, /device:TPU:0, one launch (start us, length us, event | category | flops | bytes accessed | tf_op | source)
XLA Modules:
  0.0 238.0 jit_solution(11392869604951863235)
XLA Ops:
  2.5 12.0 %all_to_all.35.r_ref = bf16[8,16,1024]{2,1,0:T(8,128)(2,1)} all-to-all(bf16[8,16,1024]{2,1,0:T(8,128)(2,1)} %pack.1), channel_id=1, replica_groups=mesh['dp'=16,'ep'=8] {'ep'}, dimensions={0} | all-to-all | bytes 524288 | tf_op jit(solution)/shard_map/all_to_all | solution.py:685
  14.5 3.4 %dispatch.1 = (bf16[16,48,896]{2,1,0:T(8,128)(2,1)}, bf16[16,48,896]{2,1,0:T(8,128)(2,1)}) custom-call(bf16[8,16,1024]{2,1,0:T(8,128)(2,1)} %all_to_all.35.r_ref), custom_call_target="tpu_custom_call" | custom-call | tf_op jit(solution)/shard_map/dispatch/pallas_call | solution.py:687
  17.9 8.1 %all-to-all-start.1 = ((bf16[16,48,896]{2,1,0:T(8,128)(2,1)}), bf16[16,48,896]{2,1,0:T(8,128)(2,1)}, u32[]{:S(2)}, u32[]{:S(2)}) async-start(bf16[16,48,896]{2,1,0:T(8,128)(2,1)} %get-tuple-element.32), calls=%async_computation.1 | async-start | bytes 2752512 | tf_op jit(solution)/shard_map/all_to_all | solution.py:585
  27.9 8.0 %old0.1 = (f32[8,128,512]{2,1,0:T(8,128)S(1)}, f32[8,128,128]{2,1,0:T(8,128)S(1)}) custom-call(s32[8,128]{1,0:T(8,128)S(1)} %get-tuple-element.33.len_ref.leaving_ref.after_ref.tab_ref.idx_ref, bf16[2,8,576,128]{3,2,1,0:T(8,128)(2,1)S(1)} %bitcast.44, bf16[8,576,512]{2,1,0:T(8,128)(2,1)} %bitcast.52), custom_call_target="tpu_custom_call" | custom-call | flops 5000000000 | bytes 8000000 | tf_op jit(solution)/shard_map/old0/pallas_call | solution.py:378
  37.3 10.0 %all-to-all-done.1.x_ref = bf16[16,48,896]{2,1,0:T(8,128)(2,1)} async-done(((bf16[16,48,896]{2,1,0:T(8,128)(2,1)}), bf16[16,48,896]{2,1,0:T(8,128)(2,1)}, u32[]{:S(2)}, u32[]{:S(2)}) %all-to-all-start.1) | async-done | bytes 1376288 | tf_op jit(solution)/shard_map/all_to_all | solution.py:585
  47.3 8.8 %gate_up.2 = (bf16[4,2,384,256]{3,2,1,0:T(8,128)(2,1)S(1)}, bf16[4,2,384,256]{3,2,1,0:T(8,128)(2,1)}) custom-call(s32[2]{0:T(128)S(1)} %pad_add_fusion.at_ref, bf16[16,48,896]{2,1,0:T(8,128)(2,1)} %all-to-all-done.1.x_ref, bf16[2,896,1024]{2,1,0:T(8,128)(2,1)} %wg_ref.3, bf16[2,896,1024]{2,1,0:T(8,128)(2,1)} %wu_ref.3, ...), custom_call_target="tpu_custom_call" | custom-call | flops 4000000000 | bytes 12000000 | tf_op jit(solution)/shard_map/gate_up/pallas_call | solution.py:222
  57.2 4.4 %all-to-all-start.2 = ((bf16[16,48,896]{2,1,0:T(8,128)(2,1)}), bf16[16,48,896]{2,1,0:T(8,128)(2,1)}, u32[]{:S(2)}, u32[]{:S(2)}) async-start(bf16[16,48,896]{2,1,0:T(8,128)(2,1)} %get-tuple-element.38), calls=%async_computation.2 | async-start | bytes 2752512 | tf_op jit(solution)/shard_map/all_to_all | solution.py:585
  66.2 8.1 %old1.1 = (f32[8,128,512]{2,1,0:T(8,128)S(1)}, f32[8,128,128]{2,1,0:T(8,128)S(1)}) custom-call(s32[8,128]{1,0:T(8,128)S(1)} %get-tuple-element.33.len_ref.leaving_ref.after_ref.tab_ref.idx_ref, bf16[2,8,576,128]{3,2,1,0:T(8,128)(2,1)S(1)} %bitcast.45, bf16[8,576,512]{2,1,0:T(8,128)(2,1)} %bitcast.53, bf16[2,384,256]{2,1,0:T(8,128)(2,1)S(1)} %get-tuple-element.67.after_ref), custom_call_target="tpu_custom_call" | custom-call | flops 5000000000 | bytes 8000000 | tf_op jit(solution)/shard_map/old1/pallas_call | solution.py:397
  78.2 7.7 %collective-permute-done.1 = bf16[2,384,256]{2,1,0:T(8,128)(2,1)S(1)} collective-permute-done((bf16[2,384,256]{2,1,0:T(8,128)(2,1)S(1)}, bf16[2,384,256]{2,1,0:T(8,128)(2,1)S(1)}, u32[]{:S(2)}, u32[]{:S(2)}) %collective-permute-start.1) | collective-permute-done | bytes 393248 | tf_op jit(solution)/shard_map/ppermute | solution.py:589
  87.4 8.8 %gate_up.3 = (bf16[4,2,384,256]{3,2,1,0:T(8,128)(2,1)S(1)}, bf16[4,2,384,256]{3,2,1,0:T(8,128)(2,1)}) custom-call(s32[2]{0:T(128)S(1)} %pad_add_fusion.at_ref, bf16[16,48,896]{2,1,0:T(8,128)(2,1)} %all-to-all-done.2.after_ref.x_ref, bf16[2,896,1024]{2,1,0:T(8,128)(2,1)} %wg_ref.3, bf16[2,896,1024]{2,1,0:T(8,128)(2,1)} %wu_ref.3, ...), custom_call_target="tpu_custom_call" | custom-call | flops 4000000000 | bytes 12000000 | tf_op jit(solution)/shard_map/gate_up/pallas_call | solution.py:222
  100.7 6.8 %all-to-all-start.3 = ((bf16[16,2,144,128]{3,2,1,0:T(8,128)(2,1)}), bf16[16,2,144,128]{3,2,1,0:T(8,128)(2,1)S(1)}, u32[]{:S(2)}, u32[]{:S(2)}) async-start(bf16[16,2,144,128]{3,2,1,0:T(8,128)(2,1)} %copy-done.5), calls=%async_computation.3 | async-start | bytes 2359296 | tf_op jit(solution)/shard_map/all_to_all | solution.py:585
  107.6 3.2 %collective-permute-start.5 = (bf16[2,384,128]{2,1,0:T(8,128)(2,1)}, bf16[2,384,128]{2,1,0:T(8,128)(2,1)}, u32[]{:S(2)}, u32[]{:S(2)}) collective-permute-start(bf16[2,384,128]{2,1,0:T(8,128)(2,1)} %copy-done.15), channel_id=1, source_target_pairs={{0,6},{1,7},{2,0},{3,1},{4,2},{5,3},{6,4},{7,5},{8,14},{9,15},{10,... | collective-permute-start | bytes 589832 | tf_op jit(solution)/shard_map/ppermute | solution.py:589
  111.0 9.2 %collective-permute-done.4.refs_1_ = bf16[2,384,128]{2,1,0:T(8,128)(2,1)S(1)} collective-permute-done((bf16[2,384,128]{2,1,0:T(8,128)(2,1)}, bf16[2,384,128]{2,1,0:T(8,128)(2,1)S(1)}, u32[]{:S(2)}, u32[]{:S(2)}) %collective-permute-start.4) | collective-permute-done | bytes 196640 | tf_op jit(solution)/shard_map/ppermute | solution.py:589
  120.8 2.8 %fusion.7 = (bf16[2,384,256]{2,1,0:T(8,128)(2,1)}, bf16[2,384,256]{2,1,0:T(8,128)(2,1)}, bf16[2,384,256]{2,1,0:T(8,128)(2,1)}) fusion(bf16[4,2,384,256]{3,2,1,0:T(8,128)(2,1)} %collective-permute-done.15, bf16[4,2,384,256]{3,2,1,0:T(8,128)(2,1)} %copy-done.13), kind=kLoop, calls=%fused_computation.15 | loop fusion | flops 2359296 | bytes 3538944 | tf_op jit(solution)/shard_map/convert_element_type | solution.py:594
  123.6 3.0 %collective-permute-start.18 = (bf16[2,384,256]{2,1,0:T(8,128)(2,1)}, bf16[2,384,256]{2,1,0:T(8,128)(2,1)}, u32[]{:S(2)}, u32[]{:S(2)}) collective-permute-start(bf16[2,384,256]{2,1,0:T(8,128)(2,1)} %get-tuple-element.63), channel_id=1, source_target_pairs={{0,6},{1,7},{2,0},{3,1},{4,2},{5,3},{6,4},{7,5},{8,14},{9,15},{10,... | collective-permute-start | bytes 1179656 | tf_op jit(solution)/shard_map/ppermute | solution.py:589
  129.2 5.5 %down.2 = bf16[16,48,896]{2,1,0:T(8,128)(2,1)} custom-call(s32[2]{0:T(128)} %copy-done.22, bf16[2,384,128]{2,1,0:T(8,128)(2,1)} %copy-done.15, bf16[2,384,128]{2,1,0:T(8,128)(2,1)} %copy-done.30, bf16[2,384,128]{2,1,0:T(8,128)(2,1)} %collective-permute-done.5.refs_2_, bf16[2,384,128]{2,1,0:T(8,128)(2,1)} %collective-permute-done.6.refs_3_, ...), custom_call_target="tpu_custom_call" | custom-call | flops 2000000000 | bytes 8000000 | tf_op jit(solution)/shard_map/down/pallas_call | solution.py:266
  134.8 6.9 %all-to-all-start.4 = ((bf16[16,48,896]{2,1,0:T(8,128)(2,1)}), bf16[16,48,896]{2,1,0:T(8,128)(2,1)}, u32[]{:S(2)}, u32[]{:S(2)}) async-start(bf16[16,48,896]{2,1,0:T(8,128)(2,1)} %down.2), calls=%async_computation.4 | async-start | bytes 2752512 | tf_op jit(solution)/shard_map/all_to_all | solution.py:585
  143.9 3.7 %collective-permute-done.16 = bf16[2,384,256]{2,1,0:T(8,128)(2,1)} collective-permute-done((bf16[2,384,256]{2,1,0:T(8,128)(2,1)}, bf16[2,384,256]{2,1,0:T(8,128)(2,1)}, u32[]{:S(2)}, u32[]{:S(2)}) %collective-permute-start.16) | collective-permute-done | bytes 393248 | tf_op jit(solution)/shard_map/ppermute | solution.py:589
  149.5 3.2 %collective-permute-start.20 = (bf16[2,384,128]{2,1,0:T(8,128)(2,1)S(1)}, bf16[2,384,128]{2,1,0:T(8,128)(2,1)S(1)}, u32[]{:S(2)}, u32[]{:S(2)}) collective-permute-start(bf16[2,384,128]{2,1,0:T(8,128)(2,1)S(1)} %fusion.10.refs_0_), channel_id=1, source_target_pairs={{0,6},{1,7},{2,0},{3,1},{4,2},{5,3},{6,4},{7,5},{8,14},{9,15},{10,... | collective-permute-start | bytes 589832 | tf_op jit(solution)/shard_map/ppermute | solution.py:589
  152.7 9.0 %collective-permute-done.19.refs_1_ = bf16[2,384,128]{2,1,0:T(8,128)(2,1)S(1)} collective-permute-done((bf16[2,384,128]{2,1,0:T(8,128)(2,1)S(1)}, bf16[2,384,128]{2,1,0:T(8,128)(2,1)S(1)}, u32[]{:S(2)}, u32[]{:S(2)}) %collective-permute-start.19) | collective-permute-done | bytes 196640 | tf_op jit(solution)/shard_map/ppermute | solution.py:589
  164.8 5.6 %down.3 = bf16[16,48,896]{2,1,0:T(8,128)(2,1)} custom-call(s32[2]{0:T(128)} %copy-done.22, bf16[2,384,128]{2,1,0:T(8,128)(2,1)} %copy-done.29, bf16[2,384,128]{2,1,0:T(8,128)(2,1)} %copy-done.33, bf16[2,384,128]{2,1,0:T(8,128)(2,1)} %copy-done.34, bf16[2,384,128]{2,1,0:T(8,128)(2,1)} %copy-done.35, bf16[2,384,128]{2,1,0:T(8,128)(2,1)} %copy-done.36, ...), custom_call_target="tpu_custom_call" | custom-call | flops 2000000000 | bytes 8000000 | tf_op jit(solution)/shard_map/down/pallas_call | solution.py:266
  170.4 7.1 %all-to-all-start.5 = ((bf16[16,48,896]{2,1,0:T(8,128)(2,1)}), bf16[16,48,896]{2,1,0:T(8,128)(2,1)}, u32[]{:S(2)}, u32[]{:S(2)}) async-start(bf16[16,48,896]{2,1,0:T(8,128)(2,1)} %down.3), calls=%async_computation.5 | async-start | bytes 2752512 | tf_op jit(solution)/shard_map/all_to_all | solution.py:585
  182.9 2.7 %collective-permute-start.12 = (f32[8,2560]{1,0:T(8,128)S(1)}, f32[8,2560]{1,0:T(8,128)S(1)}, u32[]{:S(2)}, u32[]{:S(2)}) collective-permute-start(f32[8,2560]{1,0:T(8,128)S(1)} %get-tuple-element.42), channel_id=1, source_target_pairs={{0,6},{1,7},{2,0},{3,1},{4,2},{5,3},{6,4},{7,5},{8,14},{9,15},{10,... | collective-permute-start | bytes 245768 | tf_op jit(solution)/shard_map/ppermute | solution.py:589
  186.6 2.8 %collective-permute-done.12.u1_ref = f32[8,2560]{1,0:T(8,128)S(1)} collective-permute-done((f32[8,2560]{1,0:T(8,128)S(1)}, f32[8,2560]{1,0:T(8,128)S(1)}, u32[]{:S(2)}, u32[]{:S(2)}) %collective-permute-start.12) | collective-permute-done | bytes 81952 | tf_op jit(solution)/shard_map/ppermute | solution.py:589
  189.4 2.8 %collective-permute-done.13.u2_ref = f32[8,2560]{1,0:T(8,128)S(1)} collective-permute-done((f32[8,2560]{1,0:T(8,128)S(1)}, f32[8,2560]{1,0:T(8,128)S(1)}, u32[]{:S(2)}, u32[]{:S(2)}) %collective-permute-start.13) | collective-permute-done | bytes 81952 | tf_op jit(solution)/shard_map/ppermute | solution.py:589
  194.1 3.0 %forward.1.after_ref = bf16[16,336,128]{2,1,0:T(8,128)(2,1)S(1)} custom-call(s32[8,128]{1,0:T(8,128)S(1)} %get-tuple-element.33.len_ref.leaving_ref.after_ref.tab_ref.idx_ref, bf16[32,144,128]{2,1,0:T(8,128)(2,1)S(1)} %bitcast.49, bf16[48,128]{1,0:T(8,128)(2,1)S(1)} %get-tuple-element.50.key_ref), custom_call_target="tpu_custom_call" | custom-call | flops 1000000 | bytes 3000000 | tf_op jit(solution)/shard_map/forward/pallas_call | solution.py:566
  202.1 3.2 %combine1.1 = (f32[4,8,1664]{2,1,0:T(8,128)S(1)}, f32[4,8,1664]{2,1,0:T(8,128)}) custom-call(s32[2]{0:T(128)S(1)} %copy-done.23, bf16[8,16,1024]{2,1,0:T(8,128)(2,1)S(1)} %copy-done.6, bf16[16,48,896]{2,1,0:T(8,128)(2,1)} %all-to-all-done.5.ret_ref, bf16[576,896]{1,0:T(8,128)(2,1)S(1)} %bitcast.51, bf16[16,336,128]{2,1,0:T(8,128)(2,1)S(1)} %copy-done.4), custom_call_target="tpu_custom_call" | custom-call | flops 400000000 | bytes 4000000 | tf_op jit(solution)/shard_map/combine1/pallas_call | solution.py:619
  205.3 6.0 %all-to-all-start.6 = ((bf16[16,336,128]{2,1,0:T(8,128)(2,1)}), bf16[16,336,128]{2,1,0:T(8,128)(2,1)}, u32[]{:S(2)}, u32[]{:S(2)}) async-start(bf16[16,336,128]{2,1,0:T(8,128)(2,1)} %copy-done.3), calls=%async_computation.6 | async-start | bytes 2752512 | tf_op jit(solution)/shard_map/all_to_all | solution.py:585
  216.0 5.8 %merge0.1.refs_2_ = bf16[2,8,128,512]{3,2,1,0:T(8,128)(2,1)} custom-call(s32[8,128]{1,0:T(8,128)S(1)} %get-tuple-element.33.len_ref.leaving_ref.after_ref.tab_ref.idx_ref, bf16[2,8,576,128]{3,2,1,0:T(8,128)(2,1)S(1)} %bitcast.46, f32[8,128,512]{2,1,0:T(8,128)S(1)} %copy-done.12, f32[8,128,128]{2,1,0:T(8,128)S(1)} %copy-done.19, f32[8,640]{1,0:T(8,128)S(1)} %copy-done.21), custom_call_target="tpu_custom_call" | custom-call | flops 100000000 | bytes 5000000 | tf_op jit(solution)/shard_map/merge0/pallas_call | solution.py:462
  223.2 6.1 %merge1.1.buffer_ref = bf16[2,8,128,512]{3,2,1,0:T(8,128)(2,1)} custom-call(s32[8,128]{1,0:T(8,128)S(1)} %get-tuple-element.33.len_ref.leaving_ref.after_ref.tab_ref.idx_ref, bf16[2,8,576,128]{3,2,1,0:T(8,128)(2,1)S(1)} %bitcast.47, f32[8,128,512]{2,1,0:T(8,128)S(1)} %copy-done.10, f32[8,128,128]{2,1,0:T(8,128)S(1)} %copy-done.17, ...), custom_call_target="tpu_custom_call", output_to_operand_aliasing={{}: (6, {})} | custom-call | flops 100000000 | bytes 5000000 | tf_op jit(solution)/shard_map/merge1/pallas_call | solution.py:462
  230.0 3.6 %all-to-all-done.6.kv_ref.keys_ref = bf16[16,336,128]{2,1,0:T(8,128)(2,1)} async-done(((bf16[16,336,128]{2,1,0:T(8,128)(2,1)}), bf16[16,336,128]{2,1,0:T(8,128)(2,1)}, u32[]{:S(2)}, u32[]{:S(2)}) %all-to-all-start.6) | async-done | bytes 1376288 | tf_op jit(solution)/shard_map/all_to_all | solution.py:585
  233.6 4.3 %moved_rows.1 = bf16[2,8,128,512]{3,2,1,0:T(8,128)(2,1)} custom-call(s32[8,128]{1,0:T(8,128)S(1)} %get-tuple-element.33.len_ref.leaving_ref.after_ref.tab_ref.idx_ref, bf16[2,8,576,128]{3,2,1,0:T(8,128)(2,1)S(1)} %bitcast.48, bf16[16,336,128]{2,1,0:T(8,128)(2,1)} %all-to-all-done.6.kv_ref.keys_ref, ...), custom_call_target="tpu_custom_call", output_to_operand_aliasing={{}: (5, {})} | custom-call | flops 600000000 | bytes 3000000 | tf_op jit(solution)/shard_map/moved_rows/pallas_call | solution.py:499
  (159 shorter events, 51.3 us)
Async XLA Ops:
  17.9 29.3 %all-to-all-start.1 = ((bf16[16,48,896]{2,1,0:T(8,128)(2,1)}), bf16[16,48,896]{2,1,0:T(8,128)(2,1)}, u32[]{:S(2)}, u32[]{:S(2)}) async-start(bf16[16,48,896]{2,1,0:T(8,128)(2,1)} %get-tuple-element.32), calls=%async_computation.1 | async-start | bytes 2752512 | tf_op jit(solution)/shard_map/all_to_all | solution.py:585
  57.2 4.4 %collective-permute-start = (bf16[4,2,384,256]{3,2,1,0:T(8,128)(2,1)}, bf16[4,2,384,256]{3,2,1,0:T(8,128)(2,1)}, u32[]{:S(2)}, u32[]{:S(2)}) collective-permute-start(bf16[4,2,384,256]{3,2,1,0:T(8,128)(2,1)} %get-tuple-element.37), channel_id=1, source_target_pairs={{0,1},{1,0},{2,3},{3,2},{4,5},{5,4},{6,7},{7,6},{8,9},{9,8},{10,11... | collective-permute-start | bytes 4718600 | tf_op jit(solution)/shard_map/ppermute | solution.py:589
  57.2 30.2 %all-to-all-start.2 = ((bf16[16,48,896]{2,1,0:T(8,128)(2,1)}), bf16[16,48,896]{2,1,0:T(8,128)(2,1)}, u32[]{:S(2)}, u32[]{:S(2)}) async-start(bf16[16,48,896]{2,1,0:T(8,128)(2,1)} %get-tuple-element.38), calls=%async_computation.2 | async-start | bytes 2752512 | tf_op jit(solution)/shard_map/all_to_all | solution.py:585
  63.5 12.1 %collective-permute-start.3 = (bf16[2,384,256]{2,1,0:T(8,128)(2,1)S(1)}, bf16[2,384,256]{2,1,0:T(8,128)(2,1)S(1)}, u32[]{:S(2)}, u32[]{:S(2)}) collective-permute-start(bf16[2,384,256]{2,1,0:T(8,128)(2,1)S(1)} %get-tuple-element.66), channel_id=1, source_target_pairs={{0,6},{1,7},{2,0},{3,1},{4,2},{5,3},{6,4},{7,5},{8,14},{9,15},{10,... | collective-permute-start | bytes 1179656 | tf_op jit(solution)/shard_map/ppermute | solution.py:589
  64.7 13.5 %collective-permute-start.2 = (bf16[2,384,256]{2,1,0:T(8,128)(2,1)S(1)}, bf16[2,384,256]{2,1,0:T(8,128)(2,1)S(1)}, u32[]{:S(2)}, u32[]{:S(2)}) collective-permute-start(bf16[2,384,256]{2,1,0:T(8,128)(2,1)S(1)} %get-tuple-element.65), channel_id=1, source_target_pairs={{0,4},{1,5},{2,6},{3,7},{4,0},{5,1},{6,2},{7,3},{8,12},{9,13},{10,... | collective-permute-start | bytes 1179656 | tf_op jit(solution)/shard_map/ppermute | solution.py:589
  66.2 19.7 %collective-permute-start.1 = (bf16[2,384,256]{2,1,0:T(8,128)(2,1)S(1)}, bf16[2,384,256]{2,1,0:T(8,128)(2,1)S(1)}, u32[]{:S(2)}, u32[]{:S(2)}) collective-permute-start(bf16[2,384,256]{2,1,0:T(8,128)(2,1)S(1)} %get-tuple-element.67.after_ref), channel_id=1, source_target_pairs={{0,2},{1,3},{2,4},{3,5},{4,6},{5,7},{6,0},{7,1},{8,10},{9,11},{10,... | collective-permute-start | bytes 1179656 | tf_op jit(solution)/shard_map/ppermute | solution.py:589
  97.4 23.4 %collective-permute-start.15 = (bf16[4,2,384,256]{3,2,1,0:T(8,128)(2,1)}, bf16[4,2,384,256]{3,2,1,0:T(8,128)(2,1)}, u32[]{:S(2)}, u32[]{:S(2)}) collective-permute-start(bf16[4,2,384,256]{3,2,1,0:T(8,128)(2,1)} %get-tuple-element.49), channel_id=1, source_target_pairs={{0,1},{1,0},{2,3},{3,2},{4,5},{5,4},{6,7},{7,6},{8,9},{9,8},{10,11... | collective-permute-start | bytes 4718600 | tf_op jit(solution)/shard_map/ppermute | solution.py:589
  100.7 27.5 %all-to-all-start.3 = ((bf16[16,2,144,128]{3,2,1,0:T(8,128)(2,1)}), bf16[16,2,144,128]{3,2,1,0:T(8,128)(2,1)S(1)}, u32[]{:S(2)}, u32[]{:S(2)}) async-start(bf16[16,2,144,128]{3,2,1,0:T(8,128)(2,1)} %copy-done.5), calls=%async_computation.3 | async-start | bytes 2359296 | tf_op jit(solution)/shard_map/all_to_all | solution.py:585
  107.5 12.7 %collective-permute-start.4 = (bf16[2,384,128]{2,1,0:T(8,128)(2,1)}, bf16[2,384,128]{2,1,0:T(8,128)(2,1)S(1)}, u32[]{:S(2)}, u32[]{:S(2)}) collective-permute-start(bf16[2,384,128]{2,1,0:T(8,128)(2,1)} %copy-done.15), channel_id=1, source_target_pairs={{0,2},{1,3},{2,4},{3,5},{4,6},{5,7},{6,0},{7,1},{8,10},{9,11},{10,... | collective-permute-start | bytes 589832 | tf_op jit(solution)/shard_map/ppermute | solution.py:589
  107.6 12.7 %collective-permute-start.5 = (bf16[2,384,128]{2,1,0:T(8,128)(2,1)}, bf16[2,384,128]{2,1,0:T(8,128)(2,1)}, u32[]{:S(2)}, u32[]{:S(2)}) collective-permute-start(bf16[2,384,128]{2,1,0:T(8,128)(2,1)} %copy-done.15), channel_id=1, source_target_pairs={{0,6},{1,7},{2,0},{3,1},{4,2},{5,3},{6,4},{7,5},{8,14},{9,15},{10,... | collective-permute-start | bytes 589832 | tf_op jit(solution)/shard_map/ppermute | solution.py:589
  110.8 9.9 %collective-permute-start.6 = (bf16[2,384,128]{2,1,0:T(8,128)(2,1)}, bf16[2,384,128]{2,1,0:T(8,128)(2,1)}, u32[]{:S(2)}, u32[]{:S(2)}) collective-permute-start(bf16[2,384,128]{2,1,0:T(8,128)(2,1)} %copy-done.15), channel_id=1, source_target_pairs={{0,4},{1,5},{2,6},{3,7},{4,0},{5,1},{6,2},{7,3},{8,12},{9,13},{10,... | collective-permute-start | bytes 589832 | tf_op jit(solution)/shard_map/ppermute | solution.py:589
  111.0 15.5 %collective-permute-start.7 = (bf16[2,384,128]{2,1,0:T(8,128)(2,1)}, bf16[2,384,128]{2,1,0:T(8,128)(2,1)S(1)}, u32[]{:S(2)}, u32[]{:S(2)}) collective-permute-start(bf16[2,384,128]{2,1,0:T(8,128)(2,1)} %copy-done.15), channel_id=1, source_target_pairs={{0,1},{1,0},{2,3},{3,2},{4,5},{5,4},{6,7},{7,6},{8,9},{9,8},{10,11... | collective-permute-start | bytes 589832 | tf_op jit(solution)/shard_map/ppermute | solution.py:589
  120.2 6.4 %collective-permute-start.8 = (bf16[2,384,128]{2,1,0:T(8,128)(2,1)S(1)}, bf16[2,384,128]{2,1,0:T(8,128)(2,1)S(1)}, u32[]{:S(2)}, u32[]{:S(2)}) collective-permute-start(bf16[2,384,128]{2,1,0:T(8,128)(2,1)S(1)} %collective-permute-done.4.refs_1_), channel_id=1, source_target_pairs={{0,1},{1,0},{2,3},{3,2},{4,5},{5,4},{6,7},{7,6},{8,9},{9,8},{10,11... | collective-permute-start | bytes 589832 | tf_op jit(solution)/shard_map/ppermute | solution.py:589
  120.2 8.0 %collective-permute-start.9 = (bf16[2,384,128]{2,1,0:T(8,128)(2,1)}, bf16[2,384,128]{2,1,0:T(8,128)(2,1)}, u32[]{:S(2)}, u32[]{:S(2)}) collective-permute-start(bf16[2,384,128]{2,1,0:T(8,128)(2,1)} %collective-permute-done.5.refs_2_), channel_id=1, source_target_pairs={{0,1},{1,0},{2,3},{3,2},{4,5},{5,4},{6,7},{7,6},{8,9},{9,8},{10,11... | collective-permute-start | bytes 589832 | tf_op jit(solution)/shard_map/ppermute | solution.py:589
  120.7 7.5 %collective-permute-start.10 = (bf16[2,384,128]{2,1,0:T(8,128)(2,1)}, bf16[2,384,128]{2,1,0:T(8,128)(2,1)}, u32[]{:S(2)}, u32[]{:S(2)}) collective-permute-start(bf16[2,384,128]{2,1,0:T(8,128)(2,1)} %collective-permute-done.6.refs_3_), channel_id=1, source_target_pairs={{0,1},{1,0},{2,3},{3,2},{4,5},{5,4},{6,7},{7,6},{8,9},{9,8},{10,11... | collective-permute-start | bytes 589832 | tf_op jit(solution)/shard_map/ppermute | solution.py:589
  123.6 20.3 %collective-permute-start.18 = (bf16[2,384,256]{2,1,0:T(8,128)(2,1)}, bf16[2,384,256]{2,1,0:T(8,128)(2,1)}, u32[]{:S(2)}, u32[]{:S(2)}) collective-permute-start(bf16[2,384,256]{2,1,0:T(8,128)(2,1)} %get-tuple-element.63), channel_id=1, source_target_pairs={{0,6},{1,7},{2,0},{3,1},{4,2},{5,3},{6,4},{7,5},{8,14},{9,15},{10,... | collective-permute-start | bytes 1179656 | tf_op jit(solution)/shard_map/ppermute | solution.py:589
  126.6 17.3 %collective-permute-start.17 = (bf16[2,384,256]{2,1,0:T(8,128)(2,1)}, bf16[2,384,256]{2,1,0:T(8,128)(2,1)}, u32[]{:S(2)}, u32[]{:S(2)}) collective-permute-start(bf16[2,384,256]{2,1,0:T(8,128)(2,1)} %get-tuple-element.64), channel_id=1, source_target_pairs={{0,4},{1,5},{2,6},{3,7},{4,0},{5,1},{6,2},{7,3},{8,12},{9,13},{10,... | collective-permute-start | bytes 1179656 | tf_op jit(solution)/shard_map/ppermute | solution.py:589
  127.3 20.3 %collective-permute-start.16 = (bf16[2,384,256]{2,1,0:T(8,128)(2,1)}, bf16[2,384,256]{2,1,0:T(8,128)(2,1)}, u32[]{:S(2)}, u32[]{:S(2)}) collective-permute-start(bf16[2,384,256]{2,1,0:T(8,128)(2,1)} %get-tuple-element.62), channel_id=1, source_target_pairs={{0,2},{1,3},{2,4},{3,5},{4,6},{5,7},{6,0},{7,1},{8,10},{9,11},{10,... | collective-permute-start | bytes 1179656 | tf_op jit(solution)/shard_map/ppermute | solution.py:589
  134.8 35.6 %all-to-all-start.4 = ((bf16[16,48,896]{2,1,0:T(8,128)(2,1)}), bf16[16,48,896]{2,1,0:T(8,128)(2,1)}, u32[]{:S(2)}, u32[]{:S(2)}) async-start(bf16[16,48,896]{2,1,0:T(8,128)(2,1)} %down.2), calls=%async_computation.4 | async-start | bytes 2752512 | tf_op jit(solution)/shard_map/all_to_all | solution.py:585
  149.4 12.3 %collective-permute-start.19 = (bf16[2,384,128]{2,1,0:T(8,128)(2,1)S(1)}, bf16[2,384,128]{2,1,0:T(8,128)(2,1)S(1)}, u32[]{:S(2)}, u32[]{:S(2)}) collective-permute-start(bf16[2,384,128]{2,1,0:T(8,128)(2,1)S(1)} %fusion.10.refs_0_), channel_id=1, source_target_pairs={{0,2},{1,3},{2,4},{3,5},{4,6},{5,7},{6,0},{7,1},{8,10},{9,11},{10,... | collective-permute-start | bytes 589832 | tf_op jit(solution)/shard_map/ppermute | solution.py:589
  149.5 12.2 %collective-permute-start.20 = (bf16[2,384,128]{2,1,0:T(8,128)(2,1)S(1)}, bf16[2,384,128]{2,1,0:T(8,128)(2,1)S(1)}, u32[]{:S(2)}, u32[]{:S(2)}) collective-permute-start(bf16[2,384,128]{2,1,0:T(8,128)(2,1)S(1)} %fusion.10.refs_0_), channel_id=1, source_target_pairs={{0,6},{1,7},{2,0},{3,1},{4,2},{5,3},{6,4},{7,5},{8,14},{9,15},{10,... | collective-permute-start | bytes 589832 | tf_op jit(solution)/shard_map/ppermute | solution.py:589
  152.7 9.5 %collective-permute-start.21 = (bf16[2,384,128]{2,1,0:T(8,128)(2,1)S(1)}, bf16[2,384,128]{2,1,0:T(8,128)(2,1)S(1)}, u32[]{:S(2)}, u32[]{:S(2)}) collective-permute-start(bf16[2,384,128]{2,1,0:T(8,128)(2,1)S(1)} %fusion.10.refs_0_), channel_id=1, source_target_pairs={{0,4},{1,5},{2,6},{3,7},{4,0},{5,1},{6,2},{7,3},{8,12},{9,13},{10,... | collective-permute-start | bytes 589832 | tf_op jit(solution)/shard_map/ppermute | solution.py:589
  152.7 9.6 %collective-permute-start.22 = (bf16[2,384,128]{2,1,0:T(8,128)(2,1)S(1)}, bf16[2,384,128]{2,1,0:T(8,128)(2,1)S(1)}, u32[]{:S(2)}, u32[]{:S(2)}) collective-permute-start(bf16[2,384,128]{2,1,0:T(8,128)(2,1)S(1)} %fusion.10.refs_0_), channel_id=1, source_target_pairs={{0,1},{1,0},{2,3},{3,2},{4,5},{5,4},{6,7},{7,6},{8,9},{9,8},{10,11... | collective-permute-start | bytes 589832 | tf_op jit(solution)/shard_map/ppermute | solution.py:589
  170.4 29.2 %all-to-all-start.5 = ((bf16[16,48,896]{2,1,0:T(8,128)(2,1)}), bf16[16,48,896]{2,1,0:T(8,128)(2,1)}, u32[]{:S(2)}, u32[]{:S(2)}) async-start(bf16[16,48,896]{2,1,0:T(8,128)(2,1)} %down.3), calls=%async_computation.5 | async-start | bytes 2752512 | tf_op jit(solution)/shard_map/all_to_all | solution.py:585
  182.9 6.5 %collective-permute-start.12 = (f32[8,2560]{1,0:T(8,128)S(1)}, f32[8,2560]{1,0:T(8,128)S(1)}, u32[]{:S(2)}, u32[]{:S(2)}) collective-permute-start(f32[8,2560]{1,0:T(8,128)S(1)} %get-tuple-element.42), channel_id=1, source_target_pairs={{0,6},{1,7},{2,0},{3,1},{4,2},{5,3},{6,4},{7,5},{8,14},{9,15},{10,... | collective-permute-start | bytes 245768 | tf_op jit(solution)/shard_map/ppermute | solution.py:589
  185.6 6.6 %collective-permute-start.13 = (f32[8,2560]{1,0:T(8,128)S(1)}, f32[8,2560]{1,0:T(8,128)S(1)}, u32[]{:S(2)}, u32[]{:S(2)}) collective-permute-start(f32[8,2560]{1,0:T(8,128)S(1)} %get-tuple-element.43), channel_id=1, source_target_pairs={{0,4},{1,5},{2,6},{3,7},{4,0},{5,1},{6,2},{7,3},{8,12},{9,13},{10,... | collective-permute-start | bytes 245768 | tf_op jit(solution)/shard_map/ppermute | solution.py:589
  185.6 7.2 %collective-permute-start.14 = (f32[8,2560]{1,0:T(8,128)S(1)}, f32[8,2560]{1,0:T(8,128)S(1)}, u32[]{:S(2)}, u32[]{:S(2)}) collective-permute-start(f32[8,2560]{1,0:T(8,128)S(1)} %get-tuple-element.44), channel_id=1, source_target_pairs={{0,2},{1,3},{2,4},{3,5},{4,6},{5,7},{6,0},{7,1},{8,10},{9,11},{10,... | collective-permute-start | bytes 245768 | tf_op jit(solution)/shard_map/ppermute | solution.py:589
  205.3 6.0 %collective-permute-start.26 = (f32[4,8,1664]{2,1,0:T(8,128)}, f32[4,8,1664]{2,1,0:T(8,128)S(1)}, u32[]{:S(2)}, u32[]{:S(2)}) collective-permute-start(f32[4,8,1664]{2,1,0:T(8,128)} %get-tuple-element.52), channel_id=1, source_target_pairs={{0,1},{1,0},{2,3},{3,2},{4,5},{5,4},{6,7},{7,6},{8,9},{9,8},{10,11... | collective-permute-start | bytes 638984 | tf_op jit(solution)/shard_map/ppermute | solution.py:589
  205.3 28.3 %all-to-all-start.6 = ((bf16[16,336,128]{2,1,0:T(8,128)(2,1)}), bf16[16,336,128]{2,1,0:T(8,128)(2,1)}, u32[]{:S(2)}, u32[]{:S(2)}) async-start(bf16[16,336,128]{2,1,0:T(8,128)(2,1)} %copy-done.3), calls=%async_computation.6 | async-start | bytes 2752512 | tf_op jit(solution)/shard_map/all_to_all | solution.py:585
  211.4 10.5 %collective-permute-start.27 = (f32[8,2560]{1,0:T(8,128)S(1)}, f32[8,2560]{1,0:T(8,128)S(1)}, u32[]{:S(2)}, u32[]{:S(2)}) collective-permute-start(f32[8,2560]{1,0:T(8,128)S(1)} %get-tuple-element.54), channel_id=1, source_target_pairs={{0,6},{1,7},{2,0},{3,1},{4,2},{5,3},{6,4},{7,5},{8,14},{9,15},{10,... | collective-permute-start | bytes 245768 | tf_op jit(solution)/shard_map/ppermute | solution.py:589
  212.4 9.4 %collective-permute-start.28 = (f32[8,2560]{1,0:T(8,128)S(1)}, f32[8,2560]{1,0:T(8,128)S(1)}, u32[]{:S(2)}, u32[]{:S(2)}) collective-permute-start(f32[8,2560]{1,0:T(8,128)S(1)} %get-tuple-element.55), channel_id=1, source_target_pairs={{0,4},{1,5},{2,6},{3,7},{4,0},{5,1},{6,2},{7,3},{8,12},{9,13},{10,... | collective-permute-start | bytes 245768 | tf_op jit(solution)/shard_map/ppermute | solution.py:589
  212.6 9.3 %collective-permute-start.29 = (f32[8,2560]{1,0:T(8,128)S(1)}, f32[8,2560]{1,0:T(8,128)S(1)}, u32[]{:S(2)}, u32[]{:S(2)}) collective-permute-start(f32[8,2560]{1,0:T(8,128)S(1)} %get-tuple-element.56), channel_id=1, source_target_pairs={{0,2},{1,3},{2,4},{3,5},{4,6},{5,7},{6,0},{7,1},{8,10},{9,11},{10,... | collective-permute-start | bytes 245768 | tf_op jit(solution)/shard_map/ppermute | solution.py:589
  (46 other events, 284.5 us)
